TPU v7x, 32 devices: a whole 2x2x4 slice. The times are simulated.
32 devices in a mesh: tm: 16 (over z, y, x), mp: 2 (over core).
Axes of the slice: x: 2, y: 2, z: 4, core: 2. Of those that a mesh axis runs over, the one named last changes fastest.
Arguments:
- x_input: float32 [8192, 512], P('tm', 'mp')
- mel_frames: float32 [80, 8192], P(None, 'tm'), may hold values from -6 to 6
- sample_mask: int32 [8192], P('tm'), may hold values 0 or 1
- clip_length_array: int32 [8], replicated, may hold values from 1 to 8185, as said below
- speaker_ids: int32 [8], replicated, may hold values from 0 to 108
- cot_out: float32 [8192, 512], P('tm', 'mp')
- cot_skip: float32 [8192, 512], P('tm', 'mp')
- dilated_kernel_weight: float32 [2, 2, 512, 2, 512], P(None, None, 'tm', None, 'mp'), may hold values from -0.1875 to 0.1875
- dilated_first_moment: float32 [2, 2, 512, 2, 512], P(None, None, 'tm', None, 'mp'), may hold values from -0.0007324219 to 0.0007324219
- dilated_second_moment: float32 [2, 2, 512, 2, 512], P(None, None, 'tm', None, 'mp'), may hold values from 2.828976e-10 to 1.1315904e-09
- gate_bias: float32 [2, 2, 512], P(None, None, ('mp', 'tm')), may hold values from -1.5 to 1.5
- bias_mean: float32 [2, 2, 512], P(None, None, ('mp', 'tm')), may hold values from -0.0007324219 to 0.0007324219
- bias_square: float32 [2, 2, 512], P(None, None, ('mp', 'tm')), may hold values from 2.828976e-10 to 1.1315904e-09
- mel_weight: float32 [2, 80, 2, 512], P(None, None, None, ('mp', 'tm')), may hold values from -0.625 to 0.625
- mel_mean: float32 [2, 80, 2, 512], P(None, None, None, ('mp', 'tm')), may hold values from -0.0007324219 to 0.0007324219
- mel_square: float32 [2, 80, 2, 512], P(None, None, None, ('mp', 'tm')), may hold values from 2.828976e-10 to 1.1315904e-09
- speaker_table: float32 [2, 109, 2, 512], P(None, None, None, ('mp', 'tm')), may hold values from -4 to 4
- table_mean: float32 [2, 109, 2, 512], P(None, None, None, ('mp', 'tm')), may hold values from -0.0007324219 to 0.0007324219
- table_square: float32 [2, 109, 2, 512], P(None, None, None, ('mp', 'tm')), may hold values from 2.828976e-10 to 1.1315904e-09
- residual_weight: float32 [2, 512, 512], P(None, 'mp', 'tm')
- residual_mean: float32 [2, 512, 512], P(None, 'mp', 'tm'), may hold values from -0.0007324219 to 0.0007324219
- residual_square: float32 [2, 512, 512], P(None, 'mp', 'tm'), may hold values from 2.828976e-10 to 1.1315904e-09
- skip_weight: float32 [2, 512, 512], P(None, 'mp', 'tm')
- skip_mean: float32 [2, 512, 512], P(None, 'mp', 'tm'), may hold values from -0.0007324219 to 0.0007324219
- skip_square: float32 [2, 512, 512], P(None, 'mp', 'tm'), may hold values from 2.828976e-10 to 1.1315904e-09
Outputs:
- mixed: float32 [8192, 512], P('tm', 'mp')
- skip_total: float32 [8192, 512], P('tm', 'mp')
- grad_input: float32 [8192, 512], P('tm', 'mp')
- grad_norm: float32 [], replicated
- grad_dilated: float32 [2, 2, 512, 2, 512], P(None, None, 'tm', None, 'mp')
- grad_bias: float32 [2, 2, 512], P(None, None, ('mp', 'tm'))
- grad_mel: float32 [2, 80, 2, 512], P(None, None, None, ('mp', 'tm'))
- grad_table: float32 [2, 109, 2, 512], P(None, None, None, ('mp', 'tm'))
- grad_residual: float32 [2, 512, 512], P(None, 'mp', 'tm')
- grad_skip: float32 [2, 512, 512], P(None, 'mp', 'tm')
- new_dilated_weight: float32 [2, 2, 512, 2, 512], P(None, None, 'tm', None, 'mp')
- new_dilated_mean: float32 [2, 2, 512, 2, 512], P(None, None, 'tm', None, 'mp')
- new_dilated_square: float32 [2, 2, 512, 2, 512], P(None, None, 'tm', None, 'mp')
- new_gate_bias: float32 [2, 2, 512], P(None, None, ('mp', 'tm'))
- new_bias_mean: float32 [2, 2, 512], P(None, None, ('mp', 'tm'))
- new_bias_square: float32 [2, 2, 512], P(None, None, ('mp', 'tm'))
- new_mel_weight: float32 [2, 80, 2, 512], P(None, None, None, ('mp', 'tm'))
- new_mel_mean: float32 [2, 80, 2, 512], P(None, None, None, ('mp', 'tm'))
- new_mel_square: float32 [2, 80, 2, 512], P(None, None, None, ('mp', 'tm'))
- new_speaker_table: float32 [2, 109, 2, 512], P(None, None, None, ('mp', 'tm'))
- new_table_mean: float32 [2, 109, 2, 512], P(None, None, None, ('mp', 'tm'))
- new_table_square: float32 [2, 109, 2, 512], P(None, None, None, ('mp', 'tm'))
- new_residual_weight: float32 [2, 512, 512], P(None, 'mp', 'tm')
- new_residual_mean: float32 [2, 512, 512], P(None, 'mp', 'tm')
- new_residual_square: float32 [2, 512, 512], P(None, 'mp', 'tm')
- new_skip_weight: float32 [2, 512, 512], P(None, 'mp', 'tm')
- new_skip_mean: float32 [2, 512, 512], P(None, 'mp', 'tm')
- new_skip_square: float32 [2, 512, 512], P(None, 'mp', 'tm')
- low_dilated: bfloat16 [2, 2, 512, 2, 512], P(None, None, 'tm', None, 'mp')
- low_bias: bfloat16 [2, 2, 512], P(None, None, ('mp', 'tm'))
- low_mel: bfloat16 [2, 80, 2, 512], P(None, None, None, ('mp', 'tm'))
- low_table: bfloat16 [2, 109, 2, 512], P(None, None, None, ('mp', 'tm'))
- low_residual: bfloat16 [2, 512, 512], P(None, 'mp', 'tm')
- low_skip: bfloat16 [2, 512, 512], P(None, 'mp', 'tm')
Inputs may be any that keep to these rules, and one draw needn't show every extreme that they name: `clip_length_array`: the lengths sum to 8192; one clip, which one drawn from the seed, starts within the first 512 samples and ends within the last 512; every other clip is shorter than 64.
All inputs are finite; a program needn't handle non-finite values. No bound on the sum of `sample_mask` on one device may be relied on, other than what follows from the above.
Results may differ from a plain program's by a relative error of at most 0.0083.
The roundings to bfloat16 on the way count: a program that leaves them out, or rounds other values in their place, can miss the bound.
Values may be sent and summed in bfloat16 or wider, within the bound.
No kernel may reach another device: no remote copies, remote signals or barrier semaphores. Data moves between devices by JAX's collectives and lax.ppermute only.
A program may use at most 128 MiB of HBM per device.

v0:
```python
import jax
import jax.numpy as jnp
from jax import lax
from jax.sharding import PartitionSpec as P

SPK = 109
FIRST_DILATION = 512
STEP = 10


ROOT_HALF = 0.7071067811865476
BETA_ONE = 0.9
BETA_TWO = 0.999
ADAM_EPS = 1e-08
LEARN_RATE = 0.07
DECAY = 0.01
CLIP_NORM = 1.0


def shifted(block, axis, distance):
    devices = range(lax.axis_size(axis))
    route = [(i - distance, i) for i in devices if i - distance in devices]
    return lax.ppermute(block, axis, route)


def segment_ids(sample_positions, clip_length_array):
    ends = jnp.cumsum(clip_length_array)
    return jnp.sum((sample_positions[:, None] >= ends[None, :]).astype(jnp.int32), axis=1)


def lagged_valid_mask(sample_positions, clip_length_array, span):
    here = segment_ids(sample_positions, clip_length_array)
    there = segment_ids(sample_positions - span, clip_length_array)
    return ((sample_positions >= span) & (here == there)).astype(jnp.float32)


def matmul(left, right):
    return jnp.dot(left, right, preferred_element_type=jnp.float32)


def inner_left(left, right):
    return lax.dot_general(
        left, right, (((0,), (0,)), ((), ())), preferred_element_type=jnp.float32
    )


def inner_right(left, right):
    return lax.dot_general(
        left, right, (((1,), (1,)), ((), ())), preferred_element_type=jnp.float32
    )


def phase_move(value_list, forward_pass):
    input_rows, channel_width = value_list.shape
    block_list = input_rows // FIRST_DILATION
    grouped = lax.all_to_all(
        value_list.reshape(block_list, FIRST_DILATION, channel_width),
        "tm",
        split_axis=1,
        concat_axis=0,
        tiled=True,
    )
    blank = jnp.zeros((1,) + grouped.shape[1:], value_list.dtype)
    if forward_pass:
        moved = jnp.concatenate([blank, grouped[:-1]], axis=0)
    else:
        moved = jnp.concatenate([grouped[1:], blank], axis=0)
    back = lax.all_to_all(moved, "tm", split_axis=0, concat_axis=1, tiled=True)
    return back.reshape(input_rows, channel_width)


def pull_lag(value_list, span):
    if span == 1:
        got = shifted(value_list[-1:], "tm", 1)
        return jnp.concatenate([got, value_list[:-1]], axis=0)
    else:
        return phase_move(value_list, True)


def push_lag(value_list, span):
    if span == 1:
        got = shifted(value_list[:1], "tm", -1)
        return jnp.concatenate([value_list[1:], got], axis=0)
    else:
        return phase_move(value_list, False)


def adamw_update_step(weight, mean, square, gradient_value, scale_factor):
    clipped = gradient_value * scale_factor
    new_mean = BETA_ONE * mean + (1.0 - BETA_ONE) * clipped
    new_square = BETA_TWO * square + (1.0 - BETA_TWO) * clipped * clipped
    fix_one = 1.0 - BETA_ONE**STEP
    fix_two = 1.0 - BETA_TWO**STEP
    update = new_mean / fix_one / (jnp.sqrt(new_square / fix_two) + ADAM_EPS)
    return (weight - LEARN_RATE * (update + DECAY * weight), new_mean, new_square)


def on_device(
    x_input,
    mel_frames,
    sample_mask,
    clip_length_array,
    speaker_ids,
    cot_out,
    cot_skip,
    dilated_kernel_weight,
    dilated_first_moment,
    dilated_second_moment,
    gate_bias,
    bias_mean,
    bias_square,
    mel_weight,
    mel_mean,
    mel_square,
    speaker_table,
    table_mean,
    table_square,
    residual_weight,
    residual_mean,
    residual_square,
    skip_weight,
    skip_mean,
    skip_square,
):
    input_rows = x_input.shape[0]
    sample_positions = lax.axis_index("tm") * input_rows + jnp.arange(input_rows, dtype=jnp.int32)
    valid_mask_list = (
        lagged_valid_mask(sample_positions, clip_length_array, FIRST_DILATION),
        lagged_valid_mask(sample_positions, clip_length_array, 1),
    )
    clip_spans = (FIRST_DILATION, 1)
    keep = sample_mask.astype(jnp.float32)[:, None]
    segment = segment_ids(sample_positions, clip_length_array)
    clip_count = clip_length_array.shape[0]
    clip_hot = (segment[:, None] == jnp.arange(clip_count, dtype=jnp.int32)[None, :]).astype(
        jnp.float32
    )
    speaker_clip = (speaker_ids[:, None] == jnp.arange(SPK, dtype=jnp.int32)[None, :]).astype(
        jnp.float32
    )
    speaker_hot = jnp.dot(clip_hot, speaker_clip).astype(jnp.bfloat16)
    mel_low = mel_frames.astype(jnp.bfloat16)
    (
        weight_dilated,
        weight_bias,
        weight_mel_projection,
        weight_speaker_table,
        weight_residual,
        weight_skip,
    ) = (
        lax.all_gather(dilated_kernel_weight.astype(jnp.bfloat16), "tm", axis=2, tiled=True),
        lax.all_gather(gate_bias.astype(jnp.bfloat16), "tm", axis=2, tiled=True),
        lax.all_gather(mel_weight.astype(jnp.bfloat16), "tm", axis=3, tiled=True),
        lax.all_gather(speaker_table.astype(jnp.bfloat16), "tm", axis=3, tiled=True),
        lax.all_gather(residual_weight.astype(jnp.bfloat16), "tm", axis=2, tiled=True),
        lax.all_gather(skip_weight.astype(jnp.bfloat16), "tm", axis=2, tiled=True),
    )
    residual_dimension = weight_dilated.shape[2]
    local_half_slice = weight_dilated.shape[4]
    local_gate_slice = 2 * local_half_slice

    def taps(layer_number):
        return (
            weight_dilated[layer_number, 0].reshape(residual_dimension, local_gate_slice),
            weight_dilated[layer_number, 1].reshape(residual_dimension, local_gate_slice),
        )

    saved = []
    state = x_input
    skip_sum = jnp.zeros((input_rows, weight_skip.shape[2] // lax.axis_size("mp")), jnp.float32)
    for layer_number in range(2):
        xin = lax.all_gather(state.astype(jnp.bfloat16), "mp", axis=1, tiled=True)
        lag = pull_lag(xin, clip_spans[layer_number]) * valid_mask_list[layer_number][
            :, None
        ].astype(jnp.bfloat16)
        far_tap_input, near_tap_input = taps(layer_number)
        z_value = matmul(lag, far_tap_input) + matmul(xin, near_tap_input)
        z_value = (
            z_value
            + weight_bias[layer_number].reshape(local_gate_slice).astype(jnp.float32)[None, :]
        )
        z_value = z_value + inner_left(
            mel_low, weight_mel_projection[layer_number].reshape(-1, local_gate_slice)
        )
        z_value = z_value + matmul(
            speaker_hot, weight_speaker_table[layer_number].reshape(-1, local_gate_slice)
        )
        tanh_a = jnp.tanh(z_value[:, :local_half_slice])
        sig_b = jax.nn.sigmoid(z_value[:, local_half_slice:])
        hidden = (keep * tanh_a * sig_b).astype(jnp.bfloat16)
        res_part, skip_part = (
            lax.psum_scatter(
                matmul(hidden, weight_residual[layer_number]), "mp", scatter_dimension=1, tiled=True
            ),
            lax.psum_scatter(
                matmul(hidden, weight_skip[layer_number]), "mp", scatter_dimension=1, tiled=True
            ),
        )
        state = (state + res_part) * ROOT_HALF
        skip_sum = skip_sum + skip_part
        saved.append((xin, lag, tanh_a, sig_b, hidden))
    grad_state = cot_out
    skip_grad = None
    layer_grads = [None, None]
    for layer_number in (1, 0):
        xin, lag, tanh_a, sig_b, hidden = saved[layer_number]
        res_half = (grad_state * ROOT_HALF).astype(jnp.bfloat16)
        if layer_number == 1:
            res_grad, skip_grad = (
                lax.all_gather(res_half, "mp", axis=1, tiled=True),
                lax.all_gather(cot_skip.astype(jnp.bfloat16), "mp", axis=1, tiled=True),
            )
        else:
            res_grad = lax.all_gather(res_half, "mp", axis=1, tiled=True)
        grad_hidden = inner_right(res_grad, weight_residual[layer_number]) + inner_right(
            skip_grad, weight_skip[layer_number]
        )
        grad_a = grad_hidden * keep * sig_b * (1.0 - tanh_a * tanh_a)
        grad_b = grad_hidden * keep * tanh_a * sig_b * (1.0 - sig_b)
        grad_z = jnp.concatenate([grad_a, grad_b], axis=1).astype(jnp.bfloat16)
        far_tap_input, near_tap_input = taps(layer_number)
        now_half, lag_half = (
            lax.psum_scatter(
                inner_right(grad_z, near_tap_input), "mp", scatter_dimension=1, tiled=True
            ),
            lax.psum_scatter(
                inner_right(grad_z, far_tap_input), "mp", scatter_dimension=1, tiled=True
            ),
        )
        lag_grad = (lag_half * valid_mask_list[layer_number][:, None]).astype(jnp.bfloat16)
        pushed = push_lag(lag_grad, clip_spans[layer_number]).astype(jnp.float32)
        grad_far = inner_left(lag, grad_z).reshape(residual_dimension, 2, local_half_slice)
        grad_near = inner_left(xin, grad_z).reshape(residual_dimension, 2, local_half_slice)
        partial_terms = (
            jnp.stack([grad_far, grad_near]),
            jnp.sum(grad_z.astype(jnp.float32), axis=0).reshape(2, local_half_slice),
            matmul(mel_low, grad_z).reshape(-1, 2, local_half_slice),
            inner_left(speaker_hot, grad_z).reshape(-1, 2, local_half_slice),
            inner_left(hidden, res_grad),
            inner_left(hidden, skip_grad),
        )
        layer_grads[layer_number] = partial_terms
        grad_state = grad_state * ROOT_HALF + now_half + pushed
    stacked = [jnp.stack([layer_grads[0][kind], layer_grads[1][kind]]) for kind in range(6)]
    (
        gradient_dilated,
        gradient_bias,
        gradient_mel_weight,
        gradient_speaker_table,
        gradient_residual,
        gradient_skip,
    ) = (
        lax.psum_scatter(stacked[0], "tm", scatter_dimension=2, tiled=True),
        lax.psum_scatter(stacked[1], "tm", scatter_dimension=2, tiled=True),
        lax.psum_scatter(stacked[2], "tm", scatter_dimension=3, tiled=True),
        lax.psum_scatter(stacked[3], "tm", scatter_dimension=3, tiled=True),
        lax.psum_scatter(stacked[4], "tm", scatter_dimension=2, tiled=True),
        lax.psum_scatter(stacked[5], "tm", scatter_dimension=2, tiled=True),
    )
    squares = jnp.float32(0.0)
    for gradient_value in (
        gradient_dilated,
        gradient_bias,
        gradient_mel_weight,
        gradient_speaker_table,
        gradient_residual,
        gradient_skip,
    ):
        squares = squares + jnp.sum(gradient_value * gradient_value)
    grad_norm = jnp.sqrt(lax.psum(squares, ("tm", "mp")))
    scale_factor = jnp.minimum(1.0, CLIP_NORM / grad_norm)
    result_list = []
    result_list.extend(
        adamw_update_step(
            dilated_kernel_weight,
            dilated_first_moment,
            dilated_second_moment,
            gradient_dilated,
            scale_factor,
        )
    )
    result_list.extend(
        adamw_update_step(gate_bias, bias_mean, bias_square, gradient_bias, scale_factor)
    )
    result_list.extend(
        adamw_update_step(mel_weight, mel_mean, mel_square, gradient_mel_weight, scale_factor)
    )
    result_list.extend(
        adamw_update_step(
            speaker_table, table_mean, table_square, gradient_speaker_table, scale_factor
        )
    )
    result_list.extend(
        adamw_update_step(
            residual_weight, residual_mean, residual_square, gradient_residual, scale_factor
        )
    )
    result_list.extend(
        adamw_update_step(skip_weight, skip_mean, skip_square, gradient_skip, scale_factor)
    )
    lows = [result_list[3 * index].astype(jnp.bfloat16) for index in range(6)]
    return (
        state,
        skip_sum,
        grad_state,
        grad_norm,
        gradient_dilated,
        gradient_bias,
        gradient_mel_weight,
        gradient_speaker_table,
        gradient_residual,
        gradient_skip,
        result_list[0],
        result_list[1],
        result_list[2],
        result_list[3],
        result_list[4],
        result_list[5],
        result_list[6],
        result_list[7],
        result_list[8],
        result_list[9],
        result_list[10],
        result_list[11],
        result_list[12],
        result_list[13],
        result_list[14],
        result_list[15],
        result_list[16],
        result_list[17],
        lows[0],
        lows[1],
        lows[2],
        lows[3],
        lows[4],
        lows[5],
    )


def solution(mesh):
    placed = (
        P("tm", "mp"),
        P(None, "tm"),
        P("tm"),
        P(),
        P(),
        P("tm", "mp"),
        P("tm", "mp"),
        P(None, None, "tm", None, "mp"),
        P(None, None, "tm", None, "mp"),
        P(None, None, "tm", None, "mp"),
        P(None, None, ("mp", "tm")),
        P(None, None, ("mp", "tm")),
        P(None, None, ("mp", "tm")),
        P(None, None, None, ("mp", "tm")),
        P(None, None, None, ("mp", "tm")),
        P(None, None, None, ("mp", "tm")),
        P(None, None, None, ("mp", "tm")),
        P(None, None, None, ("mp", "tm")),
        P(None, None, None, ("mp", "tm")),
        P(None, "mp", "tm"),
        P(None, "mp", "tm"),
        P(None, "mp", "tm"),
        P(None, "mp", "tm"),
        P(None, "mp", "tm"),
        P(None, "mp", "tm"),
    )
    return jax.shard_map(
        on_device,
        mesh=mesh,
        in_specs=placed,
        out_specs=(
            P("tm", "mp"),
            P("tm", "mp"),
            P("tm", "mp"),
            P(),
            P(None, None, "tm", None, "mp"),
            P(None, None, ("mp", "tm")),
            P(None, None, None, ("mp", "tm")),
            P(None, None, None, ("mp", "tm")),
            P(None, "mp", "tm"),
            P(None, "mp", "tm"),
            P(None, None, "tm", None, "mp"),
            P(None, None, "tm", None, "mp"),
            P(None, None, "tm", None, "mp"),
            P(None, None, ("mp", "tm")),
            P(None, None, ("mp", "tm")),
            P(None, None, ("mp", "tm")),
            P(None, None, None, ("mp", "tm")),
            P(None, None, None, ("mp", "tm")),
            P(None, None, None, ("mp", "tm")),
            P(None, None, None, ("mp", "tm")),
            P(None, None, None, ("mp", "tm")),
            P(None, None, None, ("mp", "tm")),
            P(None, "mp", "tm"),
            P(None, "mp", "tm"),
            P(None, "mp", "tm"),
            P(None, "mp", "tm"),
            P(None, "mp", "tm"),
            P(None, "mp", "tm"),
            P(None, None, "tm", None, "mp"),
            P(None, None, ("mp", "tm")),
            P(None, None, None, ("mp", "tm")),
            P(None, None, None, ("mp", "tm")),
            P(None, "mp", "tm"),
            P(None, "mp", "tm"),
        ),
        check_vma=False,
    )
```

profile of v0, /device:TPU:0, one launch (start us, length us, event | category | flops | bytes accessed | tf_op | source)
XLA Modules:
  0.0 846.4 jit_solution(4731055952956641881)
XLA Ops:
  13.7 3.8 reduce
  18.7 8.2 all-to-all-start
  28.2 44.0 %all_gather.35 = bf16[2,2,256]{1,0,2:T(2,128)(2,1)S(1)} all-gather(bf16[2,2,16]{1,0,2:T(2,128)(2,1)S(1)} %copy.250), channel_id=1, replica_groups=mesh['tm'=16,'mp'=2] {'tm'}, dimensions={2}, use_global_device_ids=true | all-gather | bytes 2176 | tf_op jit(solution)/shard_map/all_gather | solution.py:152
  73.1 39.1 %all_gather.37 = bf16[2,109,2,256]{1,3,2,0:T(8,128)(2,1)S(1)} all-gather(bf16[2,109,2,16]{1,3,2,0:T(8,128)(2,1)S(1)} %convert_element_type.177), channel_id=1, replica_groups=mesh['tm'=16,'mp'=2] {'tm'}, dimensions={3}, use_global_device_ids=true | all-gather | bytes 237184 | tf_op jit(solution)/shard_map/all_gather | solution.py:154
  113.8 3.6 all-to-all-start.1
  117.4 42.5 %all_gather.36 = bf16[2,80,2,256]{1,3,2,0:T(8,128)(2,1)S(1)} all-gather(bf16[2,80,2,16]{1,3,2,0:T(8,128)(2,1)S(1)} %convert_element_type.175), channel_id=1, replica_groups=mesh['tm'=16,'mp'=2] {'tm'}, dimensions={3}, use_global_device_ids=true | all-gather | bytes 174080 | tf_op jit(solution)/shard_map/all_gather | solution.py:153
  161.6 39.2 %all_gather.38 = bf16[2,256,512]{1,2,0:T(8,128)(2,1)S(1)} all-gather(bf16[2,256,32]{1,2,0:T(8,128)(2,1)S(1)} %convert_element_type.179), channel_id=1, replica_groups=mesh['tm'=16,'mp'=2] {'tm'}, dimensions={2}, use_global_device_ids=true | all-gather | bytes 557056 | tf_op jit(solution)/shard_map/all_gather | solution.py:155
  201.0 3.6 fusion.64
  214.5 42.1 %all_gather.40 = bf16[2,256,512]{1,2,0:T(8,128)(2,1)} all-gather(bf16[2,256,32]{1,2,0:T(8,128)(2,1)S(1)} %convert_element_type.187), channel_id=1, replica_groups=mesh['tm'=16,'mp'=2] {'tm'}, dimensions={2}, use_global_device_ids=true | all-gather | bytes 557056 | tf_op jit(solution)/shard_map/all_gather | solution.py:156
  263.0 2.8 collective-permute-start
  272.5 2.7 fusion.44
  275.2 3.9 reduce-scatter.20.cloned.1.call-done
  282.4 8.5 %reduce-scatter.18.cloned.1.call-done = f32[512,256]{1,0:T(8,128)} async-done(((f32[512,512]{1,0:T(8,128)}), f32[512,256]{1,0:T(8,128)}) %reduce-scatter.18.cloned.1.call-update) | async-done | bytes 524304 | tf_op jit(solution)/shard_map/reduce_scatter | solution.py:223
  329.3 2.6 copy.255
  333.3 2.4 pad_maximum_fusion
  344.6 6.9 all-to-all-start.2
  354.9 45.1 %reduce-scatter.34.cloned.1.call-done = f32[16,4]{1,0:T(8,128)} async-done(((f32[256,4]{1,0:T(8,128)}), f32[16,4]{1,0:T(8,128)}) %reduce-scatter.34.cloned.1.call-update) | async-done | bytes 272
  402.6 3.5 all-to-all-start.3
  406.2 69.7 %reduce-scatter.28.cloned.1.call-done = f32[2,80,2,16]{1,3,2,0:T(8,128)} async-done(((f32[2,80,2,256]{1,3,2,0:T(8,128)}), f32[2,80,2,16]{1,3,2,0:T(8,128)}) %reduce-scatter.28.cloned.1.call-update) | async-done | bytes 20496 | tf_op jit(solution)/shard_map/reduce_scatter | solution.py:255
  477.2 74.6 %reduce-scatter.30.cloned.1.call-done = f32[2,109,2,16]{1,3,2,0:T(8,128)} async-done(((f32[2,109,2,256]{1,3,2,0:T(8,128)}), f32[2,109,2,16]{1,3,2,0:T(8,128)}) %reduce-scatter.30.cloned.1.call-update) | async-done | bytes 27920 | tf_op jit(solution)/shard_map/reduce_scatter | solution.py:256
  553.1 126.8 %all-reduce.7.cloned.1.call-done = (f32[2,256,512]{1,0,2:T(2,128)}, f32[2,256,512]{1,0,2:T(2,128)}) async-done(((f32[2,256,512]{1,0,2:T(2,128)}, f32[2,256,512]{1,0,2:T(2,128)}), (f32[2,256,512]{1,0,2:T(2,128)}, f32[2,256,512]{1,0,2:T(2,128)})) %all-reduce.7.cloned.1.call-update) | async-done | bytes 2097168
  682.9 93.9 %reduce-scatter.26.cloned.1.call-done = f32[2,2,32,2,256]{4,2,3,1,0:T(8,128)} async-done(((f32[2,2,512,2,256]{4,2,3,1,0:T(8,128)}), f32[2,2,32,2,256]{4,2,3,1,0:T(8,128)}) %reduce-scatter.26.cloned.1.call-update) | async-done | bytes 262160 | tf_op jit(solution)/shard_map/reduce_scatter | solution.py:253
  782.4 4.7 reduce-scatter.22.cloned.1.call-done
  789.2 40.5 %psum.7 = f32[]{:T(128)} all-reduce(f32[]{:T(128)S(6)} %add.275), channel_id=1, replica_groups=mesh['tm'=16,'mp'=2] {'tm','mp'}, use_global_device_ids=true, to_apply=%region_26.27 | all-reduce | flops 1 | bytes 8 | tf_op jit(solution)/shard_map/psum | solution.py:270
  (344 shorter events, 109.9 us)
Async XLA Ops:
  7.2 193.7 %all-gather.2.cloned.1.call-start = ((), (), s32[]{:S(2)}) async-start(), calls=%async_computation.15 | async-start | bytes 2228224 | tf_op jit(solution)/shard_map/all_gather | solution.py:151
  18.7 93.5 %all-to-all-start = ((bf16[16,2,8192]{2,1,0:T(2,128)(2,1)}), bf16[16,2,8192]{2,1,0:T(2,128)(2,1)S(1)}, u32[]{:S(2)}, u32[]{:S(2)}) async-start(bf16[16,2,8192]{2,1,0:T(2,128)(2,1)} %reshape.218), calls=%async_computation | async-start | bytes 1048576 | tf_op jit(solution)/shard_map/all_to_all | solution.py:56
  113.8 87.0 %all-to-all-start.1 = ((bf16[16,32,512]{2,1,0:T(8,128)(2,1)}), bf16[16,32,512]{2,1,0:T(8,128)(2,1)S(1)}, u32[]{:S(2)}, u32[]{:S(2)}) async-start(bf16[16,32,512]{2,1,0:T(8,128)(2,1)} %concatenate.20), calls=%async_computation.1 | async-start | bytes 1048576 | tf_op jit(solution)/shard_map/all_to_all | solution.py:68
  117.4 142.2 %reduce-scatter.14.cloned.1.call-start = ((), (), s32[]{:S(2)}) async-start(), calls=%async_computation.16 | async-start | bytes 1572864 | tf_op jit(solution)/shard_map/reduce_scatter | solution.py:192
  209.0 70.2 %reduce-scatter.20.cloned.1.call-start = ((), (), s32[]{:S(2)}) async-start(), calls=%async_computation.19 | async-start | bytes 1572864 | tf_op jit(solution)/shard_map/reduce_scatter | solution.py:226
  263.0 4.0 collective-permute-start
  272.4 18.6 %reduce-scatter.18.cloned.1.call-start = ((), (), s32[]{:S(2)}) async-start(), calls=%async_computation.18 | async-start | bytes 1572864 | tf_op jit(solution)/shard_map/reduce_scatter | solution.py:223
  275.2 64.8 %reduce-scatter.24.cloned.1.call-start = ((), (), s32[]{:S(2)}) async-start(), calls=%async_computation.21 | async-start | bytes 1572864 | tf_op jit(solution)/shard_map/reduce_scatter | solution.py:226
  280.3 10.6 %collective-permute-start.1 = (bf16[1,256]{1,0:T(2,128)(2,1)S(1)}, bf16[1,256]{1,0:T(2,128)(2,1)S(1)}, u32[]{:S(2)}, u32[]{:S(2)}) collective-permute-start(bf16[1,256]{1,0:T(2,128)(2,1)S(1)} %slice.134), channel_id=1, source_target_pairs={{2,0},{4,2},{6,4},{8,6},{10,8},{12,10},{14,12},{16,14},{18,16},{20... | collective-permute-start | bytes 1544 | tf_op jit(solution)/shard_map/ppermute | solution.py:23
  298.2 54.7 %reduce-scatter.16.cloned.1.call-start = ((), (), s32[]{:S(2)}) async-start(), calls=%async_computation.17 | async-start | bytes 1572864 | tf_op jit(solution)/shard_map/reduce_scatter | solution.py:192
  300.6 99.4 %reduce-scatter.34.cloned.1.call-start = ((), (), s32[]{:S(2)}) async-start(), calls=%async_computation.26 | async-start | bytes 139264
  312.7 163.1 %reduce-scatter.28.cloned.1.call-start = ((), (), s32[]{:S(2)}) async-start(), calls=%async_computation.23 | async-start | bytes 557056 | tf_op jit(solution)/shard_map/reduce_scatter | solution.py:255
  314.7 237.1 %reduce-scatter.30.cloned.1.call-start = ((), (), s32[]{:S(2)}) async-start(), calls=%async_computation.24 | async-start | bytes 557056 | tf_op jit(solution)/shard_map/reduce_scatter | solution.py:256
  316.2 363.7 %all-reduce.7.cloned.1.call-start = ((), (), s32[]{:S(2)}) async-start(), calls=%async_computation.27 | async-start | bytes 4194304
  322.4 454.5 %reduce-scatter.26.cloned.1.call-start = ((), (), s32[]{:S(2)}) async-start(), calls=%async_computation.22 | async-start | bytes 4456448 | tf_op jit(solution)/shard_map/reduce_scatter | solution.py:253
  335.8 451.4 %reduce-scatter.22.cloned.1.call-start = ((), (), s32[]{:S(2)}) async-start(), calls=%async_computation.20 | async-start | bytes 1572864 | tf_op jit(solution)/shard_map/reduce_scatter | solution.py:223
  344.6 56.9 %all-to-all-start.2 = ((bf16[16,2,4096]{2,1,0:T(2,128)(2,1)}), bf16[16,2,4096]{2,1,0:T(2,128)(2,1)S(1)}, u32[]{:S(2)}, u32[]{:S(2)}) async-start(bf16[16,2,4096]{2,1,0:T(2,128)(2,1)} %reshape.220), calls=%async_computation.8 | async-start | bytes 524288 | tf_op jit(solution)/shard_map/all_to_all | solution.py:56
  351.5 487.2 %reduce-scatter.32.cloned.1.call-start = ((), (), s32[]{:S(2)}) async-start(), calls=%async_computation.25 | async-start | bytes 1572864 | tf_op jit(solution)/shard_map/reduce_scatter | solution.py:195
  354.9 432.3 %copy-start.5 = (f32[512,256]{1,0:T(8,128)S(1)}, f32[512,256]{1,0:T(8,128)}, u32[]{:S(2)}) copy-start(f32[512,256]{1,0:T(8,128)} %param.30) | copy-start | bytes 1572868
  354.9 432.3 %copy-start.29 = (bf16[511,256]{1,0:T(8,128)(2,1)S(1)}, bf16[511,256]{1,0:T(8,128)(2,1)}, u32[]{:S(2)}) copy-start(bf16[511,256]{1,0:T(8,128)(2,1)} %slice.133) | copy-start | bytes 784900
  354.9 432.3 %copy-start.30 = (f32[512,256]{1,0:T(8,128)S(1)}, f32[512,256]{1,0:T(8,128)}, u32[]{:S(2)}) copy-start(f32[512,256]{1,0:T(8,128)} %reduce-scatter.18.cloned.1.call-done) | copy-start | bytes 1572868
  354.9 432.3 %copy-start.77 = (bf16[1,256]{1,0:T(2,128)(2,1)S(1)}, bf16[1,256]{1,0:T(2,128)(2,1)}, u32[]{:S(2)}) copy-start(bf16[1,256]{1,0:T(2,128)(2,1)} %copy-done.76) | copy-start | bytes 1540
  400.9 434.4 %copy-start.66 = (f32[2,2,16]{2,1,0:T(2,128)}, f32[2,2,16]{2,1,0:T(2,128)S(1)}, u32[]{:S(2)}) copy-start(f32[2,2,16]{2,1,0:T(2,128)S(1)} %copy.284) | copy-start | bytes 772
  402.6 384.6 %all-to-all-start.3 = ((bf16[16,32,256]{2,1,0:T(8,128)(2,1)}), bf16[16,32,256]{2,1,0:T(8,128)(2,1)S(1)}, u32[]{:S(2)}, u32[]{:S(2)}) async-start(bf16[16,32,256]{2,1,0:T(8,128)(2,1)} %concatenate.25), calls=%async_computation.9 | async-start | bytes 524288 | tf_op jit(solution)/shard_map/all_to_all | solution.py:68
  (81 other events, 2150.3 us)
Sparse Core Ops, SparseCore 0:
  11.4 67.5 all-gather.1
  209.1 5.7 reduce-scatter.13
  272.5 6.5 reduce-scatter.19
  281.2 9.6 reduce-scatter.17
  298.3 9.6 reduce-scatter.23
  310.2 9.6 reduce-scatter.15
  322.8 77.1 reduce-scatter.33
  402.8 72.9 reduce-scatter.27
  478.8 72.9 reduce-scatter.29
  557.1 122.7 all-reduce.6
  682.3 94.5 reduce-scatter.25
  779.0 8.0 reduce-scatter.21
  790.0 9.6 reduce-scatter.31
where the time goes:
time: 848 us; the launch traced here: 846 us
  waiting for transfers between devices  428 us (50%)
  blocking collectives  259 us (31%)
  local copies, waits for them, and re-layouts  43.2 us (5%)
  other arithmetic  41.5 us (5%)
  starting transfers between devices  27.1 us (3%)
  matrix products  26.1 us (3%)
  between operations  21.7 us (3%)
    unnamed x15, waiting for transfers between devices  172 us
    reduce_scatter x1, waiting for transfers between devices, on_device(): lax.psum_scatter(stacked[0], 'tm', scatter_dimension=2, tiled=True)  93.9 us
    reduce_scatter x1, waiting for transfers between devices, on_device(): lax.psum_scatter(stacked[3], 'tm', scatter_dimension=3, tiled=True)  74.6 us
    reduce_scatter x1, waiting for transfers between devices, on_device(): lax.psum_scatter(stacked[2], 'tm', scatter_dimension=3, tiled=True)  69.7 us
    all_gather x1, blocking collectives, on_device(): lax.all_gather(gate_bias.astype(jnp.bfloat16), 'tm', axis=2, tiled=True)  44 us
    all_gather x1, blocking collectives, on_device(): lax.all_gather(mel_weight.astype(jnp.bfloat16), 'tm', axis=3, tiled=True)  42.5 us
    all_gather x1, blocking collectives, on_device(): lax.all_gather(skip_weight.astype(jnp.bfloat16), 'tm', axis=2, tiled=True)  42.1 us
    psum x1, blocking collectives, on_device(): grad_norm = jnp.sqrt(lax.psum(squares, ('tm', 'mp')))  40.5 us
  transfers between devices with their start and end apart: 19, of which 9 were waited for; matrix products, arithmetic and copies ran while one was open for 10% of the time, Pallas kernels for 0%

commit v1 on v0

v1 whole, which is shorter than its diff:
```python
import functools

import jax
import jax.numpy as jnp
from jax import lax
from jax.experimental import pallas as pl
from jax.experimental.pallas import tpu as pltpu
from jax.sharding import PartitionSpec as P

FIRST_DILATION = 512
STEP = 10
ROOT_HALF = 0.7071067811865476
BETA_ONE = 0.9
BETA_TWO = 0.999
ADAM_EPS = 1e-08
LEARN_RATE = 0.07
DECAY = 0.01
CLIP_NORM = 1.0

F32 = jnp.float32
BF16 = jnp.bfloat16
LANES = 128
EDGE = 8
BLOCKS = 16
NEAR = 4
VMEM_BYTES = 26 * 1024 * 1024
BOTH = ("tm", "mp")


def struct(shape, dtype=F32):
    return jax.ShapeDtypeStruct(shape, dtype)


def call(body, out_shape, *operands, scalars=(), scratch=(), space=pltpu.VMEM, unread=(), flops=1024, grant=VMEM_BYTES):
    specs = [pl.BlockSpec(memory_space=pltpu.SMEM)] * len(scalars)
    specs += [pl.BlockSpec(memory_space=space)] * len(operands)
    specs += [pl.BlockSpec(memory_space=pl.ANY)] * len(unread)
    return pl.pallas_call(
        body,
        out_shape=out_shape,
        in_specs=specs,
        scratch_shapes=list(scratch),
        compiler_params=pltpu.CompilerParams(vmem_limit_bytes=grant),
        cost_estimate=pl.CostEstimate(flops=flops, bytes_accessed=1024, transcendentals=0),
    )(*scalars, *operands, *unread)


def dot(left, right):
    return jnp.dot(left, right, preferred_element_type=F32)


def dot_right(left, right):
    return lax.dot_general(left, right, (((1,), (1,)), ((), ())), preferred_element_type=F32)


def dot_left(left, right):
    return lax.dot_general(left, right, (((0,), (0,)), ((), ())), preferred_element_type=F32)


def place():
    index = lax.axis_index("tm")
    core = lax.axis_index("mp")
    return index // NEAR, index % NEAR, core, 1 + core, 2 - core


def route(target):
    return [
        (index * 2 + core, target(index, core) * 2 + core)
        for index in range(lax.axis_size("tm"))
        for core in range(2)
    ]


def across(value, bit):
    return lax.ppermute(value, BOTH, route(lambda i, c: i ^ (1 + (c ^ bit))))


def along_far(value, distance):
    far = lax.axis_size("tm") // NEAR
    return lax.ppermute(
        value, BOTH, route(lambda i, c: (i // NEAR + distance) % far * NEAR + i % NEAR)
    )


def swap_cores(value):
    return lax.ppermute(value, "mp", [(0, 1), (1, 0)])


def shifted(value, axis, distance):
    devices = range(lax.axis_size(axis))
    pairs = [(i - distance, i) for i in devices if i - distance in devices]
    return lax.ppermute(value, axis, pairs)


def crossed(value, distance):
    parts = lax.axis_size("tm")
    pairs = [
        (index * 2 + core, (index + distance) * 2 + 1 - core)
        for index in range(parts)
        for core in range(2)
        if 0 <= index + distance < parts
    ]
    return lax.ppermute(value, BOTH, pairs)


def sections(rows):
    found, at = [], 0
    for count in (rows,) * 6 + (rows // 2,):
        found.append((at, count))
        at += count
    return found, at


WHERE, ROWS = sections(32)


def dilated_view(array):
    layers, taps, rows, halves, width = array.shape
    tiles = width // LANES
    split = array.reshape(layers, taps, rows, halves, tiles, LANES)
    return split.transpose(0, 1, 2, 4, 3, 5).reshape(-1, LANES)


def dilated_back(array, shape):
    layers, taps, rows, halves, width = shape
    tiles = width // LANES
    split = array.reshape(layers, taps, rows, tiles, halves, LANES)
    return split.transpose(0, 1, 2, 4, 3, 5).reshape(shape)


def strided(layer, tap, half, tile, rows):
    return pl.ds((layer * 2 + tap) * rows * 4 + tile * 2 + half, rows, stride=4)


def start_body(rows, mel, clips, who, *refs):
    sources, inputs, (out_one, out_two, kept, given, low) = refs[:6], refs[6:9], refs[9:14]
    held, samples, sems = refs[14:20], refs[20], refs[21]
    core = place()[2]
    own, width = kept.shape[0], kept.shape[1] // 3
    copies = [
        pltpu.make_async_copy(source, target, sems.at[index])
        for index, (source, target) in enumerate(zip(sources + inputs[:1], held + (samples,)))
    ]
    moves = []
    for index, source in enumerate(inputs):
        columns = pl.ds(index * width, width)
        for half, target in ((core, kept), (1 - core, given)):
            moves.append(
                pltpu.make_async_copy(
                    source.at[pl.ds(half * own, own), :],
                    target.at[:, columns],
                    sems.at[len(copies) + len(moves)],
                )
            )
    for copy in copies + moves:
        copy.start()
    dil, res, skip, mel_w, table, bias = held
    where, total = sections(rows)
    chans = rows // 2
    speakers = table.shape[-1]
    lane = lax.broadcasted_iota(jnp.int32, (1, speakers), 1)
    hot = jnp.concatenate([(lane == who[k]).astype(F32) for k in range(clips)], axis=0).astype(BF16)
    eye = lax.broadcasted_iota(jnp.int32, (chans, chans), 0) == lax.broadcasted_iota(
        jnp.int32, (chans, chans), 1
    )

    def write(out, at, count, columns, value):
        out[at : at + count, columns] = value.astype(out.dtype)

    for copy in copies:
        copy.wait()
    for layer, out in enumerate((out_one, out_two)):
        for tap in range(2):
            for half in range(2):
                at, count = where[2 * tap + half]
                for tile in range(2):
                    part = dil[strided(layer, tap, half, tile, rows), :]
                    write(out, at, count, slice(tile * LANES, (tile + 1) * LANES), part)
        for kind, source in ((4, res), (5, skip)):
            at, count = where[kind]
            write(out, at, count, slice(None), source[layer])
        at, count = where[6]
        for half in range(2):
            picked = dot_right(table[layer, half].astype(BF16), hot)
            line = jnp.broadcast_to(bias[layer, half : half + 1, :], (chans, chans))
            column = jnp.sum(jnp.where(eye, line, 0.0), axis=1, keepdims=True)
            blank = jnp.zeros((chans, LANES - mel - clips - 1), F32)
            row = jnp.concatenate([mel_w[layer, half], picked, column, blank], axis=1)
            columns = slice(half * LANES, (half + 1) * LANES)
            write(out, at, count, columns, row.astype(BF16).astype(F32))
    low[...] = samples[...].astype(BF16)
    for move in moves:
        move.wait()


def assemble_body(group, first, second, last, *refs):
    out = refs[-1]
    count = group.shape[0]
    far, near, _, first_bit, second_bit = place()
    for ref, mask in ((group, 0), (first, first_bit), (second, second_bit), (last, 3)):
        for back in range(count):
            out[lax.rem(far + count - back, count) * NEAR + (near ^ mask)] = ref[back]


def relay_body(value, *refs):
    out, token = refs[-2:]
    out[...] = value[...]
    token[...] = jnp.zeros_like(token)


TOKEN = struct((8, LANES))
LONG = 20_000_000_000


def stack_body(count, *refs):
    out, token = refs[-2:]
    for index in range(count):
        out[index] = refs[index][...]
    token[...] = jnp.zeros_like(token)


def along_all(pack, unread):
    far = lax.axis_size("tm") // NEAR
    got = [along_far(pack, distance) for distance in range(1, far)]
    return call(
        functools.partial(stack_body, far),
        (struct((far,) + pack.shape, BF16), TOKEN),
        pack,
        *got,
        unread=unread,
    )


def near_exchange(group, before_last):
    first = across(group, 0)
    second = across(group, 1)
    passed, token = call(
        relay_body, (struct(first.shape, BF16), TOKEN), first, unread=(second,) + before_last
    )
    return (group, first, second, across(passed, 1)), token


def joined(parts, before_end):
    count = NEAR * parts[0].shape[0]
    own = call(
        assemble_body, struct((count,) + parts[0].shape[1:], BF16), *parts, unread=before_end
    )
    if count != BLOCKS:
        own = to_canonical(own)
    return own, swap_cores(own)


def to_canonical(gathered):
    parts = gathered.shape[0]
    where, total = sections(BLOCKS * 32 // parts)
    return jnp.concatenate(
        [gathered[:, at : at + n, :].reshape(BLOCKS, -1, 256) for at, n in where], axis=1
    )


def from_canonical(packed, parts):
    where, total = sections(32)
    return jnp.concatenate(
        [packed[:, at : at + n, :].reshape(parts, -1, 256) for at, n in where], axis=1
    )


def piece(ref, kind):
    at, count = WHERE[kind]
    return ref[:, at : at + count, :].reshape(-1, 256)


def conditioning(ref, half):
    at, count = WHERE[6]
    return ref[:, at : at + count, half * LANES : (half + 1) * LANES].reshape(-1, LANES)


def slot(ordered, first, block):
    if not ordered:
        return block
    near = lax.axis_index("tm") % NEAR
    mask = (block % NEAR) ^ near
    group = jnp.where(mask == 3, 0, jnp.where(mask == 0, 3, jnp.where(mask == first, 2, 1)))
    return group * (BLOCKS // NEAR) + block // NEAR


def store(ref, slots, kind, value):
    at, count = WHERE[kind]
    value = value.astype(BF16)
    for block in range(BLOCKS):
        ref[slots[block], at : at + count, :] = value[block * count : (block + 1) * count]


def store_conditioning(ref, slots, half, value):
    at, count = WHERE[6]
    value = value.astype(BF16)
    for block in range(BLOCKS):
        ref[slots[block], at : at + count, half * LANES : (half + 1) * LANES] = value[
            block * count : (block + 1) * count
        ]


def order_body(own, other, own_out, other_out):
    parts = own.shape[0]
    far = parts // NEAR
    _, near, _, first, second = place()
    for source, out, bit, next_bit in (
        (own, own_out, first, second),
        (other, other_out, second, first),
    ):
        for group, mask in enumerate((3, next_bit, bit, 0)):
            for index in range(far):
                out[group * far + index] = source[index * NEAR + (near ^ mask)]


def first_sum_body(own, got, *refs):
    out, token = refs[-2:]
    half = out.shape[0]
    out[...] = own[:half] + got[:half]
    token[...] = jnp.zeros_like(token)


def second_sum_body(own, got, near_got, *refs):
    out, token = refs[-2:]
    count = out.shape[0]
    kept = slice(2 * count, 3 * count)
    out[...] = (
        own[kept].astype(F32) + got[kept].astype(F32) + near_got[:count].astype(F32)
    ).astype(BF16)
    token[...] = jnp.zeros_like(token)


def third_sum_body(own, got, near_got, last_got, *refs):
    far = place()[0]
    count = last_got.shape[0]
    token = refs[-1]
    token[...] = jnp.zeros_like(token)
    for distance, out in enumerate(refs[-count - 1 : -1]):
        index = lax.rem(far + distance, count)
        out[...] = (
            own[3 * count + index].astype(F32)
            + got[3 * count + index].astype(F32)
            + near_got[count + index].astype(F32)
            + last_got[index].astype(F32)
        ).astype(out.dtype)


def ordered(grads):
    parts = lax.axis_size("tm")
    return grads if parts == BLOCKS else from_canonical(grads, parts)


def cores_summed(own, other, unread=()):
    own, other = ordered(own), ordered(other)
    if own.shape[0] != BLOCKS:
        own, other = call(order_body, (struct(own.shape, BF16),) * 2, own, other)
    got = swap_cores(other)
    half = struct((own.shape[0] // 2,) + own.shape[1:], BF16)
    sent, token = call(first_sum_body, (half, TOKEN), own, got, unread=unread)
    return (own, got), sent, token


def near_summed(grads, sent, flops=1024, unread=()):
    near_got = across(sent, 1)
    shape = (grads[0].shape[0] // NEAR,) + grads[0].shape[1:]
    sent, token = call(
        second_sum_body,
        (struct(shape, BF16), TOKEN),
        *grads,
        near_got,
        flops=flops,
        unread=unread,
    )
    return grads + (near_got,), sent, token


def far_terms(grads, last_got, unread=()):
    far, *shape = last_got.shape
    kept, *sends, token = call(
        third_sum_body,
        (struct(shape),) + (struct(shape, BF16),) * (far - 1) + (TOKEN,),
        *grads,
        last_got,
        unread=unread,
    )
    return [kept] + [along_far(value, k + 1) for k, value in enumerate(sends)], token


def gates(weights, lag, xin, cond):
    za = dot(lag, piece(weights, 0)) + dot(xin, piece(weights, 2))
    za = za + dot_right(cond, conditioning(weights, 0))
    zb = dot(lag, piece(weights, 1)) + dot(xin, piece(weights, 3))
    zb = zb + dot_right(cond, conditioning(weights, 1))
    return jnp.tanh(za), jax.nn.sigmoid(zb)


def gate_gradients(weights, res_grad, skip_grad, keep, tanh_a, sig_b):
    hidden_grad = dot(res_grad, piece(weights, 4)) + dot(skip_grad, piece(weights, 5))
    hidden_grad = hidden_grad * keep
    grad_a = (hidden_grad * sig_b * (1.0 - tanh_a * tanh_a)).astype(BF16)
    grad_b = (hidden_grad * tanh_a * sig_b * (1.0 - sig_b)).astype(BF16)
    return grad_a, grad_b


def weight_gradients(out, bit, lag, xin, cond, grad_a, grad_b, res_grad, skip_grad, hidden):
    slots = [slot(lax.axis_size("tm") == BLOCKS, bit, block) for block in range(BLOCKS)]
    store(out, slots, 0, dot_left(lag, grad_a))
    store(out, slots, 1, dot_left(lag, grad_b))
    store(out, slots, 2, dot_left(xin, grad_a))
    store(out, slots, 3, dot_left(xin, grad_b))
    store(out, slots, 4, dot_left(res_grad, hidden))
    store(out, slots, 5, dot_left(skip_grad, hidden))
    store_conditioning(out, slots, 0, dot_left(grad_a, cond))
    store_conditioning(out, slots, 1, dot_left(grad_b, cond))


def first_body(own, x, lag_raw, cond, marks, weights, *refs):
    earlier, (u2, s1, lag_out, ta, sb, hid, token) = refs[:-7], refs[-7:]
    token[...] = jnp.zeros_like(token)
    keep = marks[:, 0:1]
    xin = x[...].astype(BF16)
    lag = (lag_raw[...].astype(F32) * marks[:, 1:2]).astype(BF16)
    tanh_a, sig_b = gates(weights, lag, xin, cond[...])
    hidden = (keep * tanh_a * sig_b).astype(BF16)
    res = dot_right(hidden, piece(weights, 4))
    skip = dot_right(hidden[:own], piece(weights, 5))
    ta[...] = tanh_a[:own]
    sb[...] = sig_b[:own]
    hid[...] = hidden[:own]
    lag_out[...] = lag[:own]
    if len(earlier) == 2:
        u2[...] = (x[...] + (earlier[0][...] + res)) * ROOT_HALF
        s1[...] = earlier[1][...] + skip
    else:
        u2[...] = res
        s1[...] = skip


def second_input(u2, marks):
    xin = u2[...].astype(BF16)
    lag = (pltpu.roll(xin.astype(F32), 1, 0) * marks[:, 2:3]).astype(BF16)
    return xin, lag


def second_forward_body(u2, cond, marks, weights, ta, sb):
    xin, lag = second_input(u2, marks)
    ta[...], sb[...] = gates(weights, lag, xin, cond[...])


def second_body(own, u2, s1, cond, marks, cot, cot_skip, weights, *refs):
    last = len(refs) > 5
    earlier, (mixed, total, g2, lag_sum, grads) = refs[:-5], refs[-5:]
    rows = u2.shape[0]
    keep = marks[:, 0:1]
    xin, lag = second_input(u2, marks)
    res_grad = (cot[...] * ROOT_HALF).astype(BF16)
    skip_grad = cot_skip[...]
    if last:
        tanh_a, sig_b = earlier[4][...], earlier[5][...]
    else:
        tanh_a, sig_b = gates(weights, lag, xin, cond[...])
    hidden = (keep * tanh_a * sig_b).astype(BF16)[:own]
    grad_a, grad_b = gate_gradients(weights, res_grad, skip_grad, keep, tanh_a, sig_b)
    _, _, _, first_bit, second_bit = place()
    weight_gradients(
        grads,
        first_bit if last else second_bit,
        lag[:own],
        xin[:own],
        cond[:own, :],
        grad_a[:own],
        grad_b[:own],
        res_grad[:own],
        skip_grad[:own],
        hidden,
    )
    res = dot_right(hidden, piece(weights, 4))
    skip = dot_right(hidden, piece(weights, 5))
    lag_grad = dot_right(grad_a, piece(weights, 0)) + dot_right(grad_b, piece(weights, 1))
    now = dot_right(grad_a[:own], piece(weights, 2)) + dot_right(grad_b[:own], piece(weights, 3))
    if last:
        res, skip, now, lag_grad = (
            before[...] + value for before, value in zip(earlier, (res, skip, now, lag_grad))
        )
        mixed[...] = (u2[:own, :] + res) * ROOT_HALF
        total[...] = s1[...] + skip
        pushed = (lag_grad * marks[:, 2:3]).astype(BF16).astype(F32)
        g2[...] = cot[:own, :] * ROOT_HALF + now + pltpu.roll(pushed, rows - 1, 0)[:own]
    else:
        mixed[...] = res
        total[...] = skip
        g2[...] = now
        lag_sum[...] = lag_grad


def third_body(own, last, g2, x, lag, cond, marks, cot_skip, ta, sb, hid, weights, *refs):
    earlier, (g1, dlag, lag_sum, grads) = refs[:-4], refs[-4:]
    keep = marks[:own, 0:1]
    xin = x[:own, :].astype(BF16)
    res_grad = (g2[...] * ROOT_HALF).astype(BF16)
    skip_grad = cot_skip[:own, :]
    grad_a, grad_b = gate_gradients(weights, res_grad, skip_grad, keep, ta[...], sb[...])
    _, _, _, first_bit, second_bit = place()
    weight_gradients(
        grads,
        first_bit if last else second_bit,
        lag[...],
        xin,
        cond[:own, :],
        grad_a,
        grad_b,
        res_grad,
        skip_grad,
        hid[...],
    )
    lag_grad = dot_right(grad_a, piece(weights, 0)) + dot_right(grad_b, piece(weights, 1))
    now = dot_right(grad_a, piece(weights, 2)) + dot_right(grad_b, piece(weights, 3))
    if last:
        g1[...] = g2[...] * ROOT_HALF + (earlier[0][...] + now)
        dlag[...] = ((earlier[1][...] + lag_grad) * marks[:own, 1:2]).astype(BF16)
    else:
        g1[...] = now
        lag_sum[...] = lag_grad


def join_body(kept, got, mel, mask, x, cot, skip, side, before, after, tail):
    core = place()[2]
    own, width = kept.shape[0], kept.shape[1] // 3
    for index, ref in enumerate((x, cot, skip)):
        for source, at in ((kept, core), (got, 1 - core)):
            value = source[:, index * width : (index + 1) * width]
            ref[:, pl.ds(at * width, width)] = value.astype(ref.dtype)
    bands = mel.shape[0]
    samples = pl.ds(core * own, own)
    stack = jnp.concatenate(
        [
            mel[:, samples],
            mask[:, samples].astype(F32),
            jnp.zeros((LANES - bands - 1, own), F32),
        ],
        axis=0,
    )
    side[...] = stack.T
    full = 2 * width
    for ref, edge in ((before, own - EDGE), (after, 0)):
        ref[:, :LANES] = side[edge : edge + EDGE, :]
        ref[:, LANES : LANES + full] = x[edge : edge + EDGE, :]
    before[:, LANES + full :] = x[:EDGE, :]
    tail[...] = x[own - EDGE :, :]
    after[:, LANES + full : LANES + 2 * full] = cot[:EDGE, :]
    after[:, LANES + 2 * full :] = skip[:EDGE, :]


def widen_body(
    mel,
    clips,
    lengths,
    x,
    cot,
    skip,
    side,
    before,
    after,
    x_out,
    cot_out,
    skip_out,
    cond,
    marks,
):
    far, near, core = place()[:3]
    own, full = x.shape
    wide = own + 2 * EDGE

    def widened(at, inner):
        return jnp.concatenate(
            [inner, after[:, at : at + inner.shape[1]], before[:, at : at + inner.shape[1]]], axis=0
        )

    x_wide = widened(LANES, x[...])
    x_out[...] = x_wide
    blank = jnp.zeros((EDGE, full), F32)
    cot_out[...] = jnp.concatenate(
        [cot[...], after[:, LANES + full : LANES + 2 * full], blank], axis=0
    )
    skip_out[...] = jnp.concatenate([skip[...], after[:, LANES + 2 * full :], blank], axis=0).astype(
        BF16
    )
    side_wide = widened(0, side[...])
    lane = lax.broadcasted_iota(jnp.int32, (wide, LANES), 1)
    line = lax.broadcasted_iota(jnp.int32, (wide, LANES), 0)
    first = ((far * NEAR + near) * 2 + core) * own
    position = first + jnp.where(line < own + EDGE, line, line - wide)

    def segment(at):
        total = jnp.zeros((wide, LANES), jnp.int32)
        end = jnp.int32(0)
        for clip in range(clips):
            end = end + lengths[clip]
            total = total + (at >= end).astype(jnp.int32)
        return total

    here = segment(position)

    def valid(span):
        return ((position >= span) & (segment(position - span) == here)).astype(F32)

    hot = ((lane - mel) == here).astype(F32)
    value = jnp.where(lane < mel, side_wide, jnp.where(lane < mel + clips, hot, 0.0))
    cond[...] = jnp.where(lane == mel + clips, 1.0, value).astype(BF16)
    keep = side_wide[:, mel : mel + 1]
    marks[...] = jnp.where(
        lane == 0, keep, jnp.where(lane == 1, valid(FIRST_DILATION), valid(1))
    )


def lag_body(same, other, before, tail, out):
    core = place()[2]
    own, width = same.shape[0] // 2, same.shape[1]
    for source, at in ((same, core), (other, 1 - core)):
        out[:own, pl.ds(at * width, width)] = source[pl.ds(core * own, own), :]
    edges = [before[:, LANES + 2 * width :], tail[...]]
    out[own:, :] = jnp.concatenate(edges, axis=0).astype(BF16)


def divide_body(mixed, total, g1, kept, given):
    core = place()[2]
    width = kept.shape[1] // 3
    for index, ref in enumerate((mixed, total, g1)):
        kept[:, index * width : (index + 1) * width] = ref[:, pl.ds(core * width, width)]
        given[:, index * width : (index + 1) * width] = ref[:, pl.ds((1 - core) * width, width)]


def finish_body(kept, got, *refs):
    core = place()[2]
    outs, token = refs[:-1], refs[-1]
    token[...] = jnp.zeros_like(token)
    own, width = kept.shape[0], kept.shape[1] // 3
    for index, ref in enumerate(outs):
        for source, at in ((kept, core), (got, 1 - core)):
            ref[pl.ds(at * own, own), :] = source[:, index * width : (index + 1) * width]


def push_body(dlag, *refs):
    core = place()[2]
    same, other = refs[-2:]
    width = same.shape[1]
    same[...] = dlag[:, pl.ds(core * width, width)]
    other[...] = dlag[:, pl.ds((1 - core) * width, width)]


def input_gradient_body(g1, same, other, out):
    core = place()[2]
    own = same.shape[0]
    for source, at in ((same, core), (other, 1 - core)):
        lines = pl.ds(at * own, own)
        out[lines, :] = g1[lines, :] + source[...].astype(F32)


def table_gradient(cond_grad, who, mel, clips, speakers):
    lane = lax.broadcasted_iota(jnp.int32, (cond_grad.shape[0], speakers), 1)
    result = jnp.zeros((cond_grad.shape[0], speakers), F32)
    for clip in range(clips):
        column = cond_grad[:, mel + clip : mel + clip + 1]
        result = result + jnp.where(lane == who[clip], column, 0.0)
    return result


def square_body(rows, mel, clips, speakers, count, who, *refs):
    terms, (out, squares) = refs[:count], refs[-2:]
    where, total = sections(rows)
    start = where[6][0]
    value = terms[0][...]
    for term in terms[1:]:
        value = value + term[...].astype(F32)
    out[...] = value
    main = out[:start, :]
    amount = jnp.sum(main * main, keepdims=True)
    for half in range(2):
        block = out[start:, half * LANES : (half + 1) * LANES]
        lane = lax.broadcasted_iota(jnp.int32, block.shape, 1)
        plain = jnp.where((lane < mel) | (lane == mel + clips), block, 0.0)
        amount = amount + jnp.sum(plain * plain, keepdims=True)
        table = table_gradient(block, who, mel, clips, speakers)
        amount = amount + jnp.sum(table * table, keepdims=True)
    squares[...] = jnp.broadcast_to(amount, squares.shape)


def adamw(weight, mean, square, gradient, scale):
    clipped = gradient * scale
    new_mean = BETA_ONE * mean + (1.0 - BETA_ONE) * clipped
    new_square = BETA_TWO * square + (1.0 - BETA_TWO) * clipped * clipped
    fix_one = 1.0 - BETA_ONE**STEP
    fix_two = 1.0 - BETA_TWO**STEP
    update = new_mean / fix_one / (jnp.sqrt(new_square / fix_two) + ADAM_EPS)
    return weight - LEARN_RATE * (update + DECAY * weight), new_mean, new_square


def update_body(rows, mel, clips, who, *refs):
    grads = refs[0:2]
    squares = refs[2]
    old = [refs[3 + 3 * kind : 6 + 3 * kind] for kind in range(6)]
    norm = refs[21]
    new = [refs[22 + 5 * kind : 27 + 5 * kind] for kind in range(6)]
    where, total = sections(rows)
    chans = rows // 2
    grad_norm = jnp.sqrt(jnp.sum(squares[...], axis=0, keepdims=True)[:, 0:1])
    norm[...] = grad_norm
    scale = jnp.minimum(1.0, CLIP_NORM / grad_norm)

    def write(kind, index, gradient):
        weight, mean, square = (ref[index] for ref in old[kind])
        new_weight, new_mean, new_square = adamw(weight, mean, square, gradient, scale)
        for ref, value in zip(
            new[kind],
            (gradient, new_weight, new_mean, new_square, new_weight.astype(BF16)),
        ):
            ref[index] = value

    dil = new[0][0]
    for layer in range(2):
        for tap in range(2):
            for half in range(2):
                at, n = where[2 * tap + half]
                for tile in range(2):
                    dil[strided(layer, tap, half, tile, rows), :] = grads[layer][
                        at : at + n, tile * LANES : (tile + 1) * LANES
                    ]
    weight, mean, square = (ref[...] for ref in old[0])
    new_weight, new_mean, new_square = adamw(weight, mean, square, dil[...], scale)
    new[0][1][...] = new_weight
    new[0][2][...] = new_mean
    new[0][3][...] = new_square
    new[0][4][...] = new_weight.astype(BF16)
    for layer in range(2):
        for half in range(2):
            block = grads[layer][where[6][0] :, half * LANES : (half + 1) * LANES]
            eye = lax.broadcasted_iota(jnp.int32, (chans, chans), 0) == lax.broadcasted_iota(
                jnp.int32, (chans, chans), 1
            )
            column = block[:, mel + clips : mel + clips + 1]
            line = jnp.sum(jnp.where(eye, column, 0.0), axis=0, keepdims=True)
            write(1, (layer, slice(half, half + 1), slice(None)), line)
            write(2, (layer, half), block[:, :mel])
            speakers = old[3][0].shape[-1]
            write(3, (layer, half), table_gradient(block, who, mel, clips, speakers))
        for kind, section in ((4, 4), (5, 5)):
            at, n = where[section]
            write(kind, (layer,), grads[layer][at : at + n, :])


def on_device(
    x_input,
    mel_frames,
    sample_mask,
    clip_length_array,
    speaker_ids,
    cot_out,
    cot_skip,
    *states,
):
    parts = lax.axis_size("tm")
    held_rows, width = x_input.shape
    own, full = held_rows // 2, 2 * width
    wide = own + 2 * EDGE
    mel = mel_frames.shape[0]
    clips = clip_length_array.shape[0]
    hop = FIRST_DILATION // held_rows

    dil_shape = states[0].shape
    rows = dil_shape[2]
    views = (
        [dilated_view(s) for s in states[0:3]]
        + list(states[3:6])
        + [s.transpose(0, 2, 3, 1) for s in states[6:12]]
        + [s.transpose(0, 2, 1) for s in states[12:18]]
    )
    speakers = views[9].shape[-1]
    where, total = sections(rows)
    far = parts // NEAR
    taken = [views[k] for k in (0, 12, 15, 6, 9, 3)]
    packed_type = BF16 if rows % 32 == 0 else F32
    taken = [views[k] for k in (0, 12, 15, 6, 9, 3)]
    packed_type = BF16 if rows % 32 == 0 else F32
    pack_one, pack_two, kept, given, x_low = call(
        functools.partial(start_body, rows, mel, clips),
        (struct((total, 256), packed_type),) * 2
        + (struct((own, 3 * width)),) * 2
        + (struct(x_input.shape, BF16),),
        *taken,
        x_input,
        cot_out,
        cot_skip,
        scalars=(speaker_ids,),
        space=pl.ANY,
        grant=None,
        scratch=[pltpu.VMEM(v.shape, F32) for v in taken + [x_input]]
        + [pltpu.SemaphoreType.DMA((len(taken) + 7,))],
    )
    lag_same = shifted(x_low, "tm", hop)
    lag_other = swap_cores(lag_same)

    x_own, cot_own, skip_own, side, before, after, tail = call(
        join_body,
        (
            struct((own, full)),
            struct((own, full)),
            struct((own, full)),
            struct((own, LANES)),
            struct((EDGE, LANES + 2 * full)),
            struct((EDGE, LANES + 3 * full)),
            struct((EDGE, full)),
        ),
        kept,
        swap_cores(given),
        mel_frames,
        sample_mask[None, :],
    )
    before = shifted(before, BOTH, 1)
    x_wide, cot_wide, skip_wide, cond, marks = call(
        functools.partial(widen_body, mel, clips),
        (
            struct((wide, full)),
            struct((wide, full)),
            struct((wide, full), BF16),
            struct((wide, LANES), BF16),
            struct((wide, LANES)),
        ),
        x_own,
        cot_own,
        skip_own,
        side,
        before,
        shifted(after, BOTH, -1),
        scalars=(clip_length_array,),
    )
    group_one, stacked = along_all(pack_one.astype(BF16), (marks, lag_same))
    pack_two, _ = call(
        relay_body, (struct(pack_two.shape, BF16), TOKEN), pack_two.astype(BF16), unread=(stacked,)
    )
    group_two, stacked = along_all(pack_two, ())
    lag_wide = call(
        lag_body,
        struct((wide, full), BF16),
        lag_same,
        lag_other,
        before,
        shifted(tail, BOTH, 2 * hop + 1),
    )
    parts_one, _ = near_exchange(group_one, (stacked, lag_wide))
    parts_two, begun = near_exchange(group_two, ())
    w1_own, w1_oth = joined(parts_one, ())

    half = struct((own, width))
    wave = struct((own, full))
    broad = struct((wide, full))
    low_half = struct((own, width), BF16)
    low_full = struct((own, full), BF16)
    packed = struct((BLOCKS, ROWS, 256), BF16)

    def forward(weights, *earlier, unread=(), flops=1024):
        return call(
            functools.partial(first_body, own),
            (broad, wave, low_full, half, half, low_half, TOKEN),
            x_wide,
            lag_wide,
            cond,
            marks,
            weights,
            *earlier,
            unread=unread,
            flops=flops,
        )

    res, skip, lag1, ta_own, sb_own, hid_own, _ = forward(w1_own, unread=(begun,), flops=LONG)
    u2, s1, _, ta_oth, sb_oth, hid_oth, token = forward(w1_oth, res, skip)

    w2_own, w2_oth = joined(parts_two, (token,))

    def middle(weights, *earlier):
        return call(
            functools.partial(second_body, own),
            (wave, wave, wave, TOKEN if earlier else broad, packed),
            u2,
            s1,
            cond,
            marks,
            cot_wide,
            skip_wide,
            weights,
            *earlier,
        )

    gate_two = call(
        second_forward_body, (struct((wide, width)),) * 2, u2, cond, marks, w2_own
    )
    *sums, grad_oth = middle(w2_oth)
    mixed, skip_total, g2, _, grad_own = middle(w2_own, *sums, *gate_two)

    def totals(terms, unread=()):
        return call(
            functools.partial(square_body, rows, mel, clips, speakers, len(terms)),
            (struct((total, 256)), struct((8, LANES))),
            *terms,
            scalars=(speaker_ids,),
            unread=unread,
        )

    def backward(weights, tanh_a, sig_b, hidden, *earlier, unread):
        last = bool(earlier)
        return call(
            functools.partial(third_body, own, last),
            (wave, low_full if last else TOKEN, TOKEN if last else wave, packed),
            g2,
            x_wide,
            lag1,
            cond,
            marks,
            skip_wide,
            tanh_a,
            sig_b,
            hidden,
            weights,
            *earlier,
            unread=unread,
        )

    grads2, sent2, token = cores_summed(grad_own, grad_oth)
    now, _, lag_sum, grad_oth = backward(w1_oth, ta_oth, sb_oth, hid_oth, unread=(token,))
    grads2, sent2, token = near_summed(grads2, sent2, LONG)
    g1_part, dlag1, _, grad_own = backward(
        w1_own, ta_own, sb_own, hid_own, now, lag_sum, unread=()
    )
    grads1, sent1, _ = cores_summed(grad_own, grad_oth, (token,))
    kept, given = call(
        divide_body, (struct((own, 3 * width)),) * 2, mixed, skip_total, g1_part
    )
    mixed, skip_total, grad_input, token = call(
        finish_body, (struct((held_rows, width)),) * 3 + (TOKEN,), kept, swap_cores(given)
    )
    last_got = across(sent2, 0)
    grads1, sent1, _ = near_summed(grads1, sent1, unread=(last_got, token))
    terms2, _ = far_terms(grads2, last_got)
    terms1, token = far_terms(grads1, across(sent1, 0))
    same, other = call(push_body, (low_half,) * 2, dlag1, unread=(token,))
    same = shifted(same, "tm", -hop)
    other = crossed(other, -hop)
    grad_input = call(input_gradient_body, struct((held_rows, width)), grad_input, same, other)

    sum2, squares2 = totals(terms2)
    sum1, squares1 = totals(terms1, (same, other))
    squares = squares1[:1] + squares2[:1]
    squares = squares + swap_cores(squares)
    sent = jnp.broadcast_to(squares[None], (parts, 1, LANES))
    squares = lax.all_to_all(sent, "tm", split_axis=0, concat_axis=0, tiled=True)
    outs = [struct((1, 1))]
    for view in views[0::3]:
        outs += [struct(view.shape)] * 4 + [struct(view.shape, BF16)]
    updated = call(
        functools.partial(update_body, rows, mel, clips),
        tuple(outs),
        sum1,
        sum2,
        squares.reshape(parts, LANES),
        *views,
        scalars=(speaker_ids,),
    )
    grad_norm = updated[0].reshape(())
    backs = (
        [lambda v: dilated_back(v, dil_shape), lambda v: v]
        + [lambda v: v.transpose(0, 3, 1, 2)] * 2
        + [lambda v: v.transpose(0, 2, 1)] * 2
    )
    new = [
        [back(v) for v in updated[1 + 5 * kind : 6 + 5 * kind]] for kind, back in enumerate(backs)
    ]
    return (
        mixed,
        skip_total,
        grad_input,
        grad_norm,
        *[group[0] for group in new],
        *[value for group in new for value in group[1:4]],
        *[group[4] for group in new],
    )


def solution(mesh):
    rows = P("tm", "mp")
    dil = P(None, None, "tm", None, "mp")
    bias = P(None, None, ("mp", "tm"))
    wide = P(None, None, None, ("mp", "tm"))
    square = P(None, "mp", "tm")
    kinds = (dil, bias, wide, wide, square, square)
    thrice = tuple(kind for kind in kinds for _ in range(3))
    return jax.shard_map(
        on_device,
        mesh=mesh,
        in_specs=(rows, P(None, "tm"), P("tm"), P(), P(), rows, rows) + thrice,
        out_specs=(rows, rows, rows, P()) + kinds + thrice + kinds,
        check_vma=False,
    )
```

time: 848 us -> 159 us (0.19)
  waiting for transfers between devices: 428 us -> 69 us
  blocking collectives: 259 us -> 0 us
  other arithmetic: 41.5 us -> 0.01 us
  local copies, waits for them, and re-layouts: 43.2 us -> 1.87 us
  starting transfers between devices: 27.1 us -> 61.6 us
  matrix products: 26.1 us -> 0 us
  Pallas kernels: 0 us -> 25.3 us
  between operations: 21.7 us -> 1.29 us
    reduce_scatter x10 -> x0, waiting for transfers between devices: 255 us -> none  [the longest x1 93.9 us: on_device(): lax.psum_scatter(stacked[0], 'tm', scatter_dimension=2, tiled=True)]
    all_gather x10 -> x0, blocking collectives: 218 us -> none  [the longest x1 44 us: on_device(): lax.all_gather(gate_bias.astype(jnp.bfloat16), 'tm', axis=2, tiled=True)]
    unnamed x15 -> x0, waiting for transfers between devices: 172 us -> none
    ppermute x2 -> x36, waiting for transfers between devices: 0.6 us -> 62.6 us  [the longest x10 32.9 us: across(): return lax.ppermute(value, BOTH, route(lambda i, c: i ^ 1 + (c ^ bit)))]
    ppermute x2 -> x36, starting transfers between devices: 4.13 us -> 57.2 us  [the longest x12 23.7 us: along_far(): lax.ppermute(value, BOTH, route(lambda i, c: (i // NEAR + distance) % far...]
    psum x1 -> x0, blocking collectives: 40.5 us -> none  [on_device(): grad_norm = jnp.sqrt(lax.psum(squares, ('tm', 'mp')))]
    dot_general x31 -> x0, matrix products: 25.6 us -> none  [the longest x8 10.4 us: inner_right(): lax.dot_general(left, right, (((1,), (1,)), ((), ())), preferred_element_...]
    pallas_call x0 -> x31, Pallas kernels: none -> 25.3 us  [call(): pl.pallas_call(body, out_shape=out_shape, in_specs=specs, scratch_shapes=...]
  transfers between devices with their start and end apart: 19 -> 37, of which waited for: 9 -> 19; matrix products, arithmetic and copies ran while one was open for 10% -> 0% of each run, Pallas kernels for 0% -> 9%
where the time goes in v1:
time: 159 us
  waiting for transfers between devices  69 us (43%)
  starting transfers between devices  61.6 us (39%)
  Pallas kernels  25.3 us (16%)
  local copies, waits for them, and re-layouts  1.87 us (1%)
    ppermute x10, waiting for transfers between devices, across(): return lax.ppermute(value, BOTH, route(lambda i, c: i ^ 1 + (c ^ bit)))  32.9 us
    pallas_call x31, Pallas kernels, call(): pl.pallas_call(body, out_shape=out_shape, in_specs=specs, scratch_shapes=...  25.3 us
    ppermute x12, starting transfers between devices, along_far(): lax.ppermute(value, BOTH, route(lambda i, c: (i // NEAR + distance) % far...  23.7 us
    ppermute x12, waiting for transfers between devices, along_far(): lax.ppermute(value, BOTH, route(lambda i, c: (i // NEAR + distance) % far...  15.8 us
    ppermute x10, starting transfers between devices, across(): return lax.ppermute(value, BOTH, route(lambda i, c: i ^ 1 + (c ^ bit)))  15.4 us
    ppermute x5, starting transfers between devices, shifted(): return lax.ppermute(value, axis, pairs)  10.4 us
    ppermute x8, waiting for transfers between devices, swap_cores(): return lax.ppermute(value, 'mp', [(0, 1), (1, 0)])  9.3 us
    all_to_all x1, waiting for transfers between devices, on_device(): lax.all_to_all(sent, 'tm', split_axis=0, concat_axis=0, tiled=True)  6.36 us
  transfers between devices with their start and end apart: 37, of which 19 were waited for; matrix products, arithmetic and copies ran while one was open for 0% of the time, Pallas kernels for 9%

profile of v1, /device:TPU:0, one launch (start us, length us, event | category | flops | bytes accessed | tf_op | source)
XLA Modules:
  0.0 159.1 jit_solution(3433754977472441317)
XLA Ops:
  0.7 3.9 %shard_map.504 = (bf16[208,256]{1,0:T(8,128)(2,1)}, bf16[208,256]{1,0:T(8,128)(2,1)}, f32[256,768]{1,0:T(8,128)}, f32[256,768]{1,0:T(8,128)}, bf16[512,256]{1,0:T(8,128)(2,1)}) custom-call(s32[8]{0:T(128)} %who.7, f32[512,128]{1,0:T(8,128)} %bitcast.77, f32[2,32,256]{2,1,0:T(8,128)} %bitcast.81, f32[2,32,256]{2,1,0:T(8,128)} %bitcast.83, ...), custom_call_target="tpu_custom_call" | custom-call | flops 1024 | bytes 1024 | tf_op jit(solution)/shard_map/pallas_call | solution.py:38
  5.1 4.4 %collective-permute-start.3 = (bf16[512,256]{1,0:T(8,128)(2,1)}, bf16[512,256]{1,0:T(8,128)(2,1)S(1)}, u32[]{:S(2)}, u32[]{:S(2)}) collective-permute-start(bf16[512,256]{1,0:T(8,128)(2,1)} %get-tuple-element.155), channel_id=1, source_target_pairs={{0,2},{2,4},{4,6},{6,8},{8,10},{10,12},{12,14},{14,16},{16,18},{18... | collective-permute-start | bytes 786440 | tf_op jit(solution)/shard_map/ppermute | solution.py:92
  9.6 3.6 %collective-permute-start.8 = (bf16[208,256]{1,0:T(8,128)(2,1)}, bf16[208,256]{1,0:T(8,128)(2,1)S(1)}, u32[]{:S(2)}, u32[]{:S(2)}) collective-permute-start(bf16[208,256]{1,0:T(8,128)(2,1)} %get-tuple-element.159.refs_0_), channel_id=1, source_target_pairs={{0,24},{1,25},{2,26},{3,27},{4,28},{5,29},{6,30},{7,31},{8,0},{9,1... | collective-permute-start | bytes 319496 | tf_op jit(solution)/shard_map/ppermute | solution.py:80
  19.1 3.8 %collective-permute-done.2.after = f32[8,1664]{1,0:T(8,128)S(1)} collective-permute-done((f32[8,1664]{1,0:T(8,128)S(1)}, f32[8,1664]{1,0:T(8,128)S(1)}, u32[]{:S(2)}, u32[]{:S(2)}) %collective-permute-start.2) | collective-permute-done | bytes 53280 | tf_op jit(solution)/shard_map/ppermute | solution.py:92
  23.9 4.3 %collective-permute-start.10 = (bf16[4,208,256]{2,1,0:T(8,128)(2,1)S(1)}, bf16[4,208,256]{2,1,0:T(8,128)(2,1)S(1)}, u32[]{:S(2)}, u32[]{:S(2)}) collective-permute-start(bf16[4,208,256]{2,1,0:T(8,128)(2,1)S(1)} %get-tuple-element.160.group), channel_id=1, source_target_pairs={{0,4},{1,3},{2,6},{3,1},{4,0},{5,7},{6,2},{7,5},{8,12},{9,11},{10,... | collective-permute-start | bytes 1277960 | tf_op jit(solution)/shard_map/ppermute | solution.py:75
  30.1 5.0 %collective-permute-start.4 = (bf16[512,256]{1,0:T(8,128)(2,1)S(1)}, bf16[512,256]{1,0:T(8,128)(2,1)S(1)}, u32[]{:S(2)}, u32[]{:S(2)}) collective-permute-start(bf16[512,256]{1,0:T(8,128)(2,1)S(1)} %collective-permute-done.3.same.refs_5_), channel_id=1, source_target_pairs={{0,1},{1,0},{2,3},{3,2},{4,5},{5,4},{6,7},{7,6},{8,9},{9,8},{10,11... | collective-permute-start | bytes 786440 | tf_op jit(solution)/shard_map/ppermute | solution.py:86
  39.2 3.8 %collective-permute-start.12 = (bf16[208,256]{1,0:T(8,128)(2,1)S(1)}, bf16[208,256]{1,0:T(8,128)(2,1)S(1)}, u32[]{:S(2)}, u32[]{:S(2)}) collective-permute-start(bf16[208,256]{1,0:T(8,128)(2,1)S(1)} %get-tuple-element.163.refs_0_), channel_id=1, source_target_pairs={{0,16},{1,17},{2,18},{3,19},{4,20},{5,21},{6,22},{7,23},{8,24},{9,... | collective-permute-start | bytes 319496 | tf_op jit(solution)/shard_map/ppermute | solution.py:80
  43.0 2.0 %collective-permute-start.11 = (bf16[208,256]{1,0:T(8,128)(2,1)S(1)}, bf16[208,256]{1,0:T(8,128)(2,1)S(1)}, u32[]{:S(2)}, u32[]{:S(2)}) collective-permute-start(bf16[208,256]{1,0:T(8,128)(2,1)S(1)} %get-tuple-element.163.refs_0_), channel_id=1, source_target_pairs={{0,8},{1,9},{2,10},{3,11},{4,12},{5,13},{6,14},{7,15},{8,16},{9,17... | collective-permute-start | bytes 319496 | tf_op jit(solution)/shard_map/ppermute | solution.py:80
  45.1 7.9 %collective-permute-done.12.refs_2_ = bf16[208,256]{1,0:T(8,128)(2,1)S(1)} collective-permute-done((bf16[208,256]{1,0:T(8,128)(2,1)S(1)}, bf16[208,256]{1,0:T(8,128)(2,1)S(1)}, u32[]{:S(2)}, u32[]{:S(2)}) %collective-permute-start.12) | collective-permute-done | bytes 106528 | tf_op jit(solution)/shard_map/ppermute | solution.py:80
  56.2 8.3 %collective-permute-done.17.refs_0_.second = bf16[4,208,256]{2,1,0:T(8,128)(2,1)S(1)} collective-permute-done((bf16[4,208,256]{2,1,0:T(8,128)(2,1)S(1)}, bf16[4,208,256]{2,1,0:T(8,128)(2,1)S(1)}, u32[]{:S(2)}, u32[]{:S(2)}) %collective-permute-start.17) | collective-permute-done | bytes 426016 | tf_op jit(solution)/shard_map/ppermute | solution.py:75
  70.6 2.3 %collective-permute-done.15.weights = bf16[16,208,256]{2,1,0:T(8,128)(2,1)S(1)} collective-permute-done((bf16[16,208,256]{2,1,0:T(8,128)(2,1)S(1)}, bf16[16,208,256]{2,1,0:T(8,128)(2,1)S(1)}, u32[]{:S(2)}, u32[]{:S(2)}) %collective-permute-start.15) | collective-permute-done | bytes 1703968 | tf_op jit(solution)/shard_map/ppermute | solution.py:86
  74.7 3.6 %collective-permute-done.19.weights = bf16[16,208,256]{2,1,0:T(8,128)(2,1)S(1)} collective-permute-done((bf16[16,208,256]{2,1,0:T(8,128)(2,1)S(1)}, bf16[16,208,256]{2,1,0:T(8,128)(2,1)S(1)}, u32[]{:S(2)}, u32[]{:S(2)}) %collective-permute-start.19) | collective-permute-done | bytes 1703968 | tf_op jit(solution)/shard_map/ppermute | solution.py:86
  78.3 2.1 %shard_map.517 = (f32[256,512]{1,0:T(8,128)S(1)}, f32[256,512]{1,0:T(8,128)S(1)}, f32[256,512]{1,0:T(8,128)S(1)}, f32[272,512]{1,0:T(8,128)S(1)}, bf16[16,208,256]{2,1,0:T(8,128)(2,1)S(1)}) custom-call(f32[272,512]{1,0:T(8,128)S(1)} %get-tuple-element.170.u2, f32[256,512]{1,0:T(8,128)S(1)} %get-tuple-element.171.s1, ...), custom_call_target="tpu_custom_call" | custom-call | flops 1024 | bytes 1024 | tf_op jit(solution)/shard_map/pallas_call | solution.py:38
  89.3 7.5 %collective-permute-done.23.near_got = bf16[8,208,256]{2,1,0:T(8,128)(2,1)S(1)} collective-permute-done((bf16[8,208,256]{2,1,0:T(8,128)(2,1)S(1)}, bf16[8,208,256]{2,1,0:T(8,128)(2,1)S(1)}, u32[]{:S(2)}, u32[]{:S(2)}) %collective-permute-start.23) | collective-permute-done | bytes 852000 | tf_op jit(solution)/shard_map/ppermute | solution.py:75
  102.9 9.5 %collective-permute-done.25.refs_0_.last_got = bf16[4,208,256]{2,1,0:T(8,128)(2,1)S(1)} collective-permute-done((bf16[4,208,256]{2,1,0:T(8,128)(2,1)S(1)}, bf16[4,208,256]{2,1,0:T(8,128)(2,1)S(1)}, u32[]{:S(2)}, u32[]{:S(2)}) %collective-permute-start.25) | collective-permute-done | bytes 426016 | tf_op jit(solution)/shard_map/ppermute | solution.py:75
  112.4 2.6 %collective-permute-done.24.near_got = bf16[8,208,256]{2,1,0:T(8,128)(2,1)S(1)} collective-permute-done((bf16[8,208,256]{2,1,0:T(8,128)(2,1)S(1)}, bf16[8,208,256]{2,1,0:T(8,128)(2,1)S(1)}, u32[]{:S(2)}, u32[]{:S(2)}) %collective-permute-start.24) | collective-permute-done | bytes 852000 | tf_op jit(solution)/shard_map/ppermute | solution.py:75
  117.2 2.2 %collective-permute-start.33 = (bf16[208,256]{1,0:T(8,128)(2,1)S(1)}, bf16[208,256]{1,0:T(8,128)(2,1)S(1)}, u32[]{:S(2)}, u32[]{:S(2)}) collective-permute-start(bf16[208,256]{1,0:T(8,128)(2,1)S(1)} %get-tuple-element.222), channel_id=1, source_target_pairs={{0,16},{1,17},{2,18},{3,19},{4,20},{5,21},{6,22},{7,23},{8,24},{9,... | collective-permute-start | bytes 319496 | tf_op jit(solution)/shard_map/ppermute | solution.py:80
  119.5 2.6 %collective-permute-start.34 = (bf16[208,256]{1,0:T(8,128)(2,1)S(1)}, bf16[208,256]{1,0:T(8,128)(2,1)S(1)}, u32[]{:S(2)}, u32[]{:S(2)}) collective-permute-start(bf16[208,256]{1,0:T(8,128)(2,1)S(1)} %get-tuple-element.223), channel_id=1, source_target_pairs={{0,24},{1,25},{2,26},{3,27},{4,28},{5,29},{6,30},{7,31},{8,0},{9,1... | collective-permute-start | bytes 319496 | tf_op jit(solution)/shard_map/ppermute | solution.py:80
  126.9 4.3 %collective-permute-start.29 = (bf16[208,256]{1,0:T(8,128)(2,1)S(1)}, bf16[208,256]{1,0:T(8,128)(2,1)S(1)}, u32[]{:S(2)}, u32[]{:S(2)}) collective-permute-start(bf16[208,256]{1,0:T(8,128)(2,1)S(1)} %get-tuple-element.216), channel_id=1, source_target_pairs={{0,8},{1,9},{2,10},{3,11},{4,12},{5,13},{6,14},{7,15},{8,16},{9,17... | collective-permute-start | bytes 319496 | tf_op jit(solution)/shard_map/ppermute | solution.py:80
  134.5 3.8 %collective-permute-done.29.refs_1_ = bf16[208,256]{1,0:T(8,128)(2,1)S(1)} collective-permute-done((bf16[208,256]{1,0:T(8,128)(2,1)S(1)}, bf16[208,256]{1,0:T(8,128)(2,1)S(1)}, u32[]{:S(2)}, u32[]{:S(2)}) %collective-permute-start.29) | collective-permute-done | bytes 106528 | tf_op jit(solution)/shard_map/ppermute | solution.py:80
  138.3 4.1 %collective-permute-done.30.refs_2_ = bf16[208,256]{1,0:T(8,128)(2,1)S(1)} collective-permute-done((bf16[208,256]{1,0:T(8,128)(2,1)S(1)}, bf16[208,256]{1,0:T(8,128)(2,1)S(1)}, u32[]{:S(2)}, u32[]{:S(2)}) %collective-permute-start.30) | collective-permute-done | bytes 106528 | tf_op jit(solution)/shard_map/ppermute | solution.py:80
  145.0 4.4 %all-to-all-start = ((f32[16,1,128]{2,1,0:T(1,128)}), f32[16,1,128]{2,1,0:T(1,128)S(1)}, u32[]{:S(2)}, u32[]{:S(2)}) async-start(f32[16,1,128]{2,1,0:T(1,128)} %broadcast_in_dim.13), calls=%async_computation | async-start | bytes 16384 | tf_op jit(solution)/shard_map/all_to_all | solution.py:954
  150.3 6.4 %all-to-all-done = f32[16,1,128]{2,1,0:T(1,128)S(1)} async-done(((f32[16,1,128]{2,1,0:T(1,128)}), f32[16,1,128]{2,1,0:T(1,128)S(1)}, u32[]{:S(2)}, u32[]{:S(2)}) %all-to-all-start) | async-done | bytes 8224 | tf_op jit(solution)/shard_map/all_to_all | solution.py:954
  156.8 2.2 %shard_map.534 = (f32[1,1]{1,0:T(1,128)}, f32[512,128]{1,0:T(8,128)}, f32[512,128]{1,0:T(8,128)}, f32[512,128]{1,0:T(8,128)}, f32[512,128]{1,0:T(8,128)}, /*inde...) custom-call(s32[8]{0:T(128)S(1)} %copy-done.20, ...), custom_call_target="tpu_custom_call" | custom-call | flops 1024 | bytes 1024 | tf_op jit(solution)/shard_map/pallas_call | solution.py:38
  (134 shorter events, 53.3 us)
Async XLA Ops:
  4.6 9.6 %collective-permute-start = (f32[256,768]{1,0:T(8,128)}, f32[256,768]{1,0:T(8,128)S(1)}, u32[]{:S(2)}, u32[]{:S(2)}) collective-permute-start(f32[256,768]{1,0:T(8,128)} %get-tuple-element.147), channel_id=1, source_target_pairs={{0,1},{1,0},{2,3},{3,2},{4,5},{5,4},{6,7},{7,6},{8,9},{9,8},{10,11... | collective-permute-start | bytes 2359304 | tf_op jit(solution)/shard_map/ppermute | solution.py:86
  5.1 18.7 %collective-permute-start.3 = (bf16[512,256]{1,0:T(8,128)(2,1)}, bf16[512,256]{1,0:T(8,128)(2,1)S(1)}, u32[]{:S(2)}, u32[]{:S(2)}) collective-permute-start(bf16[512,256]{1,0:T(8,128)(2,1)} %get-tuple-element.155), channel_id=1, source_target_pairs={{0,2},{2,4},{4,6},{6,8},{8,10},{10,12},{12,14},{14,16},{16,18},{18... | collective-permute-start | bytes 786440 | tf_op jit(solution)/shard_map/ppermute | solution.py:92
  9.6 14.3 %collective-permute-start.8 = (bf16[208,256]{1,0:T(8,128)(2,1)}, bf16[208,256]{1,0:T(8,128)(2,1)S(1)}, u32[]{:S(2)}, u32[]{:S(2)}) collective-permute-start(bf16[208,256]{1,0:T(8,128)(2,1)} %get-tuple-element.159.refs_0_), channel_id=1, source_target_pairs={{0,24},{1,25},{2,26},{3,27},{4,28},{5,29},{6,30},{7,31},{8,0},{9,1... | collective-permute-start | bytes 319496 | tf_op jit(solution)/shard_map/ppermute | solution.py:80
  13.2 10.7 %collective-permute-start.7 = (bf16[208,256]{1,0:T(8,128)(2,1)}, bf16[208,256]{1,0:T(8,128)(2,1)S(1)}, u32[]{:S(2)}, u32[]{:S(2)}) collective-permute-start(bf16[208,256]{1,0:T(8,128)(2,1)} %get-tuple-element.159.refs_0_), channel_id=1, source_target_pairs={{0,16},{1,17},{2,18},{3,19},{4,20},{5,21},{6,22},{7,23},{8,24},{9,... | collective-permute-start | bytes 319496 | tf_op jit(solution)/shard_map/ppermute | solution.py:80
  13.2 10.7 %collective-permute-start.6 = (bf16[208,256]{1,0:T(8,128)(2,1)}, bf16[208,256]{1,0:T(8,128)(2,1)S(1)}, u32[]{:S(2)}, u32[]{:S(2)}) collective-permute-start(bf16[208,256]{1,0:T(8,128)(2,1)} %get-tuple-element.159.refs_0_), channel_id=1, source_target_pairs={{0,8},{1,9},{2,10},{3,11},{4,12},{5,13},{6,14},{7,15},{8,16},{9,17... | collective-permute-start | bytes 319496 | tf_op jit(solution)/shard_map/ppermute | solution.py:80
  23.9 30.4 %collective-permute-start.10 = (bf16[4,208,256]{2,1,0:T(8,128)(2,1)S(1)}, bf16[4,208,256]{2,1,0:T(8,128)(2,1)S(1)}, u32[]{:S(2)}, u32[]{:S(2)}) collective-permute-start(bf16[4,208,256]{2,1,0:T(8,128)(2,1)S(1)} %get-tuple-element.160.group), channel_id=1, source_target_pairs={{0,4},{1,3},{2,6},{3,1},{4,0},{5,7},{6,2},{7,5},{8,12},{9,11},{10,... | collective-permute-start | bytes 1277960 | tf_op jit(solution)/shard_map/ppermute | solution.py:75
  28.2 26.1 %collective-permute-start.9 = (bf16[4,208,256]{2,1,0:T(8,128)(2,1)S(1)}, bf16[4,208,256]{2,1,0:T(8,128)(2,1)S(1)}, u32[]{:S(2)}, u32[]{:S(2)}) collective-permute-start(bf16[4,208,256]{2,1,0:T(8,128)(2,1)S(1)} %get-tuple-element.160.group), channel_id=1, source_target_pairs={{0,2},{1,5},{2,0},{3,7},{4,6},{5,1},{6,4},{7,3},{8,10},{9,13},{10,... | collective-permute-start | bytes 1277960 | tf_op jit(solution)/shard_map/ppermute | solution.py:75
  39.2 13.9 %collective-permute-start.12 = (bf16[208,256]{1,0:T(8,128)(2,1)S(1)}, bf16[208,256]{1,0:T(8,128)(2,1)S(1)}, u32[]{:S(2)}, u32[]{:S(2)}) collective-permute-start(bf16[208,256]{1,0:T(8,128)(2,1)S(1)} %get-tuple-element.163.refs_0_), channel_id=1, source_target_pairs={{0,16},{1,17},{2,18},{3,19},{4,20},{5,21},{6,22},{7,23},{8,24},{9,... | collective-permute-start | bytes 319496 | tf_op jit(solution)/shard_map/ppermute | solution.py:80
  43.0 10.1 %collective-permute-start.11 = (bf16[208,256]{1,0:T(8,128)(2,1)S(1)}, bf16[208,256]{1,0:T(8,128)(2,1)S(1)}, u32[]{:S(2)}, u32[]{:S(2)}) collective-permute-start(bf16[208,256]{1,0:T(8,128)(2,1)S(1)} %get-tuple-element.163.refs_0_), channel_id=1, source_target_pairs={{0,8},{1,9},{2,10},{3,11},{4,12},{5,13},{6,14},{7,15},{8,16},{9,17... | collective-permute-start | bytes 319496 | tf_op jit(solution)/shard_map/ppermute | solution.py:80
  53.1 11.4 %collective-permute-start.17 = (bf16[4,208,256]{2,1,0:T(8,128)(2,1)S(1)}, bf16[4,208,256]{2,1,0:T(8,128)(2,1)S(1)}, u32[]{:S(2)}, u32[]{:S(2)}) collective-permute-start(bf16[4,208,256]{2,1,0:T(8,128)(2,1)S(1)} %get-tuple-element.166.group), channel_id=1, source_target_pairs={{0,4},{1,3},{2,6},{3,1},{4,0},{5,7},{6,2},{7,5},{8,12},{9,11},{10,... | collective-permute-start | bytes 1277960 | tf_op jit(solution)/shard_map/ppermute | solution.py:75
  53.5 12.8 %collective-permute-start.16 = (bf16[4,208,256]{2,1,0:T(8,128)(2,1)S(1)}, bf16[4,208,256]{2,1,0:T(8,128)(2,1)S(1)}, u32[]{:S(2)}, u32[]{:S(2)}) collective-permute-start(bf16[4,208,256]{2,1,0:T(8,128)(2,1)S(1)} %get-tuple-element.166.group), channel_id=1, source_target_pairs={{0,2},{1,5},{2,0},{3,7},{4,6},{5,1},{6,4},{7,3},{8,10},{9,13},{10,... | collective-permute-start | bytes 1277960 | tf_op jit(solution)/shard_map/ppermute | solution.py:75
  54.9 14.1 %collective-permute-start.14 = (bf16[4,208,256]{2,1,0:T(8,128)(2,1)S(1)}, bf16[4,208,256]{2,1,0:T(8,128)(2,1)S(1)}, u32[]{:S(2)}, u32[]{:S(2)}) collective-permute-start(bf16[4,208,256]{2,1,0:T(8,128)(2,1)S(1)} %get-tuple-element.165), channel_id=1, source_target_pairs={{0,4},{1,3},{2,6},{3,1},{4,0},{5,7},{6,2},{7,5},{8,12},{9,11},{10,... | collective-permute-start | bytes 1277960 | tf_op jit(solution)/shard_map/ppermute | solution.py:75
  84.1 12.8 %collective-permute-start.23 = (bf16[8,208,256]{2,1,0:T(8,128)(2,1)S(1)}, bf16[8,208,256]{2,1,0:T(8,128)(2,1)S(1)}, u32[]{:S(2)}, u32[]{:S(2)}) collective-permute-start(bf16[8,208,256]{2,1,0:T(8,128)(2,1)S(1)} %get-tuple-element.206), channel_id=1, source_target_pairs={{0,4},{1,3},{2,6},{3,1},{4,0},{5,7},{6,2},{7,5},{8,12},{9,11},{10,... | collective-permute-start | bytes 2555912 | tf_op jit(solution)/shard_map/ppermute | solution.py:75
  97.7 17.3 %collective-permute-start.24 = (bf16[8,208,256]{2,1,0:T(8,128)(2,1)S(1)}, bf16[8,208,256]{2,1,0:T(8,128)(2,1)S(1)}, u32[]{:S(2)}, u32[]{:S(2)}) collective-permute-start(bf16[8,208,256]{2,1,0:T(8,128)(2,1)S(1)} %get-tuple-element.208), channel_id=1, source_target_pairs={{0,4},{1,3},{2,6},{3,1},{4,0},{5,7},{6,2},{7,5},{8,12},{9,11},{10,... | collective-permute-start | bytes 2555912 | tf_op jit(solution)/shard_map/ppermute | solution.py:75
  99.6 12.8 %collective-permute-start.25 = (bf16[4,208,256]{2,1,0:T(8,128)(2,1)S(1)}, bf16[4,208,256]{2,1,0:T(8,128)(2,1)S(1)}, u32[]{:S(2)}, u32[]{:S(2)}) collective-permute-start(bf16[4,208,256]{2,1,0:T(8,128)(2,1)S(1)} %get-tuple-element.209), channel_id=1, source_target_pairs={{0,2},{1,5},{2,0},{3,7},{4,6},{5,1},{6,4},{7,3},{8,10},{9,13},{10,... | collective-permute-start | bytes 1277960 | tf_op jit(solution)/shard_map/ppermute | solution.py:75
  117.2 9.7 %collective-permute-start.32 = (bf16[208,256]{1,0:T(8,128)(2,1)S(1)}, bf16[208,256]{1,0:T(8,128)(2,1)S(1)}, u32[]{:S(2)}, u32[]{:S(2)}) collective-permute-start(bf16[208,256]{1,0:T(8,128)(2,1)S(1)} %get-tuple-element.221), channel_id=1, source_target_pairs={{0,8},{1,9},{2,10},{3,11},{4,12},{5,13},{6,14},{7,15},{8,16},{9,17... | collective-permute-start | bytes 319496 | tf_op jit(solution)/shard_map/ppermute | solution.py:80
  117.2 14.0 %collective-permute-start.33 = (bf16[208,256]{1,0:T(8,128)(2,1)S(1)}, bf16[208,256]{1,0:T(8,128)(2,1)S(1)}, u32[]{:S(2)}, u32[]{:S(2)}) collective-permute-start(bf16[208,256]{1,0:T(8,128)(2,1)S(1)} %get-tuple-element.222), channel_id=1, source_target_pairs={{0,16},{1,17},{2,18},{3,19},{4,20},{5,21},{6,22},{7,23},{8,24},{9,... | collective-permute-start | bytes 319496 | tf_op jit(solution)/shard_map/ppermute | solution.py:80
  119.5 13.2 %collective-permute-start.34 = (bf16[208,256]{1,0:T(8,128)(2,1)S(1)}, bf16[208,256]{1,0:T(8,128)(2,1)S(1)}, u32[]{:S(2)}, u32[]{:S(2)}) collective-permute-start(bf16[208,256]{1,0:T(8,128)(2,1)S(1)} %get-tuple-element.223), channel_id=1, source_target_pairs={{0,24},{1,25},{2,26},{3,27},{4,28},{5,29},{6,30},{7,31},{8,0},{9,1... | collective-permute-start | bytes 319496 | tf_op jit(solution)/shard_map/ppermute | solution.py:80
  124.2 18.2 %collective-permute-start.27 = (bf16[256,256]{1,0:T(8,128)(2,1)S(1)}, bf16[256,256]{1,0:T(8,128)(2,1)S(1)}, u32[]{:S(2)}, u32[]{:S(2)}) collective-permute-start(bf16[256,256]{1,0:T(8,128)(2,1)S(1)} %get-tuple-element.213), channel_id=1, source_target_pairs={{2,0},{4,2},{6,4},{8,6},{10,8},{12,10},{14,12},{16,14},{18,16},{20... | collective-permute-start | bytes 393224 | tf_op jit(solution)/shard_map/ppermute | solution.py:92
  125.6 16.7 %collective-permute-start.28 = (bf16[256,256]{1,0:T(8,128)(2,1)S(1)}, bf16[256,256]{1,0:T(8,128)(2,1)S(1)}, u32[]{:S(2)}, u32[]{:S(2)}) collective-permute-start(bf16[256,256]{1,0:T(8,128)(2,1)S(1)} %get-tuple-element.214), channel_id=1, source_target_pairs={{2,1},{3,0},{4,3},{5,2},{6,5},{7,4},{8,7},{9,6},{10,9},{11,8},{12,... | collective-permute-start | bytes 393224 | tf_op jit(solution)/shard_map/ppermute | solution.py:103
  126.9 11.3 %collective-permute-start.29 = (bf16[208,256]{1,0:T(8,128)(2,1)S(1)}, bf16[208,256]{1,0:T(8,128)(2,1)S(1)}, u32[]{:S(2)}, u32[]{:S(2)}) collective-permute-start(bf16[208,256]{1,0:T(8,128)(2,1)S(1)} %get-tuple-element.216), channel_id=1, source_target_pairs={{0,8},{1,9},{2,10},{3,11},{4,12},{5,13},{6,14},{7,15},{8,16},{9,17... | collective-permute-start | bytes 319496 | tf_op jit(solution)/shard_map/ppermute | solution.py:80
  131.3 11.1 %collective-permute-start.30 = (bf16[208,256]{1,0:T(8,128)(2,1)S(1)}, bf16[208,256]{1,0:T(8,128)(2,1)S(1)}, u32[]{:S(2)}, u32[]{:S(2)}) collective-permute-start(bf16[208,256]{1,0:T(8,128)(2,1)S(1)} %get-tuple-element.217), channel_id=1, source_target_pairs={{0,16},{1,17},{2,18},{3,19},{4,20},{5,21},{6,22},{7,23},{8,24},{9,... | collective-permute-start | bytes 319496 | tf_op jit(solution)/shard_map/ppermute | solution.py:80
  132.6 9.8 %collective-permute-start.31 = (bf16[208,256]{1,0:T(8,128)(2,1)S(1)}, bf16[208,256]{1,0:T(8,128)(2,1)S(1)}, u32[]{:S(2)}, u32[]{:S(2)}) collective-permute-start(bf16[208,256]{1,0:T(8,128)(2,1)S(1)} %get-tuple-element.218), channel_id=1, source_target_pairs={{0,24},{1,25},{2,26},{3,27},{4,28},{5,29},{6,30},{7,31},{8,0},{9,1... | collective-permute-start | bytes 319496 | tf_op jit(solution)/shard_map/ppermute | solution.py:80
  145.0 11.6 %all-to-all-start = ((f32[16,1,128]{2,1,0:T(1,128)}), f32[16,1,128]{2,1,0:T(1,128)S(1)}, u32[]{:S(2)}, u32[]{:S(2)}) async-start(f32[16,1,128]{2,1,0:T(1,128)} %broadcast_in_dim.13), calls=%async_computation | async-start | bytes 16384 | tf_op jit(solution)/shard_map/all_to_all | solution.py:954
  (38 other events, 754.5 us)

commit v2 on v1

--- a/solution.py
+++ b/solution.py
@@ -92,14 +92,10 @@
     return lax.ppermute(value, axis, pairs)
 
 
-def crossed(value, distance):
-    parts = lax.axis_size("tm")
-    pairs = [
-        (index * 2 + core, (index + distance) * 2 + 1 - core)
-        for index in range(parts)
-        for core in range(2)
-        if 0 <= index + distance < parts
-    ]
+def across_chips(value):
+    pairs = []
+    for index in range(1, lax.axis_size("tm")):
+        pairs += [(index * 2 - 1, index * 2), (index * 2, index * 2 - 1)]
     return lax.ppermute(value, BOTH, pairs)
 
 
@@ -133,28 +129,14 @@
 
 
 def start_body(rows, mel, clips, who, *refs):
-    sources, inputs, (out_one, out_two, kept, given, low) = refs[:6], refs[6:9], refs[9:14]
-    held, samples, sems = refs[14:20], refs[20], refs[21]
-    core = place()[2]
-    own, width = kept.shape[0], kept.shape[1] // 3
+    sources, (out_one, out_two, low), held, sems = refs[:7], refs[7:10], refs[10:17], refs[17]
     copies = [
         pltpu.make_async_copy(source, target, sems.at[index])
-        for index, (source, target) in enumerate(zip(sources + inputs[:1], held + (samples,)))
+        for index, (source, target) in enumerate(zip(sources, held))
     ]
-    moves = []
-    for index, source in enumerate(inputs):
-        columns = pl.ds(index * width, width)
-        for half, target in ((core, kept), (1 - core, given)):
-            moves.append(
-                pltpu.make_async_copy(
-                    source.at[pl.ds(half * own, own), :],
-                    target.at[:, columns],
-                    sems.at[len(copies) + len(moves)],
-                )
-            )
-    for copy in copies + moves:
+    for copy in copies:
         copy.start()
-    dil, res, skip, mel_w, table, bias = held
+    dil, res, skip, mel_w, table, bias, samples = held
     where, total = sections(rows)
     chans = rows // 2
     speakers = table.shape[-1]
@@ -167,7 +149,7 @@
     def write(out, at, count, columns, value):
         out[at : at + count, columns] = value.astype(out.dtype)
 
-    for copy in copies:
+    for copy in copies[:-1]:
         copy.wait()
     for layer, out in enumerate((out_one, out_two)):
         for tap in range(2):
@@ -188,9 +170,8 @@
             row = jnp.concatenate([mel_w[layer, half], picked, column, blank], axis=1)
             columns = slice(half * LANES, (half + 1) * LANES)
             write(out, at, count, columns, row.astype(BF16).astype(F32))
+    copies[-1].wait()
     low[...] = samples[...].astype(BF16)
-    for move in moves:
-        move.wait()
 
 
 def assemble_body(group, first, second, last, *refs):
@@ -374,14 +355,14 @@
     return grads + (near_got,), sent, token
 
 
-def far_terms(grads, last_got, unread=()):
+def far_terms(grads, last_got, flops=1024):
     far, *shape = last_got.shape
     kept, *sends, token = call(
         third_sum_body,
         (struct(shape),) + (struct(shape, BF16),) * (far - 1) + (TOKEN,),
         *grads,
         last_got,
-        unread=unread,
+        flops=flops,
     )
     return [kept] + [along_far(value, k + 1) for k, value in enumerate(sends)], token
 
@@ -516,6 +497,7 @@
     lag_grad = dot_right(grad_a, piece(weights, 0)) + dot_right(grad_b, piece(weights, 1))
     now = dot_right(grad_a, piece(weights, 2)) + dot_right(grad_b, piece(weights, 3))
     if last:
+        lag_sum[...] = jnp.zeros_like(lag_sum)
         g1[...] = g2[...] * ROOT_HALF + (earlier[0][...] + now)
         dlag[...] = ((earlier[1][...] + lag_grad) * marks[:own, 1:2]).astype(BF16)
     else:
@@ -523,69 +505,54 @@
         lag_sum[...] = lag_grad
 
 
-def join_body(kept, got, mel, mask, x, cot, skip, side, before, after, tail):
+def part_body(x, cot, skip, lag, kept, given, held):
     core = place()[2]
-    own, width = kept.shape[0], kept.shape[1] // 3
-    for index, ref in enumerate((x, cot, skip)):
+    span, width = kept.shape[0], x.shape[1]
+    beyond = x.shape[0] - span
+    held[...] = lag[...].astype(F32)
+    for index, ref in enumerate((x, cot, skip, held)):
+        columns = slice(index * width, (index + 1) * width)
+        kept[:, columns] = ref[pl.ds(core * beyond, span), :]
+        given[:, columns] = ref[pl.ds((1 - core) * beyond, span), :]
+
+
+def join_body(kept, got, mel, mask, inner, side, near_edge, edge_sent, held, lines):
+    core = place()[2]
+    span, width = kept.shape[0], kept.shape[1] // 4
+    own, beyond = inner.shape[0], mel.shape[1] - span
+    for index in range(4):
         for source, at in ((kept, core), (got, 1 - core)):
-            value = source[:, index * width : (index + 1) * width]
-            ref[:, pl.ds(at * width, width)] = value.astype(ref.dtype)
-    bands = mel.shape[0]
-    samples = pl.ds(core * own, own)
-    stack = jnp.concatenate(
-        [
-            mel[:, samples],
-            mask[:, samples].astype(F32),
-            jnp.zeros((LANES - bands - 1, own), F32),
-        ],
-        axis=0,
-    )
-    side[...] = stack.T
-    full = 2 * width
-    for ref, edge in ((before, own - EDGE), (after, 0)):
-        ref[:, :LANES] = side[edge : edge + EDGE, :]
-        ref[:, LANES : LANES + full] = x[edge : edge + EDGE, :]
-    before[:, LANES + full :] = x[:EDGE, :]
-    tail[...] = x[own - EDGE :, :]
-    after[:, LANES + full : LANES + 2 * full] = cot[:EDGE, :]
-    after[:, LANES + 2 * full :] = skip[:EDGE, :]
+            held[:, pl.ds(index * 2 * width + at * width, width)] = source[
+                :, index * width : (index + 1) * width
+            ]
+    blank = jnp.zeros((LANES - mel.shape[0] - 1, mel.shape[1]), F32)
+    lines[...] = jnp.concatenate([mel[...], mask[...].astype(F32), blank], axis=0).T
+    inner[...] = held[pl.ds(core * EDGE, own), :]
+    side[...] = lines[pl.ds(core * own, own), :]
+    for ref, at in ((near_edge, (1 - core) * own), (edge_sent, core * own)):
+        ref[:, LANES:] = held[pl.ds(at, EDGE), :]
+        ref[:, :LANES] = lines[pl.ds(core * beyond + at, EDGE), :]
 
 
 def widen_body(
-    mel,
-    clips,
-    lengths,
-    x,
-    cot,
-    skip,
-    side,
-    before,
-    after,
-    x_out,
-    cot_out,
-    skip_out,
-    cond,
-    marks,
+    mel, clips, lengths, inner, side, near_edge, edge, x_out, cot_out, skip_out, lag_out, cond, marks
 ):
     far, near, core = place()[:3]
-    own, full = x.shape
+    own, full = inner.shape[0], inner.shape[1] // 4
     wide = own + 2 * EDGE
-
-    def widened(at, inner):
-        return jnp.concatenate(
-            [inner, after[:, at : at + inner.shape[1]], before[:, at : at + inner.shape[1]]], axis=0
-        )
-
-    x_wide = widened(LANES, x[...])
-    x_out[...] = x_wide
-    blank = jnp.zeros((EDGE, full), F32)
-    cot_out[...] = jnp.concatenate(
-        [cot[...], after[:, LANES + full : LANES + 2 * full], blank], axis=0
-    )
-    skip_out[...] = jnp.concatenate([skip[...], after[:, LANES + 2 * full :], blank], axis=0).astype(
-        BF16
-    )
-    side_wide = widened(0, side[...])
+    after = jnp.where(core == 0, near_edge[...], edge[...])
+    before = jnp.where(core == 0, edge[...], near_edge[...])
+    for index, ref in enumerate((x_out, cot_out, skip_out, lag_out)):
+        at = LANES + index * full
+        ref[...] = jnp.concatenate(
+            [
+                inner[:, index * full : (index + 1) * full],
+                after[:, at : at + full],
+                before[:, at : at + full],
+            ],
+            axis=0,
+        ).astype(ref.dtype)
+    side_wide = jnp.concatenate([side[...], after[:, :LANES], before[:, :LANES]], axis=0)
     lane = lax.broadcasted_iota(jnp.int32, (wide, LANES), 1)
     line = lax.broadcasted_iota(jnp.int32, (wide, LANES), 0)
     first = ((far * NEAR + near) * 2 + core) * own
@@ -613,47 +580,33 @@
     )
 
 
-def lag_body(same, other, before, tail, out):
+def divide_body(mixed, total, g1, push, *refs):
     core = place()[2]
-    own, width = same.shape[0] // 2, same.shape[1]
-    for source, at in ((same, core), (other, 1 - core)):
-        out[:own, pl.ds(at * width, width)] = source[pl.ds(core * own, own), :]
-    edges = [before[:, LANES + 2 * width :], tail[...]]
-    out[own:, :] = jnp.concatenate(edges, axis=0).astype(BF16)
-
-
-def divide_body(mixed, total, g1, kept, given):
-    core = place()[2]
-    width = kept.shape[1] // 3
-    for index, ref in enumerate((mixed, total, g1)):
-        kept[:, index * width : (index + 1) * width] = ref[:, pl.ds(core * width, width)]
-        given[:, index * width : (index + 1) * width] = ref[:, pl.ds((1 - core) * width, width)]
+    kept, given, held = refs[-3:]
+    width = kept.shape[1] // 4
+    held[...] = push[...].astype(F32)
+    for index, ref in enumerate((mixed, total, g1, held)):
+        columns = slice(index * width, (index + 1) * width)
+        kept[:, columns] = ref[:, pl.ds(core * width, width)]
+        given[:, columns] = ref[:, pl.ds((1 - core) * width, width)]
 
 
 def finish_body(kept, got, *refs):
     core = place()[2]
     outs, token = refs[:-1], refs[-1]
     token[...] = jnp.zeros_like(token)
-    own, width = kept.shape[0], kept.shape[1] // 3
+    own, width = kept.shape[0], kept.shape[1] // 4
     for index, ref in enumerate(outs):
         for source, at in ((kept, core), (got, 1 - core)):
             ref[pl.ds(at * own, own), :] = source[:, index * width : (index + 1) * width]
 
 
-def push_body(dlag, *refs):
-    core = place()[2]
-    same, other = refs[-2:]
-    width = same.shape[1]
-    same[...] = dlag[:, pl.ds(core * width, width)]
-    other[...] = dlag[:, pl.ds((1 - core) * width, width)]
-
-
-def input_gradient_body(g1, same, other, out):
-    core = place()[2]
-    own = same.shape[0]
-    for source, at in ((same, core), (other, 1 - core)):
-        lines = pl.ds(at * own, own)
-        out[lines, :] = g1[lines, :] + source[...].astype(F32)
+def push_body(push, *refs):
+    refs[-1][...] = push[...].astype(BF16)
+
+
+def input_gradient_body(g1, push, out):
+    out[...] = g1[...] + push[...].astype(F32)
 
 
 def table_gradient(cond_grad, who, mel, clips, speakers):
@@ -781,72 +734,66 @@
     packed_type = BF16 if rows % 32 == 0 else F32
     taken = [views[k] for k in (0, 12, 15, 6, 9, 3)]
     packed_type = BF16 if rows % 32 == 0 else F32
-    pack_one, pack_two, kept, given, x_low = call(
+    taken.append(x_input)
+    pack_one, pack_two, x_low = call(
         functools.partial(start_body, rows, mel, clips),
-        (struct((total, 256), packed_type),) * 2
-        + (struct((own, 3 * width)),) * 2
-        + (struct(x_input.shape, BF16),),
+        (struct((total, 256), packed_type),) * 2 + (struct(x_input.shape, BF16),),
         *taken,
+        scalars=(speaker_ids,),
+        space=pl.ANY,
+        grant=None,
+        scratch=[pltpu.VMEM(v.shape, F32) for v in taken]
+        + [pltpu.SemaphoreType.DMA((len(taken),))],
+    )
+
+    lag = shifted(x_low, "tm", hop)
+    span = own + EDGE
+    kept, given = call(
+        part_body,
+        (struct((span, 4 * width)),) * 2,
         x_input,
         cot_out,
         cot_skip,
-        scalars=(speaker_ids,),
-        space=pl.ANY,
-        grant=None,
-        scratch=[pltpu.VMEM(v.shape, F32) for v in taken + [x_input]]
-        + [pltpu.SemaphoreType.DMA((len(taken) + 7,))],
-    )
-    lag_same = shifted(x_low, "tm", hop)
-    lag_other = swap_cores(lag_same)
-
-    x_own, cot_own, skip_own, side, before, after, tail = call(
+        lag,
+        scratch=[pltpu.VMEM(x_input.shape, F32)],
+    )
+    group_one, stacked = along_all(pack_one.astype(BF16), (lag,))
+    joined_own = struct((own, 4 * full))
+    edge = struct((EDGE, 4 * full + LANES))
+    inner, side, near_edge, edge_sent = call(
         join_body,
-        (
-            struct((own, full)),
-            struct((own, full)),
-            struct((own, full)),
-            struct((own, LANES)),
-            struct((EDGE, LANES + 2 * full)),
-            struct((EDGE, LANES + 3 * full)),
-            struct((EDGE, full)),
-        ),
+        (joined_own, struct((own, LANES)), edge, edge),
         kept,
         swap_cores(given),
         mel_frames,
         sample_mask[None, :],
-    )
-    before = shifted(before, BOTH, 1)
-    x_wide, cot_wide, skip_wide, cond, marks = call(
+        scratch=[pltpu.VMEM((span, 4 * full), F32), pltpu.VMEM((held_rows, LANES), F32)],
+    )
+    x_wide, cot_wide, skip_wide, lag_wide, cond, marks = call(
         functools.partial(widen_body, mel, clips),
         (
             struct((wide, full)),
             struct((wide, full)),
             struct((wide, full), BF16),
+            struct((wide, full), BF16),
             struct((wide, LANES), BF16),
             struct((wide, LANES)),
         ),
-        x_own,
-        cot_own,
-        skip_own,
+        inner,
         side,
-        before,
-        shifted(after, BOTH, -1),
+        near_edge,
+        across_chips(edge_sent),
         scalars=(clip_length_array,),
     )
-    group_one, stacked = along_all(pack_one.astype(BF16), (marks, lag_same))
     pack_two, _ = call(
-        relay_body, (struct(pack_two.shape, BF16), TOKEN), pack_two.astype(BF16), unread=(stacked,)
+        relay_body,
+        (struct(pack_two.shape, BF16), TOKEN),
+        pack_two.astype(BF16),
+        unread=(stacked,),
+        flops=LONG,
     )
     group_two, stacked = along_all(pack_two, ())
-    lag_wide = call(
-        lag_body,
-        struct((wide, full), BF16),
-        lag_same,
-        lag_other,
-        before,
-        shifted(tail, BOTH, 2 * hop + 1),
-    )
-    parts_one, _ = near_exchange(group_one, (stacked, lag_wide))
+    parts_one, _ = near_exchange(group_one, (stacked, marks))
     parts_two, begun = near_exchange(group_two, ())
     w1_own, w1_oth = joined(parts_one, ())
 
@@ -926,28 +873,37 @@
 
     grads2, sent2, token = cores_summed(grad_own, grad_oth)
     now, _, lag_sum, grad_oth = backward(w1_oth, ta_oth, sb_oth, hid_oth, unread=(token,))
-    grads2, sent2, token = near_summed(grads2, sent2, LONG)
-    g1_part, dlag1, _, grad_own = backward(
+    g1_part, dlag1, token, grad_own = backward(
         w1_own, ta_own, sb_own, hid_own, now, lag_sum, unread=()
     )
+    grads2, sent2, token = near_summed(grads2, sent2, LONG, (token,))
     grads1, sent1, _ = cores_summed(grad_own, grad_oth, (token,))
+    last_got = across(sent2, 0)
     kept, given = call(
-        divide_body, (struct((own, 3 * width)),) * 2, mixed, skip_total, g1_part
-    )
-    mixed, skip_total, grad_input, token = call(
-        finish_body, (struct((held_rows, width)),) * 3 + (TOKEN,), kept, swap_cores(given)
-    )
-    last_got = across(sent2, 0)
-    grads1, sent1, _ = near_summed(grads1, sent1, unread=(last_got, token))
-    terms2, _ = far_terms(grads2, last_got)
+        divide_body,
+        (struct((own, 4 * width)),) * 2,
+        mixed,
+        skip_total,
+        g1_part,
+        dlag1,
+        scratch=[pltpu.VMEM((own, full), F32)],
+    )
+    mixed, skip_total, grad_input, push, token = call(
+        finish_body, (struct((held_rows, width)),) * 4 + (TOKEN,), kept, swap_cores(given)
+    )
+    terms2, far_token = far_terms(grads2, last_got, LONG)
+    grads1, sent1, _ = near_summed(grads1, sent1, unread=(token, far_token))
     terms1, token = far_terms(grads1, across(sent1, 0))
-    same, other = call(push_body, (low_half,) * 2, dlag1, unread=(token,))
-    same = shifted(same, "tm", -hop)
-    other = crossed(other, -hop)
-    grad_input = call(input_gradient_body, struct((held_rows, width)), grad_input, same, other)
+    push = call(push_body, struct((held_rows, width), BF16), push, unread=(token,))
+    grad_input = call(
+        input_gradient_body,
+        struct((held_rows, width)),
+        grad_input,
+        shifted(push, "tm", -hop),
+    )
 
     sum2, squares2 = totals(terms2)
-    sum1, squares1 = totals(terms1, (same, other))
+    sum1, squares1 = totals(terms1)
     squares = squares1[:1] + squares2[:1]
     squares = squares + swap_cores(squares)
     sent = jnp.broadcast_to(squares[None], (parts, 1, LANES))

time: 159 us -> 143 us (0.90)
  starting transfers between devices: 61.6 us -> 43.5 us
  blocking collectives: 0 us -> 13.7 us
  waiting for transfers between devices: 69 us -> 59.2 us
    all_to_all x0 -> x1, blocking collectives: none -> 13.7 us  [on_device(): lax.all_to_all(sent, 'tm', split_axis=0, concat_axis=0, tiled=True)]
    all_to_all x1 -> x0, waiting for transfers between devices: 6.36 us -> none  [on_device(): lax.all_to_all(sent, 'tm', split_axis=0, concat_axis=0, tiled=True)]
    ppermute x12, waiting for transfers between devices: 15.8 us -> 20.9 us  [along_far(): lax.ppermute(value, BOTH, route(lambda i, c: (i // NEAR + distance) % far...]
    ppermute x5 -> x2, waiting for transfers between devices: 4.6 us -> 0.01 us  [shifted(): return lax.ppermute(value, axis, pairs)]
    ppermute x8 -> x7, starting transfers between devices: 6.34 us -> 1.81 us  [swap_cores(): return lax.ppermute(value, 'mp', [(0, 1), (1, 0)])]
    all_to_all x1 -> x0, starting transfers between devices: 4.41 us -> none  [on_device(): lax.all_to_all(sent, 'tm', split_axis=0, concat_axis=0, tiled=True)]
    ppermute x5 -> x2, starting transfers between devices: 10.4 us -> 6.15 us  [shifted(): return lax.ppermute(value, axis, pairs)]
    ppermute x10, starting transfers between devices: 15.4 us -> 11.9 us  [across(): return lax.ppermute(value, BOTH, route(lambda i, c: i ^ 1 + (c ^ bit)))]
  transfers between devices with their start and end apart: 37 -> 32, of which waited for: 19 -> 18; matrix products, arithmetic and copies ran while one was open for 0% -> 0% of each run, Pallas kernels for 9% -> 12%
where the time goes in v2:
time: 143 us
  waiting for transfers between devices  59.2 us (41%)
  starting transfers between devices  43.5 us (30%)
  Pallas kernels  24.4 us (17%)
  blocking collectives  13.7 us (10%)
    ppermute x10, waiting for transfers between devices, across(): return lax.ppermute(value, BOTH, route(lambda i, c: i ^ 1 + (c ^ bit)))  30.8 us
    pallas_call x31, Pallas kernels, call(): pl.pallas_call(body, out_shape=out_shape, in_specs=specs, scratch_shapes=...  24.4 us
    ppermute x12, starting transfers between devices, along_far(): lax.ppermute(value, BOTH, route(lambda i, c: (i // NEAR + distance) % far...  22.9 us
    ppermute x12, waiting for transfers between devices, along_far(): lax.ppermute(value, BOTH, route(lambda i, c: (i // NEAR + distance) % far...  20.9 us
    all_to_all x1, blocking collectives, on_device(): lax.all_to_all(sent, 'tm', split_axis=0, concat_axis=0, tiled=True)  13.7 us
    ppermute x10, starting transfers between devices, across(): return lax.ppermute(value, BOTH, route(lambda i, c: i ^ 1 + (c ^ bit)))  11.9 us
    ppermute x7, waiting for transfers between devices, swap_cores(): return lax.ppermute(value, 'mp', [(0, 1), (1, 0)])  7.54 us
    ppermute x2, starting transfers between devices, shifted(): return lax.ppermute(value, axis, pairs)  6.15 us
  transfers between devices with their start and end apart: 32, of which 18 were waited for; matrix products, arithmetic and copies ran while one was open for 0% of the time, Pallas kernels for 12%

profile of v2, /device:TPU:0, one launch (start us, length us, event | category | flops | bytes accessed | tf_op | source)
XLA Modules:
  0.0 143.2 jit_solution(6815059123619176706)
XLA Ops:
  0.7 2.9 %shard_map.504 = (bf16[208,256]{1,0:T(8,128)(2,1)}, bf16[208,256]{1,0:T(8,128)(2,1)}, bf16[512,256]{1,0:T(8,128)(2,1)}) custom-call(s32[8]{0:T(128)} %who.7, f32[512,128]{1,0:T(8,128)} %bitcast.77, f32[2,32,256]{2,1,0:T(8,128)} %bitcast.81, f32[2,32,256]{2,1,0:T(8,128)} %bitcast.83, f32[2,2,16,80]{3,2,1,0:T(8,128)} %bitcast.85, f32[2,2,16,109]{3,2,1,0:T(8,128)} %bitcast.87, ...), custom_call_target="tpu_custom_call" | custom-call | flops 1024 | bytes 1024 | tf_op jit(solution)/shard_map/pallas_call | solution.py:38
  3.6 4.9 %collective-permute-start = (bf16[512,256]{1,0:T(8,128)(2,1)}, bf16[512,256]{1,0:T(8,128)(2,1)S(1)}, u32[]{:S(2)}, u32[]{:S(2)}) collective-permute-start(bf16[512,256]{1,0:T(8,128)(2,1)} %get-tuple-element.145), channel_id=1, source_target_pairs={{0,2},{2,4},{4,6},{6,8},{8,10},{10,12},{12,14},{14,16},{16,18},{18... | collective-permute-start | bytes 786440 | tf_op jit(solution)/shard_map/ppermute | solution.py:92
  8.5 3.6 %collective-permute-start.5 = (bf16[208,256]{1,0:T(8,128)(2,1)}, bf16[208,256]{1,0:T(8,128)(2,1)S(1)}, u32[]{:S(2)}, u32[]{:S(2)}) collective-permute-start(bf16[208,256]{1,0:T(8,128)(2,1)} %get-tuple-element.156.refs_0_), channel_id=1, source_target_pairs={{0,24},{1,25},{2,26},{3,27},{4,28},{5,29},{6,30},{7,31},{8,0},{9,1... | collective-permute-start | bytes 319496 | tf_op jit(solution)/shard_map/ppermute | solution.py:80
  13.1 2.7 %collective-permute-done.5.refs_3_ = bf16[208,256]{1,0:T(8,128)(2,1)S(1)} collective-permute-done((bf16[208,256]{1,0:T(8,128)(2,1)}, bf16[208,256]{1,0:T(8,128)(2,1)S(1)}, u32[]{:S(2)}, u32[]{:S(2)}) %collective-permute-start.5) | collective-permute-done | bytes 106528 | tf_op jit(solution)/shard_map/ppermute | solution.py:80
  15.8 5.4 %collective-permute-done.4.refs_2_ = bf16[208,256]{1,0:T(8,128)(2,1)S(1)} collective-permute-done((bf16[208,256]{1,0:T(8,128)(2,1)}, bf16[208,256]{1,0:T(8,128)(2,1)S(1)}, u32[]{:S(2)}, u32[]{:S(2)}) %collective-permute-start.4) | collective-permute-done | bytes 106528 | tf_op jit(solution)/shard_map/ppermute | solution.py:80
  26.2 5.3 %collective-permute-start.10 = (bf16[208,256]{1,0:T(8,128)(2,1)S(1)}, bf16[208,256]{1,0:T(8,128)(2,1)S(1)}, u32[]{:S(2)}, u32[]{:S(2)}) collective-permute-start(bf16[208,256]{1,0:T(8,128)(2,1)S(1)} %get-tuple-element.160.refs_0_), channel_id=1, source_target_pairs={{0,24},{1,25},{2,26},{3,27},{4,28},{5,29},{6,30},{7,31},{8,0},{9,1... | collective-permute-start | bytes 319496 | tf_op jit(solution)/shard_map/ppermute | solution.py:80
  31.8 2.0 %collective-permute-start.8 = (bf16[208,256]{1,0:T(8,128)(2,1)S(1)}, bf16[208,256]{1,0:T(8,128)(2,1)S(1)}, u32[]{:S(2)}, u32[]{:S(2)}) collective-permute-start(bf16[208,256]{1,0:T(8,128)(2,1)S(1)} %get-tuple-element.160.refs_0_), channel_id=1, source_target_pairs={{0,8},{1,9},{2,10},{3,11},{4,12},{5,13},{6,14},{7,15},{8,16},{9,17... | collective-permute-start | bytes 319496 | tf_op jit(solution)/shard_map/ppermute | solution.py:80
  35.5 6.8 %collective-permute-done.9.refs_2_ = bf16[208,256]{1,0:T(8,128)(2,1)S(1)} collective-permute-done((bf16[208,256]{1,0:T(8,128)(2,1)S(1)}, bf16[208,256]{1,0:T(8,128)(2,1)S(1)}, u32[]{:S(2)}, u32[]{:S(2)}) %collective-permute-start.9) | collective-permute-done | bytes 106528 | tf_op jit(solution)/shard_map/ppermute | solution.py:80
  46.1 7.5 %collective-permute-done.14.refs_0_.second = bf16[4,208,256]{2,1,0:T(8,128)(2,1)S(1)} collective-permute-done((bf16[4,208,256]{2,1,0:T(8,128)(2,1)S(1)}, bf16[4,208,256]{2,1,0:T(8,128)(2,1)S(1)}, u32[]{:S(2)}, u32[]{:S(2)}) %collective-permute-start.14) | collective-permute-done | bytes 426016 | tf_op jit(solution)/shard_map/ppermute | solution.py:75
  55.3 2.0 %collective-permute-start.15 = (bf16[4,208,256]{2,1,0:T(8,128)(2,1)S(1)}, bf16[4,208,256]{2,1,0:T(8,128)(2,1)S(1)}, u32[]{:S(2)}, u32[]{:S(2)}) collective-permute-start(bf16[4,208,256]{2,1,0:T(8,128)(2,1)S(1)} %get-tuple-element.171), channel_id=1, source_target_pairs={{0,4},{1,3},{2,6},{3,1},{4,0},{5,7},{6,2},{7,5},{8,12},{9,11},{10,... | collective-permute-start | bytes 1277960 | tf_op jit(solution)/shard_map/ppermute | solution.py:75
  59.8 2.3 %collective-permute-done.12.weights = bf16[16,208,256]{2,1,0:T(8,128)(2,1)S(1)} collective-permute-done((bf16[16,208,256]{2,1,0:T(8,128)(2,1)S(1)}, bf16[16,208,256]{2,1,0:T(8,128)(2,1)S(1)}, u32[]{:S(2)}, u32[]{:S(2)}) %collective-permute-start.12) | collective-permute-done | bytes 1703968 | tf_op jit(solution)/shard_map/ppermute | solution.py:86
  63.7 3.6 %collective-permute-done.16.weights = bf16[16,208,256]{2,1,0:T(8,128)(2,1)S(1)} collective-permute-done((bf16[16,208,256]{2,1,0:T(8,128)(2,1)S(1)}, bf16[16,208,256]{2,1,0:T(8,128)(2,1)S(1)}, u32[]{:S(2)}, u32[]{:S(2)}) %collective-permute-start.16) | collective-permute-done | bytes 1703968 | tf_op jit(solution)/shard_map/ppermute | solution.py:86
  67.3 2.1 %shard_map.517 = (f32[256,512]{1,0:T(8,128)S(1)}, f32[256,512]{1,0:T(8,128)S(1)}, f32[256,512]{1,0:T(8,128)S(1)}, f32[272,512]{1,0:T(8,128)S(1)}, bf16[16,208,256]{2,1,0:T(8,128)(2,1)S(1)}) custom-call(f32[272,512]{1,0:T(8,128)S(1)} %get-tuple-element.167.u2, f32[256,512]{1,0:T(8,128)S(1)} %get-tuple-element.168.s1, ...), custom_call_target="tpu_custom_call" | custom-call | flops 1024 | bytes 1024 | tf_op jit(solution)/shard_map/pallas_call | solution.py:38
  70.1 2.0 %shard_map.519 = (f32[256,512]{1,0:T(8,128)S(1)}, f32[256,512]{1,0:T(8,128)S(1)}, f32[256,512]{1,0:T(8,128)S(1)}, f32[8,128]{1,0:T(8,128)}, bf16[16,208,256]{2,1,0:T(8,128)(2,1)S(1)}) custom-call(f32[272,512]{1,0:T(8,128)S(1)} %get-tuple-element.167.u2, f32[256,512]{1,0:T(8,128)S(1)} %get-tuple-element.168.s1, bf16[272,128]{1,0:T(8,128)(2,1)S(1)} %get-tuple-element.154.cond, ...), custom_call_target="tpu_custom_call" | custom-call | flops 1024 | bytes 1024 | tf_op jit(solution)/shard_map/pallas_call | solution.py:38
  73.1 2.0 %collective-permute-start.20 = (bf16[8,208,256]{2,1,0:T(8,128)(2,1)S(1)}, bf16[8,208,256]{2,1,0:T(8,128)(2,1)S(1)}, u32[]{:S(2)}, u32[]{:S(2)}) collective-permute-start(bf16[8,208,256]{2,1,0:T(8,128)(2,1)S(1)} %get-tuple-element.204), channel_id=1, source_target_pairs={{0,4},{1,3},{2,6},{3,1},{4,0},{5,7},{6,2},{7,5},{8,12},{9,11},{10,... | collective-permute-start | bytes 2555912 | tf_op jit(solution)/shard_map/ppermute | solution.py:75
  79.3 6.5 %collective-permute-done.20.near_got = bf16[8,208,256]{2,1,0:T(8,128)(2,1)S(1)} collective-permute-done((bf16[8,208,256]{2,1,0:T(8,128)(2,1)S(1)}, bf16[8,208,256]{2,1,0:T(8,128)(2,1)S(1)}, u32[]{:S(2)}, u32[]{:S(2)}) %collective-permute-start.20) | collective-permute-done | bytes 852000 | tf_op jit(solution)/shard_map/ppermute | solution.py:75
  89.9 7.0 %collective-permute-done.22.last_got = bf16[4,208,256]{2,1,0:T(8,128)(2,1)S(1)} collective-permute-done((bf16[4,208,256]{2,1,0:T(8,128)(2,1)S(1)}, bf16[4,208,256]{2,1,0:T(8,128)(2,1)S(1)}, u32[]{:S(2)}, u32[]{:S(2)}) %collective-permute-start.22) | collective-permute-done | bytes 426016 | tf_op jit(solution)/shard_map/ppermute | solution.py:75
  97.1 4.7 %collective-permute-done.21.near_got = bf16[8,208,256]{2,1,0:T(8,128)(2,1)S(1)} collective-permute-done((bf16[8,208,256]{2,1,0:T(8,128)(2,1)S(1)}, bf16[8,208,256]{2,1,0:T(8,128)(2,1)S(1)}, u32[]{:S(2)}, u32[]{:S(2)}) %collective-permute-start.21) | collective-permute-done | bytes 852000 | tf_op jit(solution)/shard_map/ppermute | solution.py:75
  105.7 2.9 %collective-permute-start.30 = (bf16[208,256]{1,0:T(8,128)(2,1)S(1)}, bf16[208,256]{1,0:T(8,128)(2,1)S(1)}, u32[]{:S(2)}, u32[]{:S(2)}) collective-permute-start(bf16[208,256]{1,0:T(8,128)(2,1)S(1)} %get-tuple-element.221), channel_id=1, source_target_pairs={{0,24},{1,25},{2,26},{3,27},{4,28},{5,29},{6,30},{7,31},{8,0},{9,1... | collective-permute-start | bytes 319496 | tf_op jit(solution)/shard_map/ppermute | solution.py:80
  108.6 2.0 %collective-permute-done.23.last_got = bf16[4,208,256]{2,1,0:T(8,128)(2,1)S(1)} collective-permute-done((bf16[4,208,256]{2,1,0:T(8,128)(2,1)S(1)}, bf16[4,208,256]{2,1,0:T(8,128)(2,1)S(1)}, u32[]{:S(2)}, u32[]{:S(2)}) %collective-permute-start.23) | collective-permute-done | bytes 426016 | tf_op jit(solution)/shard_map/ppermute | solution.py:75
  113.5 2.9 %collective-permute-start.27 = (bf16[208,256]{1,0:T(8,128)(2,1)S(1)}, bf16[208,256]{1,0:T(8,128)(2,1)S(1)}, u32[]{:S(2)}, u32[]{:S(2)}) collective-permute-start(bf16[208,256]{1,0:T(8,128)(2,1)S(1)} %get-tuple-element.216), channel_id=1, source_target_pairs={{0,24},{1,25},{2,26},{3,27},{4,28},{5,29},{6,30},{7,31},{8,0},{9,1... | collective-permute-start | bytes 319496 | tf_op jit(solution)/shard_map/ppermute | solution.py:80
  118.9 4.9 %collective-permute-done.26.refs_2_ = bf16[208,256]{1,0:T(8,128)(2,1)S(1)} collective-permute-done((bf16[208,256]{1,0:T(8,128)(2,1)S(1)}, bf16[208,256]{1,0:T(8,128)(2,1)S(1)}, u32[]{:S(2)}, u32[]{:S(2)}) %collective-permute-start.26) | collective-permute-done | bytes 106528 | tf_op jit(solution)/shard_map/ppermute | solution.py:80
  126.2 13.7 %all_to_all.5 = f32[16,1,128]{2,1,0:T(1,128)S(1)} all-to-all(f32[16,1,128]{2,1,0:T(1,128)S(1)} %broadcast_in_dim.13), channel_id=1, replica_groups=mesh['tm'=16,'mp'=2] {'tm'}, dimensions={0} | all-to-all | bytes 16384 | tf_op jit(solution)/shard_map/all_to_all | solution.py:910
  140.1 2.3 %shard_map.534 = (f32[1,1]{1,0:T(1,128)}, f32[512,128]{1,0:T(8,128)}, f32[512,128]{1,0:T(8,128)}, f32[512,128]{1,0:T(8,128)}, f32[512,128]{1,0:T(8,128)}, /*inde...) custom-call(s32[8]{0:T(128)S(1)} %copy-done.20, ...), custom_call_target="tpu_custom_call" | custom-call | flops 1024 | bytes 1024 | tf_op jit(solution)/shard_map/pallas_call | solution.py:38
  (129 shorter events, 39.8 us)
Async XLA Ops:
  3.6 17.7 %collective-permute-start = (bf16[512,256]{1,0:T(8,128)(2,1)}, bf16[512,256]{1,0:T(8,128)(2,1)S(1)}, u32[]{:S(2)}, u32[]{:S(2)}) collective-permute-start(bf16[512,256]{1,0:T(8,128)(2,1)} %get-tuple-element.145), channel_id=1, source_target_pairs={{0,2},{2,4},{4,6},{6,8},{8,10},{10,12},{12,14},{14,16},{16,18},{18... | collective-permute-start | bytes 786440 | tf_op jit(solution)/shard_map/ppermute | solution.py:92
  12.1 9.2 %collective-permute-start.4 = (bf16[208,256]{1,0:T(8,128)(2,1)}, bf16[208,256]{1,0:T(8,128)(2,1)S(1)}, u32[]{:S(2)}, u32[]{:S(2)}) collective-permute-start(bf16[208,256]{1,0:T(8,128)(2,1)} %get-tuple-element.156.refs_0_), channel_id=1, source_target_pairs={{0,16},{1,17},{2,18},{3,19},{4,20},{5,21},{6,22},{7,23},{8,24},{9,... | collective-permute-start | bytes 319496 | tf_op jit(solution)/shard_map/ppermute | solution.py:80
  12.1 9.2 %collective-permute-start.3 = (bf16[208,256]{1,0:T(8,128)(2,1)}, bf16[208,256]{1,0:T(8,128)(2,1)S(1)}, u32[]{:S(2)}, u32[]{:S(2)}) collective-permute-start(bf16[208,256]{1,0:T(8,128)(2,1)} %get-tuple-element.156.refs_0_), channel_id=1, source_target_pairs={{0,8},{1,9},{2,10},{3,11},{4,12},{5,13},{6,14},{7,15},{8,16},{9,17... | collective-permute-start | bytes 319496 | tf_op jit(solution)/shard_map/ppermute | solution.py:80
  22.2 21.3 %collective-permute-start.7 = (bf16[4,208,256]{2,1,0:T(8,128)(2,1)S(1)}, bf16[4,208,256]{2,1,0:T(8,128)(2,1)S(1)}, u32[]{:S(2)}, u32[]{:S(2)}) collective-permute-start(bf16[4,208,256]{2,1,0:T(8,128)(2,1)S(1)} %get-tuple-element.157.group), channel_id=1, source_target_pairs={{0,4},{1,3},{2,6},{3,1},{4,0},{5,7},{6,2},{7,5},{8,12},{9,11},{10,... | collective-permute-start | bytes 1277960 | tf_op jit(solution)/shard_map/ppermute | solution.py:75
  23.8 19.8 %collective-permute-start.6 = (bf16[4,208,256]{2,1,0:T(8,128)(2,1)S(1)}, bf16[4,208,256]{2,1,0:T(8,128)(2,1)S(1)}, u32[]{:S(2)}, u32[]{:S(2)}) collective-permute-start(bf16[4,208,256]{2,1,0:T(8,128)(2,1)S(1)} %get-tuple-element.157.group), channel_id=1, source_target_pairs={{0,2},{1,5},{2,0},{3,7},{4,6},{5,1},{6,4},{7,3},{8,10},{9,13},{10,... | collective-permute-start | bytes 1277960 | tf_op jit(solution)/shard_map/ppermute | solution.py:75
  26.2 8.7 %collective-permute-start.10 = (bf16[208,256]{1,0:T(8,128)(2,1)S(1)}, bf16[208,256]{1,0:T(8,128)(2,1)S(1)}, u32[]{:S(2)}, u32[]{:S(2)}) collective-permute-start(bf16[208,256]{1,0:T(8,128)(2,1)S(1)} %get-tuple-element.160.refs_0_), channel_id=1, source_target_pairs={{0,24},{1,25},{2,26},{3,27},{4,28},{5,29},{6,30},{7,31},{8,0},{9,1... | collective-permute-start | bytes 319496 | tf_op jit(solution)/shard_map/ppermute | solution.py:80
  31.5 10.8 %collective-permute-start.9 = (bf16[208,256]{1,0:T(8,128)(2,1)S(1)}, bf16[208,256]{1,0:T(8,128)(2,1)S(1)}, u32[]{:S(2)}, u32[]{:S(2)}) collective-permute-start(bf16[208,256]{1,0:T(8,128)(2,1)S(1)} %get-tuple-element.160.refs_0_), channel_id=1, source_target_pairs={{0,16},{1,17},{2,18},{3,19},{4,20},{5,21},{6,22},{7,23},{8,24},{9,... | collective-permute-start | bytes 319496 | tf_op jit(solution)/shard_map/ppermute | solution.py:80
  31.8 10.5 %collective-permute-start.8 = (bf16[208,256]{1,0:T(8,128)(2,1)S(1)}, bf16[208,256]{1,0:T(8,128)(2,1)S(1)}, u32[]{:S(2)}, u32[]{:S(2)}) collective-permute-start(bf16[208,256]{1,0:T(8,128)(2,1)S(1)} %get-tuple-element.160.refs_0_), channel_id=1, source_target_pairs={{0,8},{1,9},{2,10},{3,11},{4,12},{5,13},{6,14},{7,15},{8,16},{9,17... | collective-permute-start | bytes 319496 | tf_op jit(solution)/shard_map/ppermute | solution.py:80
  42.3 11.3 %collective-permute-start.14 = (bf16[4,208,256]{2,1,0:T(8,128)(2,1)S(1)}, bf16[4,208,256]{2,1,0:T(8,128)(2,1)S(1)}, u32[]{:S(2)}, u32[]{:S(2)}) collective-permute-start(bf16[4,208,256]{2,1,0:T(8,128)(2,1)S(1)} %get-tuple-element.163.group), channel_id=1, source_target_pairs={{0,4},{1,3},{2,6},{3,1},{4,0},{5,7},{6,2},{7,5},{8,12},{9,11},{10,... | collective-permute-start | bytes 1277960 | tf_op jit(solution)/shard_map/ppermute | solution.py:75
  42.4 12.8 %collective-permute-start.13 = (bf16[4,208,256]{2,1,0:T(8,128)(2,1)S(1)}, bf16[4,208,256]{2,1,0:T(8,128)(2,1)S(1)}, u32[]{:S(2)}, u32[]{:S(2)}) collective-permute-start(bf16[4,208,256]{2,1,0:T(8,128)(2,1)S(1)} %get-tuple-element.163.group), channel_id=1, source_target_pairs={{0,2},{1,5},{2,0},{3,7},{4,6},{5,1},{6,4},{7,3},{8,10},{9,13},{10,... | collective-permute-start | bytes 1277960 | tf_op jit(solution)/shard_map/ppermute | solution.py:75
  44.2 14.0 %collective-permute-start.11 = (bf16[4,208,256]{2,1,0:T(8,128)(2,1)S(1)}, bf16[4,208,256]{2,1,0:T(8,128)(2,1)S(1)}, u32[]{:S(2)}, u32[]{:S(2)}) collective-permute-start(bf16[4,208,256]{2,1,0:T(8,128)(2,1)S(1)} %get-tuple-element.162), channel_id=1, source_target_pairs={{0,4},{1,3},{2,6},{3,1},{4,0},{5,7},{6,2},{7,5},{8,12},{9,11},{10,... | collective-permute-start | bytes 1277960 | tf_op jit(solution)/shard_map/ppermute | solution.py:75
  55.3 8.2 %collective-permute-start.15 = (bf16[4,208,256]{2,1,0:T(8,128)(2,1)S(1)}, bf16[4,208,256]{2,1,0:T(8,128)(2,1)S(1)}, u32[]{:S(2)}, u32[]{:S(2)}) collective-permute-start(bf16[4,208,256]{2,1,0:T(8,128)(2,1)S(1)} %get-tuple-element.171), channel_id=1, source_target_pairs={{0,4},{1,3},{2,6},{3,1},{4,0},{5,7},{6,2},{7,5},{8,12},{9,11},{10,... | collective-permute-start | bytes 1277960 | tf_op jit(solution)/shard_map/ppermute | solution.py:75
  73.1 12.8 %collective-permute-start.20 = (bf16[8,208,256]{2,1,0:T(8,128)(2,1)S(1)}, bf16[8,208,256]{2,1,0:T(8,128)(2,1)S(1)}, u32[]{:S(2)}, u32[]{:S(2)}) collective-permute-start(bf16[8,208,256]{2,1,0:T(8,128)(2,1)S(1)} %get-tuple-element.204), channel_id=1, source_target_pairs={{0,4},{1,3},{2,6},{3,1},{4,0},{5,7},{6,2},{7,5},{8,12},{9,11},{10,... | collective-permute-start | bytes 2555912 | tf_op jit(solution)/shard_map/ppermute | solution.py:75
  78.8 8.2 %collective-permute-start.18 = (f32[256,1024]{1,0:T(8,128)S(1)}, f32[256,1024]{1,0:T(8,128)S(1)}, u32[]{:S(2)}, u32[]{:S(2)}) collective-permute-start(f32[256,1024]{1,0:T(8,128)S(1)} %get-tuple-element.197), channel_id=1, source_target_pairs={{0,1},{1,0},{2,3},{3,2},{4,5},{5,4},{6,7},{7,6},{8,9},{9,8},{10,11... | collective-permute-start | bytes 3145736 | tf_op jit(solution)/shard_map/ppermute | solution.py:86
  78.9 9.2 %collective-permute-start.19 = (bf16[16,208,256]{2,1,0:T(8,128)(2,1)S(1)}, bf16[16,208,256]{2,1,0:T(8,128)(2,1)S(1)}, u32[]{:S(2)}, u32[]{:S(2)}) collective-permute-start(bf16[16,208,256]{2,1,0:T(8,128)(2,1)S(1)} %get-tuple-element.203), channel_id=1, source_target_pairs={{0,1},{1,0},{2,3},{3,2},{4,5},{5,4},{6,7},{7,6},{8,9},{9,8},{10,11... | collective-permute-start | bytes 5111816 | tf_op jit(solution)/shard_map/ppermute | solution.py:86
  86.0 10.9 %collective-permute-start.22 = (bf16[4,208,256]{2,1,0:T(8,128)(2,1)S(1)}, bf16[4,208,256]{2,1,0:T(8,128)(2,1)S(1)}, u32[]{:S(2)}, u32[]{:S(2)}) collective-permute-start(bf16[4,208,256]{2,1,0:T(8,128)(2,1)S(1)} %get-tuple-element.209), channel_id=1, source_target_pairs={{0,2},{1,5},{2,0},{3,7},{4,6},{5,1},{6,4},{7,3},{8,10},{9,13},{10,... | collective-permute-start | bytes 1277960 | tf_op jit(solution)/shard_map/ppermute | solution.py:75
  88.8 13.1 %collective-permute-start.21 = (bf16[8,208,256]{2,1,0:T(8,128)(2,1)S(1)}, bf16[8,208,256]{2,1,0:T(8,128)(2,1)S(1)}, u32[]{:S(2)}, u32[]{:S(2)}) collective-permute-start(bf16[8,208,256]{2,1,0:T(8,128)(2,1)S(1)} %get-tuple-element.207), channel_id=1, source_target_pairs={{0,4},{1,3},{2,6},{3,1},{4,0},{5,7},{6,2},{7,5},{8,12},{9,11},{10,... | collective-permute-start | bytes 2555912 | tf_op jit(solution)/shard_map/ppermute | solution.py:75
  102.5 8.1 %collective-permute-start.23 = (bf16[4,208,256]{2,1,0:T(8,128)(2,1)S(1)}, bf16[4,208,256]{2,1,0:T(8,128)(2,1)S(1)}, u32[]{:S(2)}, u32[]{:S(2)}) collective-permute-start(bf16[4,208,256]{2,1,0:T(8,128)(2,1)S(1)} %get-tuple-element.211), channel_id=1, source_target_pairs={{0,2},{1,5},{2,0},{3,7},{4,6},{5,1},{6,4},{7,3},{8,10},{9,13},{10,... | collective-permute-start | bytes 1277960 | tf_op jit(solution)/shard_map/ppermute | solution.py:75
  103.3 10.3 %collective-permute-start.28 = (bf16[208,256]{1,0:T(8,128)(2,1)S(1)}, bf16[208,256]{1,0:T(8,128)(2,1)S(1)}, u32[]{:S(2)}, u32[]{:S(2)}) collective-permute-start(bf16[208,256]{1,0:T(8,128)(2,1)S(1)} %get-tuple-element.219), channel_id=1, source_target_pairs={{0,8},{1,9},{2,10},{3,11},{4,12},{5,13},{6,14},{7,15},{8,16},{9,17... | collective-permute-start | bytes 319496 | tf_op jit(solution)/shard_map/ppermute | solution.py:80
  103.8 12.6 %collective-permute-start.29 = (bf16[208,256]{1,0:T(8,128)(2,1)S(1)}, bf16[208,256]{1,0:T(8,128)(2,1)S(1)}, u32[]{:S(2)}, u32[]{:S(2)}) collective-permute-start(bf16[208,256]{1,0:T(8,128)(2,1)S(1)} %get-tuple-element.220), channel_id=1, source_target_pairs={{0,16},{1,17},{2,18},{3,19},{4,20},{5,21},{6,22},{7,23},{8,24},{9,... | collective-permute-start | bytes 319496 | tf_op jit(solution)/shard_map/ppermute | solution.py:80
  105.7 10.7 %collective-permute-start.30 = (bf16[208,256]{1,0:T(8,128)(2,1)S(1)}, bf16[208,256]{1,0:T(8,128)(2,1)S(1)}, u32[]{:S(2)}, u32[]{:S(2)}) collective-permute-start(bf16[208,256]{1,0:T(8,128)(2,1)S(1)} %get-tuple-element.221), channel_id=1, source_target_pairs={{0,24},{1,25},{2,26},{3,27},{4,28},{5,29},{6,30},{7,31},{8,0},{9,1... | collective-permute-start | bytes 319496 | tf_op jit(solution)/shard_map/ppermute | solution.py:80
  111.5 12.2 %collective-permute-start.26 = (bf16[208,256]{1,0:T(8,128)(2,1)S(1)}, bf16[208,256]{1,0:T(8,128)(2,1)S(1)}, u32[]{:S(2)}, u32[]{:S(2)}) collective-permute-start(bf16[208,256]{1,0:T(8,128)(2,1)S(1)} %get-tuple-element.215), channel_id=1, source_target_pairs={{0,16},{1,17},{2,18},{3,19},{4,20},{5,21},{6,22},{7,23},{8,24},{9,... | collective-permute-start | bytes 319496 | tf_op jit(solution)/shard_map/ppermute | solution.py:80
  113.5 10.3 %collective-permute-start.27 = (bf16[208,256]{1,0:T(8,128)(2,1)S(1)}, bf16[208,256]{1,0:T(8,128)(2,1)S(1)}, u32[]{:S(2)}, u32[]{:S(2)}) collective-permute-start(bf16[208,256]{1,0:T(8,128)(2,1)S(1)} %get-tuple-element.216), channel_id=1, source_target_pairs={{0,24},{1,25},{2,26},{3,27},{4,28},{5,29},{6,30},{7,31},{8,0},{9,1... | collective-permute-start | bytes 319496 | tf_op jit(solution)/shard_map/ppermute | solution.py:80
  117.2 25.1 %collective-permute-start.24 = (bf16[512,256]{1,0:T(8,128)(2,1)S(1)}, bf16[512,256]{1,0:T(8,128)(2,1)S(1)}, u32[]{:S(2)}, u32[]{:S(2)}) collective-permute-start(bf16[512,256]{1,0:T(8,128)(2,1)S(1)} %shard_map.530), channel_id=1, source_target_pairs={{2,0},{4,2},{6,4},{8,6},{10,8},{12,10},{14,12},{16,14},{18,16},{20... | collective-permute-start | bytes 786440 | tf_op jit(solution)/shard_map/ppermute | solution.py:92
  (35 other events, 686.5 us)

commit v3 on v2

--- a/solution.py
+++ b/solution.py
@@ -212,11 +212,15 @@
     )
 
 
-def near_exchange(group, before_last):
+def near_exchange(group, before_last, flops=1024):
     first = across(group, 0)
     second = across(group, 1)
     passed, token = call(
-        relay_body, (struct(first.shape, BF16), TOKEN), first, unread=(second,) + before_last
+        relay_body,
+        (struct(first.shape, BF16), TOKEN),
+        first,
+        unread=(second,) + before_last,
+        flops=flops,
     )
     return (group, first, second, across(passed, 1)), token
 
@@ -505,8 +509,9 @@
         lag_sum[...] = lag_grad
 
 
-def part_body(x, cot, skip, lag, kept, given, held):
+def part_body(x, cot, skip, lag, *refs):
     core = place()[2]
+    kept, given, held = refs[-3:]
     span, width = kept.shape[0], x.shape[1]
     beyond = x.shape[0] - span
     held[...] = lag[...].astype(F32)
@@ -516,8 +521,9 @@
         given[:, columns] = ref[pl.ds((1 - core) * beyond, span), :]
 
 
-def join_body(kept, got, mel, mask, inner, side, near_edge, edge_sent, held, lines):
+def join_body(kept, got, mel, mask, *refs):
     core = place()[2]
+    inner, side, near_edge, edge_sent, held, lines = refs[-6:]
     span, width = kept.shape[0], kept.shape[1] // 4
     own, beyond = inner.shape[0], mel.shape[1] - span
     for index in range(4):
@@ -748,6 +754,8 @@
 
     lag = shifted(x_low, "tm", hop)
     span = own + EDGE
+    group_one, stacked = along_all(pack_one.astype(BF16), (lag,))
+    group_two, stacked = along_all(pack_two.astype(BF16), (stacked,))
     kept, given = call(
         part_body,
         (struct((span, 4 * width)),) * 2,
@@ -755,9 +763,10 @@
         cot_out,
         cot_skip,
         lag,
+        unread=(stacked,),
         scratch=[pltpu.VMEM(x_input.shape, F32)],
     )
-    group_one, stacked = along_all(pack_one.astype(BF16), (lag,))
+    parts_one, relayed = near_exchange(group_one, (stacked,), LONG)
     joined_own = struct((own, 4 * full))
     edge = struct((EDGE, 4 * full + LANES))
     inner, side, near_edge, edge_sent = call(
@@ -767,6 +776,7 @@
         swap_cores(given),
         mel_frames,
         sample_mask[None, :],
+        unread=(relayed,),
         scratch=[pltpu.VMEM((span, 4 * full), F32), pltpu.VMEM((held_rows, LANES), F32)],
     )
     x_wide, cot_wide, skip_wide, lag_wide, cond, marks = call(
@@ -785,17 +795,8 @@
         across_chips(edge_sent),
         scalars=(clip_length_array,),
     )
-    pack_two, _ = call(
-        relay_body,
-        (struct(pack_two.shape, BF16), TOKEN),
-        pack_two.astype(BF16),
-        unread=(stacked,),
-        flops=LONG,
-    )
-    group_two, stacked = along_all(pack_two, ())
-    parts_one, _ = near_exchange(group_one, (stacked, marks))
-    parts_two, begun = near_exchange(group_two, ())
-    w1_own, w1_oth = joined(parts_one, ())
+    parts_two, begun = near_exchange(group_two, (marks,))
+    w1_own, w1_oth = joined(parts_one, (begun,))
 
     half = struct((own, width))
     wave = struct((own, full))
@@ -891,8 +892,8 @@
     mixed, skip_total, grad_input, push, token = call(
         finish_body, (struct((held_rows, width)),) * 4 + (TOKEN,), kept, swap_cores(given)
     )
-    terms2, far_token = far_terms(grads2, last_got, LONG)
-    grads1, sent1, _ = near_summed(grads1, sent1, unread=(token, far_token))
+    terms2, _ = far_terms(grads2, last_got, LONG)
+    grads1, sent1, _ = near_summed(grads1, sent1, unread=(token, terms2[1], terms2[-1]))
     terms1, token = far_terms(grads1, across(sent1, 0))
     push = call(push_body, struct((held_rows, width), BF16), push, unread=(token,))
     grad_input = call(

time: 143 us -> 143 us (level)
    ppermute x10, starting transfers between devices: 11.9 us -> 15.9 us  [across(): return lax.ppermute(value, BOTH, route(lambda i, c: i ^ 1 + (c ^ bit)))]
    ppermute x12, starting transfers between devices: 22.9 us -> 20.8 us  [along_far(): lax.ppermute(value, BOTH, route(lambda i, c: (i // NEAR + distance) % far...]
    ppermute x10, waiting for transfers between devices: 30.8 us -> 29.1 us  [across(): return lax.ppermute(value, BOTH, route(lambda i, c: i ^ 1 + (c ^ bit)))]
    pallas_call x31 -> x30, Pallas kernels: 24.4 us -> 23.6 us  [call(): pl.pallas_call(body, out_shape=out_shape, in_specs=specs, scratch_shapes=...]
  transfers between devices with their start and end apart: 32 -> 32, of which waited for: 18 -> 19; matrix products, arithmetic and copies ran while one was open for 0% -> 0% of each run, Pallas kernels for 12% -> 12%
where the time goes in v3:
time: 143 us
  waiting for transfers between devices  58.5 us (41%)
  starting transfers between devices  44.2 us (31%)
  Pallas kernels  23.6 us (17%)
  blocking collectives  13 us (9%)
  local copies, waits for them, and re-layouts  1.95 us (1%)
    ppermute x10, waiting for transfers between devices, across(): return lax.ppermute(value, BOTH, route(lambda i, c: i ^ 1 + (c ^ bit)))  29.1 us
    pallas_call x30, Pallas kernels, call(): pl.pallas_call(body, out_shape=out_shape, in_specs=specs, scratch_shapes=...  23.6 us
    ppermute x12, starting transfers between devices, along_far(): lax.ppermute(value, BOTH, route(lambda i, c: (i // NEAR + distance) % far...  20.8 us
    ppermute x12, waiting for transfers between devices, along_far(): lax.ppermute(value, BOTH, route(lambda i, c: (i // NEAR + distance) % far...  20.7 us
    ppermute x10, starting transfers between devices, across(): return lax.ppermute(value, BOTH, route(lambda i, c: i ^ 1 + (c ^ bit)))  15.9 us
    all_to_all x1, blocking collectives, on_device(): lax.all_to_all(sent, 'tm', split_axis=0, concat_axis=0, tiled=True)  13 us
    ppermute x7, waiting for transfers between devices, swap_cores(): return lax.ppermute(value, 'mp', [(0, 1), (1, 0)])  8.71 us
    ppermute x2, starting transfers between devices, shifted(): return lax.ppermute(value, axis, pairs)  6.15 us
  transfers between devices with their start and end apart: 32, of which 19 were waited for; matrix products, arithmetic and copies ran while one was open for 0% of the time, Pallas kernels for 12%

profile of v3, /device:TPU:0, one launch (start us, length us, event | category | flops | bytes accessed | tf_op | source)
XLA Modules:
  0.0 142.6 jit_solution(5527430273981446872)
XLA Ops:
  0.7 2.9 %shard_map.504 = (bf16[208,256]{1,0:T(8,128)(2,1)}, bf16[208,256]{1,0:T(8,128)(2,1)}, bf16[512,256]{1,0:T(8,128)(2,1)}) custom-call(s32[8]{0:T(128)} %who.7, f32[512,128]{1,0:T(8,128)} %bitcast.77, f32[2,32,256]{2,1,0:T(8,128)} %bitcast.81, f32[2,32,256]{2,1,0:T(8,128)} %bitcast.83, f32[2,2,16,80]{3,2,1,0:T(8,128)} %bitcast.85, f32[2,2,16,109]{3,2,1,0:T(8,128)} %bitcast.87, ...), custom_call_target="tpu_custom_call" | custom-call | flops 1024 | bytes 1024 | tf_op jit(solution)/shard_map/pallas_call | solution.py:38
  3.6 4.9 %collective-permute-start = (bf16[512,256]{1,0:T(8,128)(2,1)}, bf16[512,256]{1,0:T(8,128)(2,1)S(1)}, u32[]{:S(2)}, u32[]{:S(2)}) collective-permute-start(bf16[512,256]{1,0:T(8,128)(2,1)} %get-tuple-element.144), channel_id=1, source_target_pairs={{0,2},{2,4},{4,6},{6,8},{8,10},{10,12},{12,14},{14,16},{16,18},{18... | collective-permute-start | bytes 786440 | tf_op jit(solution)/shard_map/ppermute | solution.py:92
  8.5 3.6 %collective-permute-start.6 = (bf16[208,256]{1,0:T(8,128)(2,1)}, bf16[208,256]{1,0:T(8,128)(2,1)S(1)}, u32[]{:S(2)}, u32[]{:S(2)}) collective-permute-start(bf16[208,256]{1,0:T(8,128)(2,1)} %get-tuple-element.146.refs_0_), channel_id=1, source_target_pairs={{0,24},{1,25},{2,26},{3,27},{4,28},{5,29},{6,30},{7,31},{8,0},{9,1... | collective-permute-start | bytes 319496 | tf_op jit(solution)/shard_map/ppermute | solution.py:80
  13.1 2.7 %collective-permute-done.6.refs_3_ = bf16[208,256]{1,0:T(8,128)(2,1)S(1)} collective-permute-done((bf16[208,256]{1,0:T(8,128)(2,1)}, bf16[208,256]{1,0:T(8,128)(2,1)S(1)}, u32[]{:S(2)}, u32[]{:S(2)}) %collective-permute-start.6) | collective-permute-done | bytes 106528 | tf_op jit(solution)/shard_map/ppermute | solution.py:80
  15.8 5.4 %collective-permute-done.5.refs_2_ = bf16[208,256]{1,0:T(8,128)(2,1)S(1)} collective-permute-done((bf16[208,256]{1,0:T(8,128)(2,1)}, bf16[208,256]{1,0:T(8,128)(2,1)S(1)}, u32[]{:S(2)}, u32[]{:S(2)}) %collective-permute-start.5) | collective-permute-done | bytes 106528 | tf_op jit(solution)/shard_map/ppermute | solution.py:80
  25.3 5.3 %collective-permute-start.3 = (bf16[208,256]{1,0:T(8,128)(2,1)}, bf16[208,256]{1,0:T(8,128)(2,1)S(1)}, u32[]{:S(2)}, u32[]{:S(2)}) collective-permute-start(bf16[208,256]{1,0:T(8,128)(2,1)} %get-tuple-element.145.refs_0_), channel_id=1, source_target_pairs={{0,24},{1,25},{2,26},{3,27},{4,28},{5,29},{6,30},{7,31},{8,0},{9,1... | collective-permute-start | bytes 319496 | tf_op jit(solution)/shard_map/ppermute | solution.py:80
  30.8 2.0 %collective-permute-start.1 = (bf16[208,256]{1,0:T(8,128)(2,1)}, bf16[208,256]{1,0:T(8,128)(2,1)S(1)}, u32[]{:S(2)}, u32[]{:S(2)}) collective-permute-start(bf16[208,256]{1,0:T(8,128)(2,1)} %get-tuple-element.145.refs_0_), channel_id=1, source_target_pairs={{0,8},{1,9},{2,10},{3,11},{4,12},{5,13},{6,14},{7,15},{8,16},{9,17... | collective-permute-start | bytes 319496 | tf_op jit(solution)/shard_map/ppermute | solution.py:80
  33.2 6.0 %collective-permute-done.2.refs_2_ = bf16[208,256]{1,0:T(8,128)(2,1)S(1)} collective-permute-done((bf16[208,256]{1,0:T(8,128)(2,1)}, bf16[208,256]{1,0:T(8,128)(2,1)S(1)}, u32[]{:S(2)}, u32[]{:S(2)}) %collective-permute-start.2) | collective-permute-done | bytes 106528 | tf_op jit(solution)/shard_map/ppermute | solution.py:80
  46.0 2.3 %collective-permute-done.13.refs_0_.second = bf16[4,208,256]{2,1,0:T(8,128)(2,1)S(1)} collective-permute-done((bf16[4,208,256]{2,1,0:T(8,128)(2,1)S(1)}, bf16[4,208,256]{2,1,0:T(8,128)(2,1)S(1)}, u32[]{:S(2)}, u32[]{:S(2)}) %collective-permute-start.13) | collective-permute-done | bytes 426016 | tf_op jit(solution)/shard_map/ppermute | solution.py:75
  48.3 4.6 %collective-permute-done.12.value.first = bf16[4,208,256]{2,1,0:T(8,128)(2,1)S(1)} collective-permute-done((bf16[4,208,256]{2,1,0:T(8,128)(2,1)S(1)}, bf16[4,208,256]{2,1,0:T(8,128)(2,1)S(1)}, u32[]{:S(2)}, u32[]{:S(2)}) %collective-permute-start.12) | collective-permute-done | bytes 426016 | tf_op jit(solution)/shard_map/ppermute | solution.py:75
  52.9 4.3 %collective-permute-start.15 = (bf16[4,208,256]{2,1,0:T(8,128)(2,1)S(1)}, bf16[4,208,256]{2,1,0:T(8,128)(2,1)S(1)}, u32[]{:S(2)}, u32[]{:S(2)}) collective-permute-start(bf16[4,208,256]{2,1,0:T(8,128)(2,1)S(1)} %get-tuple-element.170), channel_id=1, source_target_pairs={{0,4},{1,3},{2,6},{3,1},{4,0},{5,7},{6,2},{7,5},{8,12},{9,11},{10,... | collective-permute-start | bytes 1277960 | tf_op jit(solution)/shard_map/ppermute | solution.py:75
  58.8 2.3 %collective-permute-done.14.weights = bf16[16,208,256]{2,1,0:T(8,128)(2,1)S(1)} collective-permute-done((bf16[16,208,256]{2,1,0:T(8,128)(2,1)S(1)}, bf16[16,208,256]{2,1,0:T(8,128)(2,1)S(1)}, u32[]{:S(2)}, u32[]{:S(2)}) %collective-permute-start.14) | collective-permute-done | bytes 1703968 | tf_op jit(solution)/shard_map/ppermute | solution.py:86
  63.6 3.6 %collective-permute-done.16.weights = bf16[16,208,256]{2,1,0:T(8,128)(2,1)S(1)} collective-permute-done((bf16[16,208,256]{2,1,0:T(8,128)(2,1)S(1)}, bf16[16,208,256]{2,1,0:T(8,128)(2,1)S(1)}, u32[]{:S(2)}, u32[]{:S(2)}) %collective-permute-start.16) | collective-permute-done | bytes 1703968 | tf_op jit(solution)/shard_map/ppermute | solution.py:86
  67.2 2.1 %shard_map.516 = (f32[256,512]{1,0:T(8,128)S(1)}, f32[256,512]{1,0:T(8,128)S(1)}, f32[256,512]{1,0:T(8,128)S(1)}, f32[272,512]{1,0:T(8,128)S(1)}, bf16[16,208,256]{2,1,0:T(8,128)(2,1)S(1)}) custom-call(f32[272,512]{1,0:T(8,128)S(1)} %get-tuple-element.166.u2, f32[256,512]{1,0:T(8,128)S(1)} %get-tuple-element.167.s1, ...), custom_call_target="tpu_custom_call" | custom-call | flops 1024 | bytes 1024 | tf_op jit(solution)/shard_map/pallas_call | solution.py:38
  70.0 2.0 %shard_map.518 = (f32[256,512]{1,0:T(8,128)S(1)}, f32[256,512]{1,0:T(8,128)S(1)}, f32[256,512]{1,0:T(8,128)S(1)}, f32[8,128]{1,0:T(8,128)}, bf16[16,208,256]{2,1,0:T(8,128)(2,1)S(1)}) custom-call(f32[272,512]{1,0:T(8,128)S(1)} %get-tuple-element.166.u2, f32[256,512]{1,0:T(8,128)S(1)} %get-tuple-element.167.s1, bf16[272,128]{1,0:T(8,128)(2,1)S(1)} %get-tuple-element.159.cond, ...), custom_call_target="tpu_custom_call" | custom-call | flops 1024 | bytes 1024 | tf_op jit(solution)/shard_map/pallas_call | solution.py:38
  73.0 2.1 %collective-permute-start.20 = (bf16[8,208,256]{2,1,0:T(8,128)(2,1)S(1)}, bf16[8,208,256]{2,1,0:T(8,128)(2,1)S(1)}, u32[]{:S(2)}, u32[]{:S(2)}) collective-permute-start(bf16[8,208,256]{2,1,0:T(8,128)(2,1)S(1)} %get-tuple-element.203), channel_id=1, source_target_pairs={{0,4},{1,3},{2,6},{3,1},{4,0},{5,7},{6,2},{7,5},{8,12},{9,11},{10,... | collective-permute-start | bytes 2555912 | tf_op jit(solution)/shard_map/ppermute | solution.py:75
  78.6 7.2 %collective-permute-done.20.near_got = bf16[8,208,256]{2,1,0:T(8,128)(2,1)S(1)} collective-permute-done((bf16[8,208,256]{2,1,0:T(8,128)(2,1)S(1)}, bf16[8,208,256]{2,1,0:T(8,128)(2,1)S(1)}, u32[]{:S(2)}, u32[]{:S(2)}) %collective-permute-start.20) | collective-permute-done | bytes 852000 | tf_op jit(solution)/shard_map/ppermute | solution.py:75
  89.6 7.6 %collective-permute-done.22.last_got = bf16[4,208,256]{2,1,0:T(8,128)(2,1)S(1)} collective-permute-done((bf16[4,208,256]{2,1,0:T(8,128)(2,1)S(1)}, bf16[4,208,256]{2,1,0:T(8,128)(2,1)S(1)}, u32[]{:S(2)}, u32[]{:S(2)}) %collective-permute-start.22) | collective-permute-done | bytes 426016 | tf_op jit(solution)/shard_map/ppermute | solution.py:75
  99.1 2.5 %collective-permute-start.24 = (bf16[208,256]{1,0:T(8,128)(2,1)S(1)}, bf16[208,256]{1,0:T(8,128)(2,1)S(1)}, u32[]{:S(2)}, u32[]{:S(2)}) collective-permute-start(bf16[208,256]{1,0:T(8,128)(2,1)S(1)} %get-tuple-element.210), channel_id=1, source_target_pairs={{0,24},{1,25},{2,26},{3,27},{4,28},{5,29},{6,30},{7,31},{8,0},{9,1... | collective-permute-start | bytes 319496 | tf_op jit(solution)/shard_map/ppermute | solution.py:80
  107.6 6.1 %collective-permute-done.25.last_got = bf16[4,208,256]{2,1,0:T(8,128)(2,1)S(1)} collective-permute-done((bf16[4,208,256]{2,1,0:T(8,128)(2,1)S(1)}, bf16[4,208,256]{2,1,0:T(8,128)(2,1)S(1)}, u32[]{:S(2)}, u32[]{:S(2)}) %collective-permute-start.25) | collective-permute-done | bytes 426016 | tf_op jit(solution)/shard_map/ppermute | solution.py:75
  115.2 2.7 %collective-permute-start.28 = (bf16[208,256]{1,0:T(8,128)(2,1)S(1)}, bf16[208,256]{1,0:T(8,128)(2,1)S(1)}, u32[]{:S(2)}, u32[]{:S(2)}) collective-permute-start(bf16[208,256]{1,0:T(8,128)(2,1)S(1)} %get-tuple-element.215), channel_id=1, source_target_pairs={{0,16},{1,17},{2,18},{3,19},{4,20},{5,21},{6,22},{7,23},{8,24},{9,... | collective-permute-start | bytes 319496 | tf_op jit(solution)/shard_map/ppermute | solution.py:80
  121.7 2.6 %collective-permute-done.28.refs_2_ = bf16[208,256]{1,0:T(8,128)(2,1)S(1)} collective-permute-done((bf16[208,256]{1,0:T(8,128)(2,1)S(1)}, bf16[208,256]{1,0:T(8,128)(2,1)S(1)}, u32[]{:S(2)}, u32[]{:S(2)}) %collective-permute-start.28) | collective-permute-done | bytes 106528 | tf_op jit(solution)/shard_map/ppermute | solution.py:80
  126.3 13.0 %all_to_all.5 = f32[16,1,128]{2,1,0:T(1,128)S(1)} all-to-all(f32[16,1,128]{2,1,0:T(1,128)S(1)} %broadcast_in_dim.13), channel_id=1, replica_groups=mesh['tm'=16,'mp'=2] {'tm'}, dimensions={0} | all-to-all | bytes 16384 | tf_op jit(solution)/shard_map/all_to_all | solution.py:911
  139.5 2.3 %shard_map.533 = (f32[1,1]{1,0:T(1,128)}, f32[512,128]{1,0:T(8,128)}, f32[512,128]{1,0:T(8,128)}, f32[512,128]{1,0:T(8,128)}, f32[512,128]{1,0:T(8,128)}, /*inde...) custom-call(s32[8]{0:T(128)S(1)} %copy-done.21, ...), custom_call_target="tpu_custom_call" | custom-call | flops 1024 | bytes 1024 | tf_op jit(solution)/shard_map/pallas_call | solution.py:38
  (128 shorter events, 41.3 us)
Async XLA Ops:
  3.6 17.7 %collective-permute-start = (bf16[512,256]{1,0:T(8,128)(2,1)}, bf16[512,256]{1,0:T(8,128)(2,1)S(1)}, u32[]{:S(2)}, u32[]{:S(2)}) collective-permute-start(bf16[512,256]{1,0:T(8,128)(2,1)} %get-tuple-element.144), channel_id=1, source_target_pairs={{0,2},{2,4},{4,6},{6,8},{8,10},{10,12},{12,14},{14,16},{16,18},{18... | collective-permute-start | bytes 786440 | tf_op jit(solution)/shard_map/ppermute | solution.py:92
  8.5 7.4 %collective-permute-start.6 = (bf16[208,256]{1,0:T(8,128)(2,1)}, bf16[208,256]{1,0:T(8,128)(2,1)S(1)}, u32[]{:S(2)}, u32[]{:S(2)}) collective-permute-start(bf16[208,256]{1,0:T(8,128)(2,1)} %get-tuple-element.146.refs_0_), channel_id=1, source_target_pairs={{0,24},{1,25},{2,26},{3,27},{4,28},{5,29},{6,30},{7,31},{8,0},{9,1... | collective-permute-start | bytes 319496 | tf_op jit(solution)/shard_map/ppermute | solution.py:80
  12.1 9.2 %collective-permute-start.5 = (bf16[208,256]{1,0:T(8,128)(2,1)}, bf16[208,256]{1,0:T(8,128)(2,1)S(1)}, u32[]{:S(2)}, u32[]{:S(2)}) collective-permute-start(bf16[208,256]{1,0:T(8,128)(2,1)} %get-tuple-element.146.refs_0_), channel_id=1, source_target_pairs={{0,16},{1,17},{2,18},{3,19},{4,20},{5,21},{6,22},{7,23},{8,24},{9,... | collective-permute-start | bytes 319496 | tf_op jit(solution)/shard_map/ppermute | solution.py:80
  12.1 9.2 %collective-permute-start.4 = (bf16[208,256]{1,0:T(8,128)(2,1)}, bf16[208,256]{1,0:T(8,128)(2,1)S(1)}, u32[]{:S(2)}, u32[]{:S(2)}) collective-permute-start(bf16[208,256]{1,0:T(8,128)(2,1)} %get-tuple-element.146.refs_0_), channel_id=1, source_target_pairs={{0,8},{1,9},{2,10},{3,11},{4,12},{5,13},{6,14},{7,15},{8,16},{9,17... | collective-permute-start | bytes 319496 | tf_op jit(solution)/shard_map/ppermute | solution.py:80
  22.2 19.0 %collective-permute-start.9 = (bf16[4,208,256]{2,1,0:T(8,128)(2,1)S(1)}, bf16[4,208,256]{2,1,0:T(8,128)(2,1)S(1)}, u32[]{:S(2)}, u32[]{:S(2)}) collective-permute-start(bf16[4,208,256]{2,1,0:T(8,128)(2,1)S(1)} %get-tuple-element.151.group), channel_id=1, source_target_pairs={{0,4},{1,3},{2,6},{3,1},{4,0},{5,7},{6,2},{7,5},{8,12},{9,11},{10,... | collective-permute-start | bytes 1277960 | tf_op jit(solution)/shard_map/ppermute | solution.py:75
  23.8 17.4 %collective-permute-start.8 = (bf16[4,208,256]{2,1,0:T(8,128)(2,1)S(1)}, bf16[4,208,256]{2,1,0:T(8,128)(2,1)S(1)}, u32[]{:S(2)}, u32[]{:S(2)}) collective-permute-start(bf16[4,208,256]{2,1,0:T(8,128)(2,1)S(1)} %get-tuple-element.151.group), channel_id=1, source_target_pairs={{0,2},{1,5},{2,0},{3,7},{4,6},{5,1},{6,4},{7,3},{8,10},{9,13},{10,... | collective-permute-start | bytes 1277960 | tf_op jit(solution)/shard_map/ppermute | solution.py:75
  25.3 7.9 %collective-permute-start.3 = (bf16[208,256]{1,0:T(8,128)(2,1)}, bf16[208,256]{1,0:T(8,128)(2,1)S(1)}, u32[]{:S(2)}, u32[]{:S(2)}) collective-permute-start(bf16[208,256]{1,0:T(8,128)(2,1)} %get-tuple-element.145.refs_0_), channel_id=1, source_target_pairs={{0,24},{1,25},{2,26},{3,27},{4,28},{5,29},{6,30},{7,31},{8,0},{9,1... | collective-permute-start | bytes 319496 | tf_op jit(solution)/shard_map/ppermute | solution.py:80
  30.6 8.6 %collective-permute-start.2 = (bf16[208,256]{1,0:T(8,128)(2,1)}, bf16[208,256]{1,0:T(8,128)(2,1)S(1)}, u32[]{:S(2)}, u32[]{:S(2)}) collective-permute-start(bf16[208,256]{1,0:T(8,128)(2,1)} %get-tuple-element.145.refs_0_), channel_id=1, source_target_pairs={{0,16},{1,17},{2,18},{3,19},{4,20},{5,21},{6,22},{7,23},{8,24},{9,... | collective-permute-start | bytes 319496 | tf_op jit(solution)/shard_map/ppermute | solution.py:80
  30.8 8.3 %collective-permute-start.1 = (bf16[208,256]{1,0:T(8,128)(2,1)}, bf16[208,256]{1,0:T(8,128)(2,1)S(1)}, u32[]{:S(2)}, u32[]{:S(2)}) collective-permute-start(bf16[208,256]{1,0:T(8,128)(2,1)} %get-tuple-element.145.refs_0_), channel_id=1, source_target_pairs={{0,8},{1,9},{2,10},{3,11},{4,12},{5,13},{6,14},{7,15},{8,16},{9,17... | collective-permute-start | bytes 319496 | tf_op jit(solution)/shard_map/ppermute | solution.py:80
  40.1 8.2 %collective-permute-start.13 = (bf16[4,208,256]{2,1,0:T(8,128)(2,1)S(1)}, bf16[4,208,256]{2,1,0:T(8,128)(2,1)S(1)}, u32[]{:S(2)}, u32[]{:S(2)}) collective-permute-start(bf16[4,208,256]{2,1,0:T(8,128)(2,1)S(1)} %get-tuple-element.162.group), channel_id=1, source_target_pairs={{0,4},{1,3},{2,6},{3,1},{4,0},{5,7},{6,2},{7,5},{8,12},{9,11},{10,... | collective-permute-start | bytes 1277960 | tf_op jit(solution)/shard_map/ppermute | solution.py:75
  40.5 12.4 %collective-permute-start.12 = (bf16[4,208,256]{2,1,0:T(8,128)(2,1)S(1)}, bf16[4,208,256]{2,1,0:T(8,128)(2,1)S(1)}, u32[]{:S(2)}, u32[]{:S(2)}) collective-permute-start(bf16[4,208,256]{2,1,0:T(8,128)(2,1)S(1)} %get-tuple-element.162.group), channel_id=1, source_target_pairs={{0,2},{1,5},{2,0},{3,7},{4,6},{5,1},{6,4},{7,3},{8,10},{9,13},{10,... | collective-permute-start | bytes 1277960 | tf_op jit(solution)/shard_map/ppermute | solution.py:75
  41.2 16.0 %collective-permute-start.11 = (bf16[4,208,256]{2,1,0:T(8,128)(2,1)S(1)}, bf16[4,208,256]{2,1,0:T(8,128)(2,1)S(1)}, u32[]{:S(2)}, u32[]{:S(2)}) collective-permute-start(bf16[4,208,256]{2,1,0:T(8,128)(2,1)S(1)} %get-tuple-element.161), channel_id=1, source_target_pairs={{0,4},{1,3},{2,6},{3,1},{4,0},{5,7},{6,2},{7,5},{8,12},{9,11},{10,... | collective-permute-start | bytes 1277960 | tf_op jit(solution)/shard_map/ppermute | solution.py:75
  52.9 10.5 %collective-permute-start.15 = (bf16[4,208,256]{2,1,0:T(8,128)(2,1)S(1)}, bf16[4,208,256]{2,1,0:T(8,128)(2,1)S(1)}, u32[]{:S(2)}, u32[]{:S(2)}) collective-permute-start(bf16[4,208,256]{2,1,0:T(8,128)(2,1)S(1)} %get-tuple-element.170), channel_id=1, source_target_pairs={{0,4},{1,3},{2,6},{3,1},{4,0},{5,7},{6,2},{7,5},{8,12},{9,11},{10,... | collective-permute-start | bytes 1277960 | tf_op jit(solution)/shard_map/ppermute | solution.py:75
  73.0 12.8 %collective-permute-start.20 = (bf16[8,208,256]{2,1,0:T(8,128)(2,1)S(1)}, bf16[8,208,256]{2,1,0:T(8,128)(2,1)S(1)}, u32[]{:S(2)}, u32[]{:S(2)}) collective-permute-start(bf16[8,208,256]{2,1,0:T(8,128)(2,1)S(1)} %get-tuple-element.203), channel_id=1, source_target_pairs={{0,4},{1,3},{2,6},{3,1},{4,0},{5,7},{6,2},{7,5},{8,12},{9,11},{10,... | collective-permute-start | bytes 2555912 | tf_op jit(solution)/shard_map/ppermute | solution.py:75
  77.1 10.2 %collective-permute-start.19 = (bf16[16,208,256]{2,1,0:T(8,128)(2,1)S(1)}, bf16[16,208,256]{2,1,0:T(8,128)(2,1)S(1)}, u32[]{:S(2)}, u32[]{:S(2)}) collective-permute-start(bf16[16,208,256]{2,1,0:T(8,128)(2,1)S(1)} %get-tuple-element.202), channel_id=1, source_target_pairs={{0,1},{1,0},{2,3},{3,2},{4,5},{5,4},{6,7},{7,6},{8,9},{9,8},{10,11... | collective-permute-start | bytes 5111816 | tf_op jit(solution)/shard_map/ppermute | solution.py:86
  85.9 11.3 %collective-permute-start.22 = (bf16[4,208,256]{2,1,0:T(8,128)(2,1)S(1)}, bf16[4,208,256]{2,1,0:T(8,128)(2,1)S(1)}, u32[]{:S(2)}, u32[]{:S(2)}) collective-permute-start(bf16[4,208,256]{2,1,0:T(8,128)(2,1)S(1)} %get-tuple-element.208), channel_id=1, source_target_pairs={{0,2},{1,5},{2,0},{3,7},{4,6},{5,1},{6,4},{7,3},{8,10},{9,13},{10,... | collective-permute-start | bytes 1277960 | tf_op jit(solution)/shard_map/ppermute | solution.py:75
  87.1 14.5 %collective-permute-start.18 = (f32[256,1024]{1,0:T(8,128)S(1)}, f32[256,1024]{1,0:T(8,128)S(1)}, u32[]{:S(2)}, u32[]{:S(2)}) collective-permute-start(f32[256,1024]{1,0:T(8,128)S(1)} %get-tuple-element.196), channel_id=1, source_target_pairs={{0,1},{1,0},{2,3},{3,2},{4,5},{5,4},{6,7},{7,6},{8,9},{9,8},{10,11... | collective-permute-start | bytes 3145736 | tf_op jit(solution)/shard_map/ppermute | solution.py:86
  88.0 17.0 %collective-permute-start.21 = (bf16[8,208,256]{2,1,0:T(8,128)(2,1)S(1)}, bf16[8,208,256]{2,1,0:T(8,128)(2,1)S(1)}, u32[]{:S(2)}, u32[]{:S(2)}) collective-permute-start(bf16[8,208,256]{2,1,0:T(8,128)(2,1)S(1)} %get-tuple-element.206), channel_id=1, source_target_pairs={{0,4},{1,3},{2,6},{3,1},{4,0},{5,7},{6,2},{7,5},{8,12},{9,11},{10,... | collective-permute-start | bytes 2555912 | tf_op jit(solution)/shard_map/ppermute | solution.py:75
  97.8 6.6 %collective-permute-start.23 = (bf16[208,256]{1,0:T(8,128)(2,1)S(1)}, bf16[208,256]{1,0:T(8,128)(2,1)S(1)}, u32[]{:S(2)}, u32[]{:S(2)}) collective-permute-start(bf16[208,256]{1,0:T(8,128)(2,1)S(1)} %get-tuple-element.209), channel_id=1, source_target_pairs={{0,8},{1,9},{2,10},{3,11},{4,12},{5,13},{6,14},{7,15},{8,16},{9,17... | collective-permute-start | bytes 319496 | tf_op jit(solution)/shard_map/ppermute | solution.py:80
  105.6 8.1 %collective-permute-start.25 = (bf16[4,208,256]{2,1,0:T(8,128)(2,1)S(1)}, bf16[4,208,256]{2,1,0:T(8,128)(2,1)S(1)}, u32[]{:S(2)}, u32[]{:S(2)}) collective-permute-start(bf16[4,208,256]{2,1,0:T(8,128)(2,1)S(1)} %get-tuple-element.211), channel_id=1, source_target_pairs={{0,2},{1,5},{2,0},{3,7},{4,6},{5,1},{6,4},{7,3},{8,10},{9,13},{10,... | collective-permute-start | bytes 1277960 | tf_op jit(solution)/shard_map/ppermute | solution.py:75
  106.9 11.3 %collective-permute-start.30 = (bf16[208,256]{1,0:T(8,128)(2,1)S(1)}, bf16[208,256]{1,0:T(8,128)(2,1)S(1)}, u32[]{:S(2)}, u32[]{:S(2)}) collective-permute-start(bf16[208,256]{1,0:T(8,128)(2,1)S(1)} %get-tuple-element.219), channel_id=1, source_target_pairs={{0,16},{1,17},{2,18},{3,19},{4,20},{5,21},{6,22},{7,23},{8,24},{9,... | collective-permute-start | bytes 319496 | tf_op jit(solution)/shard_map/ppermute | solution.py:80
  114.2 7.6 %collective-permute-start.27 = (bf16[208,256]{1,0:T(8,128)(2,1)S(1)}, bf16[208,256]{1,0:T(8,128)(2,1)S(1)}, u32[]{:S(2)}, u32[]{:S(2)}) collective-permute-start(bf16[208,256]{1,0:T(8,128)(2,1)S(1)} %get-tuple-element.214), channel_id=1, source_target_pairs={{0,8},{1,9},{2,10},{3,11},{4,12},{5,13},{6,14},{7,15},{8,16},{9,17... | collective-permute-start | bytes 319496 | tf_op jit(solution)/shard_map/ppermute | solution.py:80
  115.2 9.1 %collective-permute-start.28 = (bf16[208,256]{1,0:T(8,128)(2,1)S(1)}, bf16[208,256]{1,0:T(8,128)(2,1)S(1)}, u32[]{:S(2)}, u32[]{:S(2)}) collective-permute-start(bf16[208,256]{1,0:T(8,128)(2,1)S(1)} %get-tuple-element.215), channel_id=1, source_target_pairs={{0,16},{1,17},{2,18},{3,19},{4,20},{5,21},{6,22},{7,23},{8,24},{9,... | collective-permute-start | bytes 319496 | tf_op jit(solution)/shard_map/ppermute | solution.py:80
  119.0 22.7 %collective-permute-start.26 = (bf16[512,256]{1,0:T(8,128)(2,1)S(1)}, bf16[512,256]{1,0:T(8,128)(2,1)S(1)}, u32[]{:S(2)}, u32[]{:S(2)}) collective-permute-start(bf16[512,256]{1,0:T(8,128)(2,1)S(1)} %shard_map.529), channel_id=1, source_target_pairs={{2,0},{4,2},{6,4},{8,6},{10,8},{12,10},{14,12},{16,14},{18,16},{20... | collective-permute-start | bytes 786440 | tf_op jit(solution)/shard_map/ppermute | solution.py:92
  (35 other events, 626.5 us)

commit v4 on v3

--- a/solution.py
+++ b/solution.py
@@ -541,9 +541,10 @@
 
 
 def widen_body(
-    mel, clips, lengths, inner, side, near_edge, edge, x_out, cot_out, skip_out, lag_out, cond, marks
+    mel, clips, lengths, inner, side, near_edge, edge, *refs
 ):
     far, near, core = place()[:3]
+    x_out, cot_out, skip_out, lag_out, cond, marks = refs[-6:]
     own, full = inner.shape[0], inner.shape[1] // 4
     wide = own + 2 * EDGE
     after = jnp.where(core == 0, near_edge[...], edge[...])
@@ -767,6 +768,7 @@
         scratch=[pltpu.VMEM(x_input.shape, F32)],
     )
     parts_one, relayed = near_exchange(group_one, (stacked,), LONG)
+    parts_two, begun = near_exchange(group_two, (), LONG)
     joined_own = struct((own, 4 * full))
     edge = struct((EDGE, 4 * full + LANES))
     inner, side, near_edge, edge_sent = call(
@@ -794,9 +796,9 @@
         near_edge,
         across_chips(edge_sent),
         scalars=(clip_length_array,),
-    )
-    parts_two, begun = near_exchange(group_two, (marks,))
-    w1_own, w1_oth = joined(parts_one, (begun,))
+        unread=(begun,),
+    )
+    w1_own, w1_oth = joined(parts_one, (marks,))
 
     half = struct((own, width))
     wave = struct((own, full))
@@ -880,6 +882,7 @@
     grads2, sent2, token = near_summed(grads2, sent2, LONG, (token,))
     grads1, sent1, _ = cores_summed(grad_own, grad_oth, (token,))
     last_got = across(sent2, 0)
+    terms2, _ = far_terms(grads2, last_got, LONG)
     kept, given = call(
         divide_body,
         (struct((own, 4 * width)),) * 2,
@@ -887,13 +890,13 @@
         skip_total,
         g1_part,
         dlag1,
+        unread=(terms2[1], terms2[-1]),
         scratch=[pltpu.VMEM((own, full), F32)],
     )
     mixed, skip_total, grad_input, push, token = call(
         finish_body, (struct((held_rows, width)),) * 4 + (TOKEN,), kept, swap_cores(given)
     )
-    terms2, _ = far_terms(grads2, last_got, LONG)
-    grads1, sent1, _ = near_summed(grads1, sent1, unread=(token, terms2[1], terms2[-1]))
+    grads1, sent1, _ = near_summed(grads1, sent1, unread=(terms2[1], terms2[-1]))
     terms1, token = far_terms(grads1, across(sent1, 0))
     push = call(push_body, struct((held_rows, width), BF16), push, unread=(token,))
     grad_input = call(

time: 143 us -> 142 us (level)
  starting transfers between devices: 44.2 us -> 40.7 us
  waiting for transfers between devices: 58.5 us -> 61.9 us
    ppermute x10, starting transfers between devices: 15.9 us -> 11.8 us  [across(): return lax.ppermute(value, BOTH, route(lambda i, c: i ^ 1 + (c ^ bit)))]
    ppermute x10, waiting for transfers between devices: 29.1 us -> 32.2 us  [across(): return lax.ppermute(value, BOTH, route(lambda i, c: i ^ 1 + (c ^ bit)))]
  transfers between devices with their start and end apart: 32 -> 32, of which waited for: 19 -> 17; matrix products, arithmetic and copies ran while one was open for 0% -> 0% of each run, Pallas kernels for 12% -> 12%
where the time goes in v4:
time: 142 us
  waiting for transfers between devices  61.9 us (44%)
  starting transfers between devices  40.7 us (29%)
  Pallas kernels  23.6 us (17%)
  blocking collectives  12.4 us (9%)
  local copies, waits for them, and re-layouts  1.95 us (1%)
    ppermute x10, waiting for transfers between devices, across(): return lax.ppermute(value, BOTH, route(lambda i, c: i ^ 1 + (c ^ bit)))  32.2 us
    pallas_call x30, Pallas kernels, call(): pl.pallas_call(body, out_shape=out_shape, in_specs=specs, scratch_shapes=...  23.6 us
    ppermute x12, starting transfers between devices, along_far(): lax.ppermute(value, BOTH, route(lambda i, c: (i // NEAR + distance) % far...  21.6 us
    ppermute x12, waiting for transfers between devices, along_far(): lax.ppermute(value, BOTH, route(lambda i, c: (i // NEAR + distance) % far...  21 us
    all_to_all x1, blocking collectives, on_device(): lax.all_to_all(sent, 'tm', split_axis=0, concat_axis=0, tiled=True)  12.4 us
    ppermute x10, starting transfers between devices, across(): return lax.ppermute(value, BOTH, route(lambda i, c: i ^ 1 + (c ^ bit)))  11.8 us
    ppermute x7, waiting for transfers between devices, swap_cores(): return lax.ppermute(value, 'mp', [(0, 1), (1, 0)])  8.72 us
    ppermute x2, starting transfers between devices, shifted(): return lax.ppermute(value, axis, pairs)  6.15 us
  transfers between devices with their start and end apart: 32, of which 17 were waited for; matrix products, arithmetic and copies ran while one was open for 0% of the time, Pallas kernels for 12%

profile of v4, /device:TPU:0, one launch (start us, length us, event | category | flops | bytes accessed | tf_op | source)
XLA Modules:
  0.0 141.9 jit_solution(17831587355887593817)
XLA Ops:
  0.7 2.9 %shard_map.504 = (bf16[208,256]{1,0:T(8,128)(2,1)}, bf16[208,256]{1,0:T(8,128)(2,1)}, bf16[512,256]{1,0:T(8,128)(2,1)}) custom-call(s32[8]{0:T(128)} %who.7, f32[512,128]{1,0:T(8,128)} %bitcast.77, f32[2,32,256]{2,1,0:T(8,128)} %bitcast.81, f32[2,32,256]{2,1,0:T(8,128)} %bitcast.83, f32[2,2,16,80]{3,2,1,0:T(8,128)} %bitcast.85, f32[2,2,16,109]{3,2,1,0:T(8,128)} %bitcast.87, ...), custom_call_target="tpu_custom_call" | custom-call | flops 1024 | bytes 1024 | tf_op jit(solution)/shard_map/pallas_call | solution.py:38
  3.6 4.9 %collective-permute-start = (bf16[512,256]{1,0:T(8,128)(2,1)}, bf16[512,256]{1,0:T(8,128)(2,1)S(1)}, u32[]{:S(2)}, u32[]{:S(2)}) collective-permute-start(bf16[512,256]{1,0:T(8,128)(2,1)} %get-tuple-element.143), channel_id=1, source_target_pairs={{0,2},{2,4},{4,6},{6,8},{8,10},{10,12},{12,14},{14,16},{16,18},{18... | collective-permute-start | bytes 786440 | tf_op jit(solution)/shard_map/ppermute | solution.py:92
  8.5 3.6 %collective-permute-start.6 = (bf16[208,256]{1,0:T(8,128)(2,1)}, bf16[208,256]{1,0:T(8,128)(2,1)S(1)}, u32[]{:S(2)}, u32[]{:S(2)}) collective-permute-start(bf16[208,256]{1,0:T(8,128)(2,1)} %get-tuple-element.145.refs_0_), channel_id=1, source_target_pairs={{0,24},{1,25},{2,26},{3,27},{4,28},{5,29},{6,30},{7,31},{8,0},{9,1... | collective-permute-start | bytes 319496 | tf_op jit(solution)/shard_map/ppermute | solution.py:80
  13.1 2.7 %collective-permute-done.6.refs_3_ = bf16[208,256]{1,0:T(8,128)(2,1)S(1)} collective-permute-done((bf16[208,256]{1,0:T(8,128)(2,1)}, bf16[208,256]{1,0:T(8,128)(2,1)S(1)}, u32[]{:S(2)}, u32[]{:S(2)}) %collective-permute-start.6) | collective-permute-done | bytes 106528 | tf_op jit(solution)/shard_map/ppermute | solution.py:80
  15.8 5.4 %collective-permute-done.5.refs_2_ = bf16[208,256]{1,0:T(8,128)(2,1)S(1)} collective-permute-done((bf16[208,256]{1,0:T(8,128)(2,1)}, bf16[208,256]{1,0:T(8,128)(2,1)S(1)}, u32[]{:S(2)}, u32[]{:S(2)}) %collective-permute-start.5) | collective-permute-done | bytes 106528 | tf_op jit(solution)/shard_map/ppermute | solution.py:80
  25.3 5.3 %collective-permute-start.3 = (bf16[208,256]{1,0:T(8,128)(2,1)}, bf16[208,256]{1,0:T(8,128)(2,1)S(1)}, u32[]{:S(2)}, u32[]{:S(2)}) collective-permute-start(bf16[208,256]{1,0:T(8,128)(2,1)} %get-tuple-element.144.refs_0_), channel_id=1, source_target_pairs={{0,24},{1,25},{2,26},{3,27},{4,28},{5,29},{6,30},{7,31},{8,0},{9,1... | collective-permute-start | bytes 319496 | tf_op jit(solution)/shard_map/ppermute | solution.py:80
  30.8 2.0 %collective-permute-start.1 = (bf16[208,256]{1,0:T(8,128)(2,1)}, bf16[208,256]{1,0:T(8,128)(2,1)S(1)}, u32[]{:S(2)}, u32[]{:S(2)}) collective-permute-start(bf16[208,256]{1,0:T(8,128)(2,1)} %get-tuple-element.144.refs_0_), channel_id=1, source_target_pairs={{0,8},{1,9},{2,10},{3,11},{4,12},{5,13},{6,14},{7,15},{8,16},{9,17... | collective-permute-start | bytes 319496 | tf_op jit(solution)/shard_map/ppermute | solution.py:80
  33.2 6.0 %collective-permute-done.2.refs_2_ = bf16[208,256]{1,0:T(8,128)(2,1)S(1)} collective-permute-done((bf16[208,256]{1,0:T(8,128)(2,1)}, bf16[208,256]{1,0:T(8,128)(2,1)S(1)}, u32[]{:S(2)}, u32[]{:S(2)}) %collective-permute-start.2) | collective-permute-done | bytes 106528 | tf_op jit(solution)/shard_map/ppermute | solution.py:80
  44.9 3.4 %collective-permute-done.12.refs_0_.second = bf16[4,208,256]{2,1,0:T(8,128)(2,1)S(1)} collective-permute-done((bf16[4,208,256]{2,1,0:T(8,128)(2,1)S(1)}, bf16[4,208,256]{2,1,0:T(8,128)(2,1)S(1)}, u32[]{:S(2)}, u32[]{:S(2)}) %collective-permute-start.12) | collective-permute-done | bytes 426016 | tf_op jit(solution)/shard_map/ppermute | solution.py:75
  48.3 4.5 %collective-permute-done.11.value.first = bf16[4,208,256]{2,1,0:T(8,128)(2,1)S(1)} collective-permute-done((bf16[4,208,256]{2,1,0:T(8,128)(2,1)S(1)}, bf16[4,208,256]{2,1,0:T(8,128)(2,1)S(1)}, u32[]{:S(2)}, u32[]{:S(2)}) %collective-permute-start.11) | collective-permute-done | bytes 426016 | tf_op jit(solution)/shard_map/ppermute | solution.py:75
  57.3 2.3 %collective-permute-done.14.weights = bf16[16,208,256]{2,1,0:T(8,128)(2,1)S(1)} collective-permute-done((bf16[16,208,256]{2,1,0:T(8,128)(2,1)S(1)}, bf16[16,208,256]{2,1,0:T(8,128)(2,1)S(1)}, u32[]{:S(2)}, u32[]{:S(2)}) %collective-permute-start.14) | collective-permute-done | bytes 1703968 | tf_op jit(solution)/shard_map/ppermute | solution.py:86
  61.3 3.6 %collective-permute-done.16.weights = bf16[16,208,256]{2,1,0:T(8,128)(2,1)S(1)} collective-permute-done((bf16[16,208,256]{2,1,0:T(8,128)(2,1)S(1)}, bf16[16,208,256]{2,1,0:T(8,128)(2,1)S(1)}, u32[]{:S(2)}, u32[]{:S(2)}) %collective-permute-start.16) | collective-permute-done | bytes 1703968 | tf_op jit(solution)/shard_map/ppermute | solution.py:86
  64.9 2.1 %shard_map.516 = (f32[256,512]{1,0:T(8,128)S(1)}, f32[256,512]{1,0:T(8,128)S(1)}, f32[256,512]{1,0:T(8,128)S(1)}, f32[272,512]{1,0:T(8,128)S(1)}, bf16[16,208,256]{2,1,0:T(8,128)(2,1)S(1)}) custom-call(f32[272,512]{1,0:T(8,128)S(1)} %get-tuple-element.165.u2, f32[256,512]{1,0:T(8,128)S(1)} %get-tuple-element.166.s1, ...), custom_call_target="tpu_custom_call" | custom-call | flops 1024 | bytes 1024 | tf_op jit(solution)/shard_map/pallas_call | solution.py:38
  67.7 2.0 %shard_map.518 = (f32[256,512]{1,0:T(8,128)S(1)}, f32[256,512]{1,0:T(8,128)S(1)}, f32[256,512]{1,0:T(8,128)S(1)}, f32[8,128]{1,0:T(8,128)}, bf16[16,208,256]{2,1,0:T(8,128)(2,1)S(1)}) custom-call(f32[272,512]{1,0:T(8,128)S(1)} %get-tuple-element.165.u2, f32[256,512]{1,0:T(8,128)S(1)} %get-tuple-element.166.s1, bf16[272,128]{1,0:T(8,128)(2,1)S(1)} %get-tuple-element.160.cond, ...), custom_call_target="tpu_custom_call" | custom-call | flops 1024 | bytes 1024 | tf_op jit(solution)/shard_map/pallas_call | solution.py:38
  72.5 1.9 %shard_map.520 = (f32[256,512]{1,0:T(8,128)S(1)}, f32[8,128]{1,0:T(8,128)}, f32[256,512]{1,0:T(8,128)S(1)}, bf16[16,208,256]{2,1,0:T(8,128)(2,1)S(1)}) custom-call(f32[256,512]{1,0:T(8,128)S(1)} %get-tuple-element.179.g2, f32[272,512]{1,0:T(8,128)S(1)} %get-tuple-element.158.x, bf16[256,512]{1,0:T(8,128)(2,1)S(1)} %get-tuple-element.180.lag, ...), custom_call_target="tpu_custom_call" | custom-call | flops 1024 | bytes 1024 | tf_op jit(solution)/shard_map/pallas_call | solution.py:38
  76.0 7.4 %collective-permute-done.18.near_got = bf16[8,208,256]{2,1,0:T(8,128)(2,1)S(1)} collective-permute-done((bf16[8,208,256]{2,1,0:T(8,128)(2,1)S(1)}, bf16[8,208,256]{2,1,0:T(8,128)(2,1)S(1)}, u32[]{:S(2)}, u32[]{:S(2)}) %collective-permute-start.18) | collective-permute-done | bytes 852000 | tf_op jit(solution)/shard_map/ppermute | solution.py:75
  86.1 9.8 %collective-permute-done.19.last_got = bf16[4,208,256]{2,1,0:T(8,128)(2,1)S(1)} collective-permute-done((bf16[4,208,256]{2,1,0:T(8,128)(2,1)S(1)}, bf16[4,208,256]{2,1,0:T(8,128)(2,1)S(1)}, u32[]{:S(2)}, u32[]{:S(2)}) %collective-permute-start.19) | collective-permute-done | bytes 426016 | tf_op jit(solution)/shard_map/ppermute | solution.py:75
  96.8 3.6 %collective-permute-start.21 = (bf16[208,256]{1,0:T(8,128)(2,1)S(1)}, bf16[208,256]{1,0:T(8,128)(2,1)S(1)}, u32[]{:S(2)}, u32[]{:S(2)}) collective-permute-start(bf16[208,256]{1,0:T(8,128)(2,1)S(1)} %get-tuple-element.198), channel_id=1, source_target_pairs={{0,24},{1,25},{2,26},{3,27},{4,28},{5,29},{6,30},{7,31},{8,0},{9,1... | collective-permute-start | bytes 319496 | tf_op jit(solution)/shard_map/ppermute | solution.py:80
  100.3 2.8 %collective-permute-done.20.refs_0_.refs_1_ = bf16[208,256]{1,0:T(8,128)(2,1)S(1)} collective-permute-done((bf16[208,256]{1,0:T(8,128)(2,1)S(1)}, bf16[208,256]{1,0:T(8,128)(2,1)S(1)}, u32[]{:S(2)}, u32[]{:S(2)}) %collective-permute-start.20) | collective-permute-done | bytes 106528 | tf_op jit(solution)/shard_map/ppermute | solution.py:80
  105.7 6.5 %collective-permute-done.25.last_got = bf16[4,208,256]{2,1,0:T(8,128)(2,1)S(1)} collective-permute-done((bf16[4,208,256]{2,1,0:T(8,128)(2,1)S(1)}, bf16[4,208,256]{2,1,0:T(8,128)(2,1)S(1)}, u32[]{:S(2)}, u32[]{:S(2)}) %collective-permute-start.25) | collective-permute-done | bytes 426016 | tf_op jit(solution)/shard_map/ppermute | solution.py:75
  114.1 2.7 %collective-permute-start.28 = (bf16[208,256]{1,0:T(8,128)(2,1)S(1)}, bf16[208,256]{1,0:T(8,128)(2,1)S(1)}, u32[]{:S(2)}, u32[]{:S(2)}) collective-permute-start(bf16[208,256]{1,0:T(8,128)(2,1)S(1)} %get-tuple-element.213), channel_id=1, source_target_pairs={{0,16},{1,17},{2,18},{3,19},{4,20},{5,21},{6,22},{7,23},{8,24},{9,... | collective-permute-start | bytes 319496 | tf_op jit(solution)/shard_map/ppermute | solution.py:80
  120.5 3.8 %collective-permute-done.28.refs_2_ = bf16[208,256]{1,0:T(8,128)(2,1)S(1)} collective-permute-done((bf16[208,256]{1,0:T(8,128)(2,1)S(1)}, bf16[208,256]{1,0:T(8,128)(2,1)S(1)}, u32[]{:S(2)}, u32[]{:S(2)}) %collective-permute-start.28) | collective-permute-done | bytes 106528 | tf_op jit(solution)/shard_map/ppermute | solution.py:80
  126.2 12.4 %all_to_all.5 = f32[16,1,128]{2,1,0:T(1,128)S(1)} all-to-all(f32[16,1,128]{2,1,0:T(1,128)S(1)} %broadcast_in_dim.13), channel_id=1, replica_groups=mesh['tm'=16,'mp'=2] {'tm'}, dimensions={0} | all-to-all | bytes 16384 | tf_op jit(solution)/shard_map/all_to_all | solution.py:914
  138.8 2.3 %shard_map.533 = (f32[1,1]{1,0:T(1,128)}, f32[512,128]{1,0:T(8,128)}, f32[512,128]{1,0:T(8,128)}, f32[512,128]{1,0:T(8,128)}, f32[512,128]{1,0:T(8,128)}, /*inde...) custom-call(s32[8]{0:T(128)S(1)} %copy-done.21, ...), custom_call_target="tpu_custom_call" | custom-call | flops 1024 | bytes 1024 | tf_op jit(solution)/shard_map/pallas_call | solution.py:38
  (128 shorter events, 36.8 us)
Async XLA Ops:
  3.6 17.7 %collective-permute-start = (bf16[512,256]{1,0:T(8,128)(2,1)}, bf16[512,256]{1,0:T(8,128)(2,1)S(1)}, u32[]{:S(2)}, u32[]{:S(2)}) collective-permute-start(bf16[512,256]{1,0:T(8,128)(2,1)} %get-tuple-element.143), channel_id=1, source_target_pairs={{0,2},{2,4},{4,6},{6,8},{8,10},{10,12},{12,14},{14,16},{16,18},{18... | collective-permute-start | bytes 786440 | tf_op jit(solution)/shard_map/ppermute | solution.py:92
  12.1 9.2 %collective-permute-start.5 = (bf16[208,256]{1,0:T(8,128)(2,1)}, bf16[208,256]{1,0:T(8,128)(2,1)S(1)}, u32[]{:S(2)}, u32[]{:S(2)}) collective-permute-start(bf16[208,256]{1,0:T(8,128)(2,1)} %get-tuple-element.145.refs_0_), channel_id=1, source_target_pairs={{0,16},{1,17},{2,18},{3,19},{4,20},{5,21},{6,22},{7,23},{8,24},{9,... | collective-permute-start | bytes 319496 | tf_op jit(solution)/shard_map/ppermute | solution.py:80
  12.1 9.2 %collective-permute-start.4 = (bf16[208,256]{1,0:T(8,128)(2,1)}, bf16[208,256]{1,0:T(8,128)(2,1)S(1)}, u32[]{:S(2)}, u32[]{:S(2)}) collective-permute-start(bf16[208,256]{1,0:T(8,128)(2,1)} %get-tuple-element.145.refs_0_), channel_id=1, source_target_pairs={{0,8},{1,9},{2,10},{3,11},{4,12},{5,13},{6,14},{7,15},{8,16},{9,17... | collective-permute-start | bytes 319496 | tf_op jit(solution)/shard_map/ppermute | solution.py:80
  22.2 19.0 %collective-permute-start.9 = (bf16[4,208,256]{2,1,0:T(8,128)(2,1)S(1)}, bf16[4,208,256]{2,1,0:T(8,128)(2,1)S(1)}, u32[]{:S(2)}, u32[]{:S(2)}) collective-permute-start(bf16[4,208,256]{2,1,0:T(8,128)(2,1)S(1)} %get-tuple-element.150.group), channel_id=1, source_target_pairs={{0,4},{1,3},{2,6},{3,1},{4,0},{5,7},{6,2},{7,5},{8,12},{9,11},{10,... | collective-permute-start | bytes 1277960 | tf_op jit(solution)/shard_map/ppermute | solution.py:75
  23.8 17.4 %collective-permute-start.8 = (bf16[4,208,256]{2,1,0:T(8,128)(2,1)S(1)}, bf16[4,208,256]{2,1,0:T(8,128)(2,1)S(1)}, u32[]{:S(2)}, u32[]{:S(2)}) collective-permute-start(bf16[4,208,256]{2,1,0:T(8,128)(2,1)S(1)} %get-tuple-element.150.group), channel_id=1, source_target_pairs={{0,2},{1,5},{2,0},{3,7},{4,6},{5,1},{6,4},{7,3},{8,10},{9,13},{10,... | collective-permute-start | bytes 1277960 | tf_op jit(solution)/shard_map/ppermute | solution.py:75
  25.3 7.9 %collective-permute-start.3 = (bf16[208,256]{1,0:T(8,128)(2,1)}, bf16[208,256]{1,0:T(8,128)(2,1)S(1)}, u32[]{:S(2)}, u32[]{:S(2)}) collective-permute-start(bf16[208,256]{1,0:T(8,128)(2,1)} %get-tuple-element.144.refs_0_), channel_id=1, source_target_pairs={{0,24},{1,25},{2,26},{3,27},{4,28},{5,29},{6,30},{7,31},{8,0},{9,1... | collective-permute-start | bytes 319496 | tf_op jit(solution)/shard_map/ppermute | solution.py:80
  30.6 8.6 %collective-permute-start.2 = (bf16[208,256]{1,0:T(8,128)(2,1)}, bf16[208,256]{1,0:T(8,128)(2,1)S(1)}, u32[]{:S(2)}, u32[]{:S(2)}) collective-permute-start(bf16[208,256]{1,0:T(8,128)(2,1)} %get-tuple-element.144.refs_0_), channel_id=1, source_target_pairs={{0,16},{1,17},{2,18},{3,19},{4,20},{5,21},{6,22},{7,23},{8,24},{9,... | collective-permute-start | bytes 319496 | tf_op jit(solution)/shard_map/ppermute | solution.py:80
  30.8 8.3 %collective-permute-start.1 = (bf16[208,256]{1,0:T(8,128)(2,1)}, bf16[208,256]{1,0:T(8,128)(2,1)S(1)}, u32[]{:S(2)}, u32[]{:S(2)}) collective-permute-start(bf16[208,256]{1,0:T(8,128)(2,1)} %get-tuple-element.144.refs_0_), channel_id=1, source_target_pairs={{0,8},{1,9},{2,10},{3,11},{4,12},{5,13},{6,14},{7,15},{8,16},{9,17... | collective-permute-start | bytes 319496 | tf_op jit(solution)/shard_map/ppermute | solution.py:80
  40.1 8.2 %collective-permute-start.12 = (bf16[4,208,256]{2,1,0:T(8,128)(2,1)S(1)}, bf16[4,208,256]{2,1,0:T(8,128)(2,1)S(1)}, u32[]{:S(2)}, u32[]{:S(2)}) collective-permute-start(bf16[4,208,256]{2,1,0:T(8,128)(2,1)S(1)} %get-tuple-element.156.group), channel_id=1, source_target_pairs={{0,4},{1,3},{2,6},{3,1},{4,0},{5,7},{6,2},{7,5},{8,12},{9,11},{10,... | collective-permute-start | bytes 1277960 | tf_op jit(solution)/shard_map/ppermute | solution.py:75
  40.5 12.3 %collective-permute-start.11 = (bf16[4,208,256]{2,1,0:T(8,128)(2,1)S(1)}, bf16[4,208,256]{2,1,0:T(8,128)(2,1)S(1)}, u32[]{:S(2)}, u32[]{:S(2)}) collective-permute-start(bf16[4,208,256]{2,1,0:T(8,128)(2,1)S(1)} %get-tuple-element.156.group), channel_id=1, source_target_pairs={{0,2},{1,5},{2,0},{3,7},{4,6},{5,1},{6,4},{7,3},{8,10},{9,13},{10,... | collective-permute-start | bytes 1277960 | tf_op jit(solution)/shard_map/ppermute | solution.py:75
  41.2 14.5 %collective-permute-start.13 = (bf16[4,208,256]{2,1,0:T(8,128)(2,1)S(1)}, bf16[4,208,256]{2,1,0:T(8,128)(2,1)S(1)}, u32[]{:S(2)}, u32[]{:S(2)}) collective-permute-start(bf16[4,208,256]{2,1,0:T(8,128)(2,1)S(1)} %get-tuple-element.162), channel_id=1, source_target_pairs={{0,4},{1,3},{2,6},{3,1},{4,0},{5,7},{6,2},{7,5},{8,12},{9,11},{10,... | collective-permute-start | bytes 1277960 | tf_op jit(solution)/shard_map/ppermute | solution.py:75
  44.3 10.4 %collective-permute-start.10 = (f32[8,2176]{1,0:T(8,128)S(1)}, f32[8,2176]{1,0:T(8,128)S(1)}, u32[]{:S(2)}, u32[]{:S(2)}) collective-permute-start(f32[8,2176]{1,0:T(8,128)S(1)} %get-tuple-element.155), channel_id=1, source_target_pairs={{1,2},{2,1},{3,4},{4,3},{5,6},{6,5},{7,8},{8,7},{9,10},{10,9},{11,... | collective-permute-start | bytes 208904 | tf_op jit(solution)/shard_map/ppermute | solution.py:99
  52.8 8.2 %collective-permute-start.15 = (bf16[4,208,256]{2,1,0:T(8,128)(2,1)S(1)}, bf16[4,208,256]{2,1,0:T(8,128)(2,1)S(1)}, u32[]{:S(2)}, u32[]{:S(2)}) collective-permute-start(bf16[4,208,256]{2,1,0:T(8,128)(2,1)S(1)} %get-tuple-element.169), channel_id=1, source_target_pairs={{0,4},{1,3},{2,6},{3,1},{4,0},{5,7},{6,2},{7,5},{8,12},{9,11},{10,... | collective-permute-start | bytes 1277960 | tf_op jit(solution)/shard_map/ppermute | solution.py:75
  70.7 12.8 %collective-permute-start.18 = (bf16[8,208,256]{2,1,0:T(8,128)(2,1)S(1)}, bf16[8,208,256]{2,1,0:T(8,128)(2,1)S(1)}, u32[]{:S(2)}, u32[]{:S(2)}) collective-permute-start(bf16[8,208,256]{2,1,0:T(8,128)(2,1)S(1)} %get-tuple-element.194), channel_id=1, source_target_pairs={{0,4},{1,3},{2,6},{3,1},{4,0},{5,7},{6,2},{7,5},{8,12},{9,11},{10,... | collective-permute-start | bytes 2555912 | tf_op jit(solution)/shard_map/ppermute | solution.py:75
  74.5 9.2 %collective-permute-start.23 = (bf16[16,208,256]{2,1,0:T(8,128)(2,1)S(1)}, bf16[16,208,256]{2,1,0:T(8,128)(2,1)S(1)}, u32[]{:S(2)}, u32[]{:S(2)}) collective-permute-start(bf16[16,208,256]{2,1,0:T(8,128)(2,1)S(1)} %get-tuple-element.206), channel_id=1, source_target_pairs={{0,1},{1,0},{2,3},{3,2},{4,5},{5,4},{6,7},{7,6},{8,9},{9,8},{10,11... | collective-permute-start | bytes 5111816 | tf_op jit(solution)/shard_map/ppermute | solution.py:86
  83.6 12.3 %collective-permute-start.19 = (bf16[4,208,256]{2,1,0:T(8,128)(2,1)S(1)}, bf16[4,208,256]{2,1,0:T(8,128)(2,1)S(1)}, u32[]{:S(2)}, u32[]{:S(2)}) collective-permute-start(bf16[4,208,256]{2,1,0:T(8,128)(2,1)S(1)} %get-tuple-element.196), channel_id=1, source_target_pairs={{0,2},{1,5},{2,0},{3,7},{4,6},{5,1},{6,4},{7,3},{8,10},{9,13},{10,... | collective-permute-start | bytes 1277960 | tf_op jit(solution)/shard_map/ppermute | solution.py:75
  84.4 19.0 %collective-permute-start.24 = (bf16[8,208,256]{2,1,0:T(8,128)(2,1)S(1)}, bf16[8,208,256]{2,1,0:T(8,128)(2,1)S(1)}, u32[]{:S(2)}, u32[]{:S(2)}) collective-permute-start(bf16[8,208,256]{2,1,0:T(8,128)(2,1)S(1)} %get-tuple-element.208), channel_id=1, source_target_pairs={{0,4},{1,3},{2,6},{3,1},{4,0},{5,7},{6,2},{7,5},{8,12},{9,11},{10,... | collective-permute-start | bytes 2555912 | tf_op jit(solution)/shard_map/ppermute | solution.py:75
  103.3 14.5 %collective-permute-start.22 = (f32[256,1024]{1,0:T(8,128)S(1)}, f32[256,1024]{1,0:T(8,128)S(1)}, u32[]{:S(2)}, u32[]{:S(2)}) collective-permute-start(f32[256,1024]{1,0:T(8,128)S(1)} %get-tuple-element.200), channel_id=1, source_target_pairs={{0,1},{1,0},{2,3},{3,2},{4,5},{5,4},{6,7},{7,6},{8,9},{9,8},{10,11... | collective-permute-start | bytes 3145736 | tf_op jit(solution)/shard_map/ppermute | solution.py:86
  104.0 8.1 %collective-permute-start.25 = (bf16[4,208,256]{2,1,0:T(8,128)(2,1)S(1)}, bf16[4,208,256]{2,1,0:T(8,128)(2,1)S(1)}, u32[]{:S(2)}, u32[]{:S(2)}) collective-permute-start(bf16[4,208,256]{2,1,0:T(8,128)(2,1)S(1)} %get-tuple-element.209), channel_id=1, source_target_pairs={{0,2},{1,5},{2,0},{3,7},{4,6},{5,1},{6,4},{7,3},{8,10},{9,13},{10,... | collective-permute-start | bytes 1277960 | tf_op jit(solution)/shard_map/ppermute | solution.py:75
  104.8 12.2 %collective-permute-start.30 = (bf16[208,256]{1,0:T(8,128)(2,1)S(1)}, bf16[208,256]{1,0:T(8,128)(2,1)S(1)}, u32[]{:S(2)}, u32[]{:S(2)}) collective-permute-start(bf16[208,256]{1,0:T(8,128)(2,1)S(1)} %get-tuple-element.217), channel_id=1, source_target_pairs={{0,16},{1,17},{2,18},{3,19},{4,20},{5,21},{6,22},{7,23},{8,24},{9,... | collective-permute-start | bytes 319496 | tf_op jit(solution)/shard_map/ppermute | solution.py:80
  112.4 8.1 %collective-permute-start.27 = (bf16[208,256]{1,0:T(8,128)(2,1)S(1)}, bf16[208,256]{1,0:T(8,128)(2,1)S(1)}, u32[]{:S(2)}, u32[]{:S(2)}) collective-permute-start(bf16[208,256]{1,0:T(8,128)(2,1)S(1)} %get-tuple-element.212), channel_id=1, source_target_pairs={{0,8},{1,9},{2,10},{3,11},{4,12},{5,13},{6,14},{7,15},{8,16},{9,17... | collective-permute-start | bytes 319496 | tf_op jit(solution)/shard_map/ppermute | solution.py:80
  114.1 10.2 %collective-permute-start.28 = (bf16[208,256]{1,0:T(8,128)(2,1)S(1)}, bf16[208,256]{1,0:T(8,128)(2,1)S(1)}, u32[]{:S(2)}, u32[]{:S(2)}) collective-permute-start(bf16[208,256]{1,0:T(8,128)(2,1)S(1)} %get-tuple-element.213), channel_id=1, source_target_pairs={{0,16},{1,17},{2,18},{3,19},{4,20},{5,21},{6,22},{7,23},{8,24},{9,... | collective-permute-start | bytes 319496 | tf_op jit(solution)/shard_map/ppermute | solution.py:80
  116.7 7.5 %collective-permute-start.29 = (bf16[208,256]{1,0:T(8,128)(2,1)S(1)}, bf16[208,256]{1,0:T(8,128)(2,1)S(1)}, u32[]{:S(2)}, u32[]{:S(2)}) collective-permute-start(bf16[208,256]{1,0:T(8,128)(2,1)S(1)} %get-tuple-element.214), channel_id=1, source_target_pairs={{0,24},{1,25},{2,26},{3,27},{4,28},{5,29},{6,30},{7,31},{8,0},{9,1... | collective-permute-start | bytes 319496 | tf_op jit(solution)/shard_map/ppermute | solution.py:80
  119.2 21.9 %collective-permute-start.26 = (bf16[512,256]{1,0:T(8,128)(2,1)S(1)}, bf16[512,256]{1,0:T(8,128)(2,1)S(1)}, u32[]{:S(2)}, u32[]{:S(2)}) collective-permute-start(bf16[512,256]{1,0:T(8,128)(2,1)S(1)} %shard_map.529), channel_id=1, source_target_pairs={{2,0},{4,2},{6,4},{8,6},{10,8},{12,10},{14,12},{16,14},{18,16},{20... | collective-permute-start | bytes 786440 | tf_op jit(solution)/shard_map/ppermute | solution.py:92
  (35 other events, 559.9 us)

commit v5 on v4

--- a/solution.py
+++ b/solution.py
@@ -203,10 +203,11 @@
 def along_all(pack, unread):
     far = lax.axis_size("tm") // NEAR
     got = [along_far(pack, distance) for distance in range(1, far)]
+    held, _ = call(relay_body, (struct(pack.shape, BF16), TOKEN), pack)
     return call(
         functools.partial(stack_body, far),
         (struct((far,) + pack.shape, BF16), TOKEN),
-        pack,
+        held,
         *got,
         unread=unread,
     )
@@ -359,7 +360,7 @@
     return grads + (near_got,), sent, token
 
 
-def far_terms(grads, last_got, flops=1024):
+def far_terms(grads, last_got, flops=1024, unread=()):
     far, *shape = last_got.shape
     kept, *sends, token = call(
         third_sum_body,
@@ -367,6 +368,7 @@
         *grads,
         last_got,
         flops=flops,
+        unread=unread,
     )
     return [kept] + [along_far(value, k + 1) for k, value in enumerate(sends)], token
 
@@ -612,10 +614,6 @@
     refs[-1][...] = push[...].astype(BF16)
 
 
-def input_gradient_body(g1, push, out):
-    out[...] = g1[...] + push[...].astype(F32)
-
-
 def table_gradient(cond_grad, who, mel, clips, speakers):
     lane = lax.broadcasted_iota(jnp.int32, (cond_grad.shape[0], speakers), 1)
     result = jnp.zeros((cond_grad.shape[0], speakers), F32)
@@ -645,6 +643,15 @@
     squares[...] = jnp.broadcast_to(amount, squares.shape)
 
 
+def add_body(left, right, out):
+    out[...] = left[...] + right[...]
+
+
+def spread_body(left, right, out):
+    total = left[0:1, :] + right[0:1, :]
+    out[...] = jnp.broadcast_to(total[None], out.shape)
+
+
 def adamw(weight, mean, square, gradient, scale):
     clipped = gradient * scale
     new_mean = BETA_ONE * mean + (1.0 - BETA_ONE) * clipped
@@ -659,8 +666,9 @@
     grads = refs[0:2]
     squares = refs[2]
     old = [refs[3 + 3 * kind : 6 + 3 * kind] for kind in range(6)]
-    norm = refs[21]
-    new = [refs[22 + 5 * kind : 27 + 5 * kind] for kind in range(6)]
+    part, push, norm, grad_input = refs[21:25]
+    new = [refs[25 + 5 * kind : 30 + 5 * kind] for kind in range(6)]
+    grad_input[...] = part[...] + push[...].astype(F32)
     where, total = sections(rows)
     chans = rows // 2
     grad_norm = jnp.sqrt(jnp.sum(squares[...], axis=0, keepdims=True)[:, 0:1])
@@ -876,13 +884,9 @@
 
     grads2, sent2, token = cores_summed(grad_own, grad_oth)
     now, _, lag_sum, grad_oth = backward(w1_oth, ta_oth, sb_oth, hid_oth, unread=(token,))
-    g1_part, dlag1, token, grad_own = backward(
+    g1_part, dlag1, backed, grad_own = backward(
         w1_own, ta_own, sb_own, hid_own, now, lag_sum, unread=()
     )
-    grads2, sent2, token = near_summed(grads2, sent2, LONG, (token,))
-    grads1, sent1, _ = cores_summed(grad_own, grad_oth, (token,))
-    last_got = across(sent2, 0)
-    terms2, _ = far_terms(grads2, last_got, LONG)
     kept, given = call(
         divide_body,
         (struct((own, 4 * width)),) * 2,
@@ -890,29 +894,25 @@
         skip_total,
         g1_part,
         dlag1,
-        unread=(terms2[1], terms2[-1]),
         scratch=[pltpu.VMEM((own, full), F32)],
     )
     mixed, skip_total, grad_input, push, token = call(
         finish_body, (struct((held_rows, width)),) * 4 + (TOKEN,), kept, swap_cores(given)
     )
+    grads2, sent2, summed = near_summed(grads2, sent2, LONG, (backed,))
+    grads1, sent1, _ = cores_summed(grad_own, grad_oth, (summed, token))
+    last_got = across(sent2, 0)
+    terms2, _ = far_terms(grads2, last_got, LONG)
     grads1, sent1, _ = near_summed(grads1, sent1, unread=(terms2[1], terms2[-1]))
-    terms1, token = far_terms(grads1, across(sent1, 0))
-    push = call(push_body, struct((held_rows, width), BF16), push, unread=(token,))
-    grad_input = call(
-        input_gradient_body,
-        struct((held_rows, width)),
-        grad_input,
-        shifted(push, "tm", -hop),
-    )
-
+    terms1, _ = far_terms(grads1, across(sent1, 0), unread=tuple(terms2[1:]))
     sum2, squares2 = totals(terms2)
-    sum1, squares1 = totals(terms1)
-    squares = squares1[:1] + squares2[:1]
-    squares = squares + swap_cores(squares)
-    sent = jnp.broadcast_to(squares[None], (parts, 1, LANES))
+    push = call(push_body, struct((held_rows, width), BF16), push)
+    push = shifted(push, "tm", -hop)
+    sum1, squares1 = totals(terms1, (push,))
+    squares = call(add_body, TOKEN, squares1, squares2)
+    sent = call(spread_body, struct((parts, 1, LANES)), squares, swap_cores(squares))
     squares = lax.all_to_all(sent, "tm", split_axis=0, concat_axis=0, tiled=True)
-    outs = [struct((1, 1))]
+    outs = [struct((1, 1)), struct((held_rows, width))]
     for view in views[0::3]:
         outs += [struct(view.shape)] * 4 + [struct(view.shape, BF16)]
     updated = call(
@@ -922,16 +922,18 @@
         sum2,
         squares.reshape(parts, LANES),
         *views,
+        grad_input,
+        push,
         scalars=(speaker_ids,),
     )
-    grad_norm = updated[0].reshape(())
+    grad_norm, grad_input = updated[0].reshape(()), updated[1]
     backs = (
         [lambda v: dilated_back(v, dil_shape), lambda v: v]
         + [lambda v: v.transpose(0, 3, 1, 2)] * 2
         + [lambda v: v.transpose(0, 2, 1)] * 2
     )
     new = [
-        [back(v) for v in updated[1 + 5 * kind : 6 + 5 * kind]] for kind, back in enumerate(backs)
+        [back(v) for v in updated[2 + 5 * kind : 7 + 5 * kind]] for kind, back in enumerate(backs)
     ]
     return (
         mixed,

time: 142 us -> 145 us (1.021)
  starting transfers between devices: 40.7 us -> 46.9 us
  waiting for transfers between devices: 61.9 us -> 58.6 us
    ppermute x10, waiting for transfers between devices: 32.2 us -> 22.5 us  [across(): return lax.ppermute(value, BOTH, route(lambda i, c: i ^ 1 + (c ^ bit)))]
    ppermute x12, waiting for transfers between devices: 21 us -> 27.4 us  [along_far(): lax.ppermute(value, BOTH, route(lambda i, c: (i // NEAR + distance) % far...]
    ppermute x12, starting transfers between devices: 21.6 us -> 27.1 us  [along_far(): lax.ppermute(value, BOTH, route(lambda i, c: (i // NEAR + distance) % far...]
    pallas_call x30 -> x33, Pallas kernels: 23.6 us -> 24.6 us  [call(): pl.pallas_call(body, out_shape=out_shape, in_specs=specs, scratch_shapes=...]
  transfers between devices with their start and end apart: 32 -> 32, of which waited for: 17 -> 17; matrix products, arithmetic and copies ran while one was open for 0% -> 0% of each run, Pallas kernels for 12% -> 11%
where the time goes in v5:
time: 145 us; the launch traced here: 144 us
  waiting for transfers between devices  58.6 us (40%)
  starting transfers between devices  46.9 us (32%)
  Pallas kernels  24.6 us (17%)
  blocking collectives  11.1 us (8%)
  local copies, waits for them, and re-layouts  2.01 us (1%)
    ppermute x12, waiting for transfers between devices, along_far(): lax.ppermute(value, BOTH, route(lambda i, c: (i // NEAR + distance) % far...  27.4 us
    ppermute x12, starting transfers between devices, along_far(): lax.ppermute(value, BOTH, route(lambda i, c: (i // NEAR + distance) % far...  27.1 us
    pallas_call x33, Pallas kernels, call(): pl.pallas_call(body, out_shape=out_shape, in_specs=specs, scratch_shapes=...  24.6 us
    ppermute x10, waiting for transfers between devices, across(): return lax.ppermute(value, BOTH, route(lambda i, c: i ^ 1 + (c ^ bit)))  22.5 us
    ppermute x10, starting transfers between devices, across(): return lax.ppermute(value, BOTH, route(lambda i, c: i ^ 1 + (c ^ bit)))  11.9 us
    all_to_all x1, blocking collectives, on_device(): lax.all_to_all(sent, 'tm', split_axis=0, concat_axis=0, tiled=True)  11.1 us
    ppermute x7, waiting for transfers between devices, swap_cores(): return lax.ppermute(value, 'mp', [(0, 1), (1, 0)])  8.77 us
    ppermute x2, starting transfers between devices, shifted(): return lax.ppermute(value, axis, pairs)  6.15 us
  transfers between devices with their start and end apart: 32, of which 17 were waited for; matrix products, arithmetic and copies ran while one was open for 0% of the time, Pallas kernels for 11%

profile of v5, /device:TPU:0, one launch (start us, length us, event | category | flops | bytes accessed | tf_op | source)
XLA Modules:
  0.0 144.5 jit_solution(12762022414567696564)
XLA Ops:
  0.7 2.9 %shard_map.504 = (bf16[208,256]{1,0:T(8,128)(2,1)}, bf16[208,256]{1,0:T(8,128)(2,1)}, bf16[512,256]{1,0:T(8,128)(2,1)}) custom-call(s32[8]{0:T(128)} %who.7, f32[512,128]{1,0:T(8,128)} %bitcast.75, f32[2,32,256]{2,1,0:T(8,128)} %bitcast.79, f32[2,32,256]{2,1,0:T(8,128)} %bitcast.81, f32[2,2,16,80]{3,2,1,0:T(8,128)} %bitcast.83, f32[2,2,16,109]{3,2,1,0:T(8,128)} %bitcast.85, ...), custom_call_target="tpu_custom_call" | custom-call | flops 1024 | bytes 1024 | tf_op jit(solution)/shard_map/pallas_call | solution.py:38
  3.6 4.9 %collective-permute-start = (bf16[512,256]{1,0:T(8,128)(2,1)}, bf16[512,256]{1,0:T(8,128)(2,1)S(1)}, u32[]{:S(2)}, u32[]{:S(2)}) collective-permute-start(bf16[512,256]{1,0:T(8,128)(2,1)} %get-tuple-element.146), channel_id=1, source_target_pairs={{0,2},{2,4},{4,6},{6,8},{8,10},{10,12},{12,14},{14,16},{16,18},{18... | collective-permute-start | bytes 786440 | tf_op jit(solution)/shard_map/ppermute | solution.py:92
  8.5 3.6 %collective-permute-start.6 = (bf16[208,256]{1,0:T(8,128)(2,1)}, bf16[208,256]{1,0:T(8,128)(2,1)S(1)}, u32[]{:S(2)}, u32[]{:S(2)}) collective-permute-start(bf16[208,256]{1,0:T(8,128)(2,1)} %get-tuple-element.149.value), channel_id=1, source_target_pairs={{0,24},{1,25},{2,26},{3,27},{4,28},{5,29},{6,30},{7,31},{8,0},{9,1... | collective-permute-start | bytes 319496 | tf_op jit(solution)/shard_map/ppermute | solution.py:80
  15.8 5.4 %collective-permute-done.5.refs_2_ = bf16[208,256]{1,0:T(8,128)(2,1)S(1)} collective-permute-done((bf16[208,256]{1,0:T(8,128)(2,1)}, bf16[208,256]{1,0:T(8,128)(2,1)S(1)}, u32[]{:S(2)}, u32[]{:S(2)}) %collective-permute-start.5) | collective-permute-done | bytes 106528 | tf_op jit(solution)/shard_map/ppermute | solution.py:80
  24.4 5.3 %collective-permute-start.3 = (bf16[208,256]{1,0:T(8,128)(2,1)}, bf16[208,256]{1,0:T(8,128)(2,1)S(1)}, u32[]{:S(2)}, u32[]{:S(2)}) collective-permute-start(bf16[208,256]{1,0:T(8,128)(2,1)} %get-tuple-element.147.value), channel_id=1, source_target_pairs={{0,24},{1,25},{2,26},{3,27},{4,28},{5,29},{6,30},{7,31},{8,0},{9,1... | collective-permute-start | bytes 319496 | tf_op jit(solution)/shard_map/ppermute | solution.py:80
  29.9 2.0 %collective-permute-start.1 = (bf16[208,256]{1,0:T(8,128)(2,1)}, bf16[208,256]{1,0:T(8,128)(2,1)S(1)}, u32[]{:S(2)}, u32[]{:S(2)}) collective-permute-start(bf16[208,256]{1,0:T(8,128)(2,1)} %get-tuple-element.147.value), channel_id=1, source_target_pairs={{0,8},{1,9},{2,10},{3,11},{4,12},{5,13},{6,14},{7,15},{8,16},{9,17... | collective-permute-start | bytes 319496 | tf_op jit(solution)/shard_map/ppermute | solution.py:80
  33.5 4.8 %collective-permute-done.2.refs_2_ = bf16[208,256]{1,0:T(8,128)(2,1)S(1)} collective-permute-done((bf16[208,256]{1,0:T(8,128)(2,1)}, bf16[208,256]{1,0:T(8,128)(2,1)S(1)}, u32[]{:S(2)}, u32[]{:S(2)}) %collective-permute-start.2) | collective-permute-done | bytes 106528 | tf_op jit(solution)/shard_map/ppermute | solution.py:80
  43.2 3.4 %collective-permute-done.12.refs_0_.second = bf16[4,208,256]{2,1,0:T(8,128)(2,1)S(1)} collective-permute-done((bf16[4,208,256]{2,1,0:T(8,128)(2,1)S(1)}, bf16[4,208,256]{2,1,0:T(8,128)(2,1)S(1)}, u32[]{:S(2)}, u32[]{:S(2)}) %collective-permute-start.12) | collective-permute-done | bytes 426016 | tf_op jit(solution)/shard_map/ppermute | solution.py:75
  46.5 4.5 %collective-permute-done.11.value.first = bf16[4,208,256]{2,1,0:T(8,128)(2,1)S(1)} collective-permute-done((bf16[4,208,256]{2,1,0:T(8,128)(2,1)S(1)}, bf16[4,208,256]{2,1,0:T(8,128)(2,1)S(1)}, u32[]{:S(2)}, u32[]{:S(2)}) %collective-permute-start.11) | collective-permute-done | bytes 426016 | tf_op jit(solution)/shard_map/ppermute | solution.py:75
  55.5 2.3 %collective-permute-done.14.weights = bf16[16,208,256]{2,1,0:T(8,128)(2,1)S(1)} collective-permute-done((bf16[16,208,256]{2,1,0:T(8,128)(2,1)S(1)}, bf16[16,208,256]{2,1,0:T(8,128)(2,1)S(1)}, u32[]{:S(2)}, u32[]{:S(2)}) %collective-permute-start.14) | collective-permute-done | bytes 1703968 | tf_op jit(solution)/shard_map/ppermute | solution.py:86
  59.5 3.6 %collective-permute-done.16.weights = bf16[16,208,256]{2,1,0:T(8,128)(2,1)S(1)} collective-permute-done((bf16[16,208,256]{2,1,0:T(8,128)(2,1)S(1)}, bf16[16,208,256]{2,1,0:T(8,128)(2,1)S(1)}, u32[]{:S(2)}, u32[]{:S(2)}) %collective-permute-start.16) | collective-permute-done | bytes 1703968 | tf_op jit(solution)/shard_map/ppermute | solution.py:86
  63.1 2.1 %shard_map.518 = (f32[256,512]{1,0:T(8,128)S(1)}, f32[256,512]{1,0:T(8,128)S(1)}, f32[256,512]{1,0:T(8,128)S(1)}, f32[272,512]{1,0:T(8,128)S(1)}, bf16[16,208,256]{2,1,0:T(8,128)(2,1)S(1)}) custom-call(f32[272,512]{1,0:T(8,128)S(1)} %get-tuple-element.170.u2, f32[256,512]{1,0:T(8,128)S(1)} %get-tuple-element.171.s1, ...), custom_call_target="tpu_custom_call" | custom-call | flops 1024 | bytes 1024 | tf_op jit(solution)/shard_map/pallas_call | solution.py:38
  65.9 2.0 %shard_map.520 = (f32[256,512]{1,0:T(8,128)S(1)}, f32[256,512]{1,0:T(8,128)S(1)}, f32[256,512]{1,0:T(8,128)S(1)}, f32[8,128]{1,0:T(8,128)}, bf16[16,208,256]{2,1,0:T(8,128)(2,1)S(1)}) custom-call(f32[272,512]{1,0:T(8,128)S(1)} %get-tuple-element.170.u2, f32[256,512]{1,0:T(8,128)S(1)} %get-tuple-element.171.s1, bf16[272,128]{1,0:T(8,128)(2,1)S(1)} %get-tuple-element.165.cond, ...), custom_call_target="tpu_custom_call" | custom-call | flops 1024 | bytes 1024 | tf_op jit(solution)/shard_map/pallas_call | solution.py:38
  70.7 1.9 %shard_map.522 = (f32[256,512]{1,0:T(8,128)S(1)}, f32[8,128]{1,0:T(8,128)}, f32[256,512]{1,0:T(8,128)S(1)}, bf16[16,208,256]{2,1,0:T(8,128)(2,1)S(1)}) custom-call(f32[256,512]{1,0:T(8,128)S(1)} %get-tuple-element.184.g2, f32[272,512]{1,0:T(8,128)S(1)} %get-tuple-element.163.x, bf16[256,512]{1,0:T(8,128)(2,1)S(1)} %get-tuple-element.185.lag, ...), custom_call_target="tpu_custom_call" | custom-call | flops 1024 | bytes 1024 | tf_op jit(solution)/shard_map/pallas_call | solution.py:38
  75.0 6.7 %collective-permute-done.20.near_got = bf16[8,208,256]{2,1,0:T(8,128)(2,1)S(1)} collective-permute-done((bf16[8,208,256]{2,1,0:T(8,128)(2,1)S(1)}, bf16[8,208,256]{2,1,0:T(8,128)(2,1)S(1)}, u32[]{:S(2)}, u32[]{:S(2)}) %collective-permute-start.20) | collective-permute-done | bytes 852000 | tf_op jit(solution)/shard_map/ppermute | solution.py:75
  85.5 7.4 %collective-permute-done.22.last_got = bf16[4,208,256]{2,1,0:T(8,128)(2,1)S(1)} collective-permute-done((bf16[4,208,256]{2,1,0:T(8,128)(2,1)S(1)}, bf16[4,208,256]{2,1,0:T(8,128)(2,1)S(1)}, u32[]{:S(2)}, u32[]{:S(2)}) %collective-permute-start.22) | collective-permute-done | bytes 426016 | tf_op jit(solution)/shard_map/ppermute | solution.py:75
  93.7 3.5 %collective-permute-start.24 = (bf16[208,256]{1,0:T(8,128)(2,1)S(1)}, bf16[208,256]{1,0:T(8,128)(2,1)S(1)}, u32[]{:S(2)}, u32[]{:S(2)}) collective-permute-start(bf16[208,256]{1,0:T(8,128)(2,1)S(1)} %get-tuple-element.212), channel_id=1, source_target_pairs={{0,24},{1,25},{2,26},{3,27},{4,28},{5,29},{6,30},{7,31},{8,0},{9,1... | collective-permute-start | bytes 319496 | tf_op jit(solution)/shard_map/ppermute | solution.py:80
  97.3 2.8 %collective-permute-done.23.refs_0_.refs_1_ = bf16[208,256]{1,0:T(8,128)(2,1)S(1)} collective-permute-done((bf16[208,256]{1,0:T(8,128)(2,1)S(1)}, bf16[208,256]{1,0:T(8,128)(2,1)S(1)}, u32[]{:S(2)}, u32[]{:S(2)}) %collective-permute-start.23) | collective-permute-done | bytes 106528 | tf_op jit(solution)/shard_map/ppermute | solution.py:80
  103.0 7.2 %collective-permute-start.26 = (bf16[208,256]{1,0:T(8,128)(2,1)S(1)}, bf16[208,256]{1,0:T(8,128)(2,1)S(1)}, u32[]{:S(2)}, u32[]{:S(2)}) collective-permute-start(bf16[208,256]{1,0:T(8,128)(2,1)S(1)} %get-tuple-element.214), channel_id=1, source_target_pairs={{0,16},{1,17},{2,18},{3,19},{4,20},{5,21},{6,22},{7,23},{8,24},{9,... | collective-permute-start | bytes 319496 | tf_op jit(solution)/shard_map/ppermute | solution.py:80
  110.2 10.0 %collective-permute-done.26.refs_1_.refs_2_ = bf16[208,256]{1,0:T(8,128)(2,1)S(1)} collective-permute-done((bf16[208,256]{1,0:T(8,128)(2,1)S(1)}, bf16[208,256]{1,0:T(8,128)(2,1)S(1)}, u32[]{:S(2)}, u32[]{:S(2)}) %collective-permute-start.26) | collective-permute-done | bytes 106528 | tf_op jit(solution)/shard_map/ppermute | solution.py:80
  120.8 3.8 %collective-permute-start.29 = (bf16[208,256]{1,0:T(8,128)(2,1)S(1)}, bf16[208,256]{1,0:T(8,128)(2,1)S(1)}, u32[]{:S(2)}, u32[]{:S(2)}) collective-permute-start(bf16[208,256]{1,0:T(8,128)(2,1)S(1)} %get-tuple-element.218), channel_id=1, source_target_pairs={{0,24},{1,25},{2,26},{3,27},{4,28},{5,29},{6,30},{7,31},{8,0},{9,1... | collective-permute-start | bytes 319496 | tf_op jit(solution)/shard_map/ppermute | solution.py:80
  125.5 2.0 %collective-permute-done.27.refs_1_ = bf16[208,256]{1,0:T(8,128)(2,1)S(1)} collective-permute-done((bf16[208,256]{1,0:T(8,128)(2,1)S(1)}, bf16[208,256]{1,0:T(8,128)(2,1)S(1)}, u32[]{:S(2)}, u32[]{:S(2)}) %collective-permute-start.27) | collective-permute-done | bytes 106528 | tf_op jit(solution)/shard_map/ppermute | solution.py:80
  130.8 11.1 %all_to_all.5 = f32[16,1,128]{2,1,0:T(1,128)S(1)} all-to-all(f32[16,1,128]{2,1,0:T(1,128)S(1)} %shard_map.535), channel_id=1, replica_groups=mesh['tm'=16,'mp'=2] {'tm'}, dimensions={0} | all-to-all | bytes 16384 | tf_op jit(solution)/shard_map/all_to_all | solution.py:914
  142.0 2.4 %shard_map.536 = (f32[1,1]{1,0:T(1,128)}, f32[512,256]{1,0:T(8,128)}, f32[512,128]{1,0:T(8,128)}, f32[512,128]{1,0:T(8,128)}, f32[512,128]{1,0:T(8,128)}, /*inde...) custom-call(s32[8]{0:T(128)S(1)} %copy-done.21, ...), custom_call_target="tpu_custom_call" | custom-call | flops 1024 | bytes 1024 | tf_op jit(solution)/shard_map/pallas_call | solution.py:38
  (128 shorter events, 37.5 us)
Async XLA Ops:
  3.6 17.7 %collective-permute-start = (bf16[512,256]{1,0:T(8,128)(2,1)}, bf16[512,256]{1,0:T(8,128)(2,1)S(1)}, u32[]{:S(2)}, u32[]{:S(2)}) collective-permute-start(bf16[512,256]{1,0:T(8,128)(2,1)} %get-tuple-element.146), channel_id=1, source_target_pairs={{0,2},{2,4},{4,6},{6,8},{8,10},{10,12},{12,14},{14,16},{16,18},{18... | collective-permute-start | bytes 786440 | tf_op jit(solution)/shard_map/ppermute | solution.py:92
  8.5 7.4 %collective-permute-start.6 = (bf16[208,256]{1,0:T(8,128)(2,1)}, bf16[208,256]{1,0:T(8,128)(2,1)S(1)}, u32[]{:S(2)}, u32[]{:S(2)}) collective-permute-start(bf16[208,256]{1,0:T(8,128)(2,1)} %get-tuple-element.149.value), channel_id=1, source_target_pairs={{0,24},{1,25},{2,26},{3,27},{4,28},{5,29},{6,30},{7,31},{8,0},{9,1... | collective-permute-start | bytes 319496 | tf_op jit(solution)/shard_map/ppermute | solution.py:80
  12.1 9.2 %collective-permute-start.5 = (bf16[208,256]{1,0:T(8,128)(2,1)}, bf16[208,256]{1,0:T(8,128)(2,1)S(1)}, u32[]{:S(2)}, u32[]{:S(2)}) collective-permute-start(bf16[208,256]{1,0:T(8,128)(2,1)} %get-tuple-element.149.value), channel_id=1, source_target_pairs={{0,16},{1,17},{2,18},{3,19},{4,20},{5,21},{6,22},{7,23},{8,24},{9,... | collective-permute-start | bytes 319496 | tf_op jit(solution)/shard_map/ppermute | solution.py:80
  12.1 9.2 %collective-permute-start.4 = (bf16[208,256]{1,0:T(8,128)(2,1)}, bf16[208,256]{1,0:T(8,128)(2,1)S(1)}, u32[]{:S(2)}, u32[]{:S(2)}) collective-permute-start(bf16[208,256]{1,0:T(8,128)(2,1)} %get-tuple-element.149.value), channel_id=1, source_target_pairs={{0,8},{1,9},{2,10},{3,11},{4,12},{5,13},{6,14},{7,15},{8,16},{9,17... | collective-permute-start | bytes 319496 | tf_op jit(solution)/shard_map/ppermute | solution.py:80
  21.3 18.1 %collective-permute-start.9 = (bf16[4,208,256]{2,1,0:T(8,128)(2,1)S(1)}, bf16[4,208,256]{2,1,0:T(8,128)(2,1)S(1)}, u32[]{:S(2)}, u32[]{:S(2)}) collective-permute-start(bf16[4,208,256]{2,1,0:T(8,128)(2,1)S(1)} %get-tuple-element.155.group), channel_id=1, source_target_pairs={{0,4},{1,3},{2,6},{3,1},{4,0},{5,7},{6,2},{7,5},{8,12},{9,11},{10,... | collective-permute-start | bytes 1277960 | tf_op jit(solution)/shard_map/ppermute | solution.py:75
  22.9 16.5 %collective-permute-start.8 = (bf16[4,208,256]{2,1,0:T(8,128)(2,1)S(1)}, bf16[4,208,256]{2,1,0:T(8,128)(2,1)S(1)}, u32[]{:S(2)}, u32[]{:S(2)}) collective-permute-start(bf16[4,208,256]{2,1,0:T(8,128)(2,1)S(1)} %get-tuple-element.155.group), channel_id=1, source_target_pairs={{0,2},{1,5},{2,0},{3,7},{4,6},{5,1},{6,4},{7,3},{8,10},{9,13},{10,... | collective-permute-start | bytes 1277960 | tf_op jit(solution)/shard_map/ppermute | solution.py:75
  24.4 9.1 %collective-permute-start.3 = (bf16[208,256]{1,0:T(8,128)(2,1)}, bf16[208,256]{1,0:T(8,128)(2,1)S(1)}, u32[]{:S(2)}, u32[]{:S(2)}) collective-permute-start(bf16[208,256]{1,0:T(8,128)(2,1)} %get-tuple-element.147.value), channel_id=1, source_target_pairs={{0,24},{1,25},{2,26},{3,27},{4,28},{5,29},{6,30},{7,31},{8,0},{9,1... | collective-permute-start | bytes 319496 | tf_op jit(solution)/shard_map/ppermute | solution.py:80
  29.7 8.6 %collective-permute-start.2 = (bf16[208,256]{1,0:T(8,128)(2,1)}, bf16[208,256]{1,0:T(8,128)(2,1)S(1)}, u32[]{:S(2)}, u32[]{:S(2)}) collective-permute-start(bf16[208,256]{1,0:T(8,128)(2,1)} %get-tuple-element.147.value), channel_id=1, source_target_pairs={{0,16},{1,17},{2,18},{3,19},{4,20},{5,21},{6,22},{7,23},{8,24},{9,... | collective-permute-start | bytes 319496 | tf_op jit(solution)/shard_map/ppermute | solution.py:80
  29.9 8.3 %collective-permute-start.1 = (bf16[208,256]{1,0:T(8,128)(2,1)}, bf16[208,256]{1,0:T(8,128)(2,1)S(1)}, u32[]{:S(2)}, u32[]{:S(2)}) collective-permute-start(bf16[208,256]{1,0:T(8,128)(2,1)} %get-tuple-element.147.value), channel_id=1, source_target_pairs={{0,8},{1,9},{2,10},{3,11},{4,12},{5,13},{6,14},{7,15},{8,16},{9,17... | collective-permute-start | bytes 319496 | tf_op jit(solution)/shard_map/ppermute | solution.py:80
  38.3 8.2 %collective-permute-start.12 = (bf16[4,208,256]{2,1,0:T(8,128)(2,1)S(1)}, bf16[4,208,256]{2,1,0:T(8,128)(2,1)S(1)}, u32[]{:S(2)}, u32[]{:S(2)}) collective-permute-start(bf16[4,208,256]{2,1,0:T(8,128)(2,1)S(1)} %get-tuple-element.161.group), channel_id=1, source_target_pairs={{0,4},{1,3},{2,6},{3,1},{4,0},{5,7},{6,2},{7,5},{8,12},{9,11},{10,... | collective-permute-start | bytes 1277960 | tf_op jit(solution)/shard_map/ppermute | solution.py:75
  38.7 12.3 %collective-permute-start.11 = (bf16[4,208,256]{2,1,0:T(8,128)(2,1)S(1)}, bf16[4,208,256]{2,1,0:T(8,128)(2,1)S(1)}, u32[]{:S(2)}, u32[]{:S(2)}) collective-permute-start(bf16[4,208,256]{2,1,0:T(8,128)(2,1)S(1)} %get-tuple-element.161.group), channel_id=1, source_target_pairs={{0,2},{1,5},{2,0},{3,7},{4,6},{5,1},{6,4},{7,3},{8,10},{9,13},{10,... | collective-permute-start | bytes 1277960 | tf_op jit(solution)/shard_map/ppermute | solution.py:75
  39.4 14.5 %collective-permute-start.13 = (bf16[4,208,256]{2,1,0:T(8,128)(2,1)S(1)}, bf16[4,208,256]{2,1,0:T(8,128)(2,1)S(1)}, u32[]{:S(2)}, u32[]{:S(2)}) collective-permute-start(bf16[4,208,256]{2,1,0:T(8,128)(2,1)S(1)} %get-tuple-element.167), channel_id=1, source_target_pairs={{0,4},{1,3},{2,6},{3,1},{4,0},{5,7},{6,2},{7,5},{8,12},{9,11},{10,... | collective-permute-start | bytes 1277960 | tf_op jit(solution)/shard_map/ppermute | solution.py:75
  42.5 10.4 %collective-permute-start.10 = (f32[8,2176]{1,0:T(8,128)S(1)}, f32[8,2176]{1,0:T(8,128)S(1)}, u32[]{:S(2)}, u32[]{:S(2)}) collective-permute-start(f32[8,2176]{1,0:T(8,128)S(1)} %get-tuple-element.160), channel_id=1, source_target_pairs={{1,2},{2,1},{3,4},{4,3},{5,6},{6,5},{7,8},{8,7},{9,10},{10,9},{11,... | collective-permute-start | bytes 208904 | tf_op jit(solution)/shard_map/ppermute | solution.py:99
  51.0 8.2 %collective-permute-start.15 = (bf16[4,208,256]{2,1,0:T(8,128)(2,1)S(1)}, bf16[4,208,256]{2,1,0:T(8,128)(2,1)S(1)}, u32[]{:S(2)}, u32[]{:S(2)}) collective-permute-start(bf16[4,208,256]{2,1,0:T(8,128)(2,1)S(1)} %get-tuple-element.174), channel_id=1, source_target_pairs={{0,4},{1,3},{2,6},{3,1},{4,0},{5,7},{6,2},{7,5},{8,12},{9,11},{10,... | collective-permute-start | bytes 1277960 | tf_op jit(solution)/shard_map/ppermute | solution.py:75
  68.9 12.8 %collective-permute-start.20 = (bf16[8,208,256]{2,1,0:T(8,128)(2,1)S(1)}, bf16[8,208,256]{2,1,0:T(8,128)(2,1)S(1)}, u32[]{:S(2)}, u32[]{:S(2)}) collective-permute-start(bf16[8,208,256]{2,1,0:T(8,128)(2,1)S(1)} %get-tuple-element.205), channel_id=1, source_target_pairs={{0,4},{1,3},{2,6},{3,1},{4,0},{5,7},{6,2},{7,5},{8,12},{9,11},{10,... | collective-permute-start | bytes 2555912 | tf_op jit(solution)/shard_map/ppermute | solution.py:75
  74.4 7.5 %collective-permute-start.18 = (f32[256,1024]{1,0:T(8,128)S(1)}, f32[256,1024]{1,0:T(8,128)S(1)}, u32[]{:S(2)}, u32[]{:S(2)}) collective-permute-start(f32[256,1024]{1,0:T(8,128)S(1)} %get-tuple-element.200), channel_id=1, source_target_pairs={{0,1},{1,0},{2,3},{3,2},{4,5},{5,4},{6,7},{7,6},{8,9},{9,8},{10,11... | collective-permute-start | bytes 3145736 | tf_op jit(solution)/shard_map/ppermute | solution.py:86
  74.5 8.6 %collective-permute-start.19 = (bf16[16,208,256]{2,1,0:T(8,128)(2,1)S(1)}, bf16[16,208,256]{2,1,0:T(8,128)(2,1)S(1)}, u32[]{:S(2)}, u32[]{:S(2)}) collective-permute-start(bf16[16,208,256]{2,1,0:T(8,128)(2,1)S(1)} %get-tuple-element.204), channel_id=1, source_target_pairs={{0,1},{1,0},{2,3},{3,2},{4,5},{5,4},{6,7},{7,6},{8,9},{9,8},{10,11... | collective-permute-start | bytes 5111816 | tf_op jit(solution)/shard_map/ppermute | solution.py:86
  81.8 11.1 %collective-permute-start.22 = (bf16[4,208,256]{2,1,0:T(8,128)(2,1)S(1)}, bf16[4,208,256]{2,1,0:T(8,128)(2,1)S(1)}, u32[]{:S(2)}, u32[]{:S(2)}) collective-permute-start(bf16[4,208,256]{2,1,0:T(8,128)(2,1)S(1)} %get-tuple-element.210), channel_id=1, source_target_pairs={{0,2},{1,5},{2,0},{3,7},{4,6},{5,1},{6,4},{7,3},{8,10},{9,13},{10,... | collective-permute-start | bytes 1277960 | tf_op jit(solution)/shard_map/ppermute | solution.py:75
  83.7 16.3 %collective-permute-start.21 = (bf16[8,208,256]{2,1,0:T(8,128)(2,1)S(1)}, bf16[8,208,256]{2,1,0:T(8,128)(2,1)S(1)}, u32[]{:S(2)}, u32[]{:S(2)}) collective-permute-start(bf16[8,208,256]{2,1,0:T(8,128)(2,1)S(1)} %get-tuple-element.209), channel_id=1, source_target_pairs={{0,4},{1,3},{2,6},{3,1},{4,0},{5,7},{6,2},{7,5},{8,12},{9,11},{10,... | collective-permute-start | bytes 2555912 | tf_op jit(solution)/shard_map/ppermute | solution.py:75
  100.7 19.5 %collective-permute-start.25 = (bf16[4,208,256]{2,1,0:T(8,128)(2,1)S(1)}, bf16[4,208,256]{2,1,0:T(8,128)(2,1)S(1)}, u32[]{:S(2)}, u32[]{:S(2)}) collective-permute-start(bf16[4,208,256]{2,1,0:T(8,128)(2,1)S(1)} %get-tuple-element.213), channel_id=1, source_target_pairs={{0,2},{1,5},{2,0},{3,7},{4,6},{5,1},{6,4},{7,3},{8,10},{9,13},{10,... | collective-permute-start | bytes 1277960 | tf_op jit(solution)/shard_map/ppermute | solution.py:75
  101.5 24.0 %collective-permute-start.30 = (bf16[512,256]{1,0:T(8,128)(2,1)S(1)}, bf16[512,256]{1,0:T(8,128)(2,1)S(1)}, u32[]{:S(2)}, u32[]{:S(2)}) collective-permute-start(bf16[512,256]{1,0:T(8,128)(2,1)S(1)} %shard_map.531), channel_id=1, source_target_pairs={{2,0},{4,2},{6,4},{8,6},{10,8},{12,10},{14,12},{16,14},{18,16},{20... | collective-permute-start | bytes 786440 | tf_op jit(solution)/shard_map/ppermute | solution.py:92
  103.0 17.2 %collective-permute-start.26 = (bf16[208,256]{1,0:T(8,128)(2,1)S(1)}, bf16[208,256]{1,0:T(8,128)(2,1)S(1)}, u32[]{:S(2)}, u32[]{:S(2)}) collective-permute-start(bf16[208,256]{1,0:T(8,128)(2,1)S(1)} %get-tuple-element.214), channel_id=1, source_target_pairs={{0,16},{1,17},{2,18},{3,19},{4,20},{5,21},{6,22},{7,23},{8,24},{9,... | collective-permute-start | bytes 319496 | tf_op jit(solution)/shard_map/ppermute | solution.py:80
  120.8 7.9 %collective-permute-start.28 = (bf16[208,256]{1,0:T(8,128)(2,1)S(1)}, bf16[208,256]{1,0:T(8,128)(2,1)S(1)}, u32[]{:S(2)}, u32[]{:S(2)}) collective-permute-start(bf16[208,256]{1,0:T(8,128)(2,1)S(1)} %get-tuple-element.217), channel_id=1, source_target_pairs={{0,16},{1,17},{2,18},{3,19},{4,20},{5,21},{6,22},{7,23},{8,24},{9,... | collective-permute-start | bytes 319496 | tf_op jit(solution)/shard_map/ppermute | solution.py:80
  120.8 7.9 %collective-permute-start.29 = (bf16[208,256]{1,0:T(8,128)(2,1)S(1)}, bf16[208,256]{1,0:T(8,128)(2,1)S(1)}, u32[]{:S(2)}, u32[]{:S(2)}) collective-permute-start(bf16[208,256]{1,0:T(8,128)(2,1)S(1)} %get-tuple-element.218), channel_id=1, source_target_pairs={{0,24},{1,25},{2,26},{3,27},{4,28},{5,29},{6,30},{7,31},{8,0},{9,1... | collective-permute-start | bytes 319496 | tf_op jit(solution)/shard_map/ppermute | solution.py:80
  (35 other events, 892.3 us)

commit v6 on v5

--- a/solution.py
+++ b/solution.py
@@ -904,7 +904,7 @@
     last_got = across(sent2, 0)
     terms2, _ = far_terms(grads2, last_got, LONG)
     grads1, sent1, _ = near_summed(grads1, sent1, unread=(terms2[1], terms2[-1]))
-    terms1, _ = far_terms(grads1, across(sent1, 0), unread=tuple(terms2[1:]))
+    terms1, _ = far_terms(grads1, across(sent1, 0))
     sum2, squares2 = totals(terms2)
     push = call(push_body, struct((held_rows, width), BF16), push)
     push = shifted(push, "tm", -hop)

time: 145 us -> 140 us (0.966)
  waiting for transfers between devices: 58.6 us -> 54.5 us
    ppermute x12, waiting for transfers between devices: 27.4 us -> 21.9 us  [along_far(): lax.ppermute(value, BOTH, route(lambda i, c: (i // NEAR + distance) % far...]
where the time goes in v6:
time: 140 us
  waiting for transfers between devices  54.5 us (39%)
  starting transfers between devices  47.2 us (34%)
  Pallas kernels  24.6 us (18%)
  blocking collectives  10.1 us (7%)
  local copies, waits for them, and re-layouts  2.01 us (1%)
    ppermute x12, starting transfers between devices, along_far(): lax.ppermute(value, BOTH, route(lambda i, c: (i // NEAR + distance) % far...  27.4 us
    pallas_call x33, Pallas kernels, call(): pl.pallas_call(body, out_shape=out_shape, in_specs=specs, scratch_shapes=...  24.6 us
    ppermute x10, waiting for transfers between devices, across(): return lax.ppermute(value, BOTH, route(lambda i, c: i ^ 1 + (c ^ bit)))  23.9 us
    ppermute x12, waiting for transfers between devices, along_far(): lax.ppermute(value, BOTH, route(lambda i, c: (i // NEAR + distance) % far...  21.9 us
    ppermute x10, starting transfers between devices, across(): return lax.ppermute(value, BOTH, route(lambda i, c: i ^ 1 + (c ^ bit)))  11.9 us
    all_to_all x1, blocking collectives, on_device(): lax.all_to_all(sent, 'tm', split_axis=0, concat_axis=0, tiled=True)  10.1 us
    ppermute x7, waiting for transfers between devices, swap_cores(): return lax.ppermute(value, 'mp', [(0, 1), (1, 0)])  8.77 us
    ppermute x2, starting transfers between devices, shifted(): return lax.ppermute(value, axis, pairs)  6.15 us
  transfers between devices with their start and end apart: 32, of which 17 were waited for; matrix products, arithmetic and copies ran while one was open for 0% of the time, Pallas kernels for 11%

profile of v6, /device:TPU:0, one launch (start us, length us, event | category | flops | bytes accessed | tf_op | source)
XLA Modules:
  0.0 139.8 jit_solution(15479856564610510905)
XLA Ops:
  0.7 2.9 %shard_map.504 = (bf16[208,256]{1,0:T(8,128)(2,1)}, bf16[208,256]{1,0:T(8,128)(2,1)}, bf16[512,256]{1,0:T(8,128)(2,1)}) custom-call(s32[8]{0:T(128)} %who.7, f32[512,128]{1,0:T(8,128)} %bitcast.75, f32[2,32,256]{2,1,0:T(8,128)} %bitcast.79, f32[2,32,256]{2,1,0:T(8,128)} %bitcast.81, f32[2,2,16,80]{3,2,1,0:T(8,128)} %bitcast.83, f32[2,2,16,109]{3,2,1,0:T(8,128)} %bitcast.85, ...), custom_call_target="tpu_custom_call" | custom-call | flops 1024 | bytes 1024 | tf_op jit(solution)/shard_map/pallas_call | solution.py:38
  3.6 4.9 %collective-permute-start = (bf16[512,256]{1,0:T(8,128)(2,1)}, bf16[512,256]{1,0:T(8,128)(2,1)S(1)}, u32[]{:S(2)}, u32[]{:S(2)}) collective-permute-start(bf16[512,256]{1,0:T(8,128)(2,1)} %get-tuple-element.146), channel_id=1, source_target_pairs={{0,2},{2,4},{4,6},{6,8},{8,10},{10,12},{12,14},{14,16},{16,18},{18... | collective-permute-start | bytes 786440 | tf_op jit(solution)/shard_map/ppermute | solution.py:92
  8.5 3.6 %collective-permute-start.6 = (bf16[208,256]{1,0:T(8,128)(2,1)}, bf16[208,256]{1,0:T(8,128)(2,1)S(1)}, u32[]{:S(2)}, u32[]{:S(2)}) collective-permute-start(bf16[208,256]{1,0:T(8,128)(2,1)} %get-tuple-element.149.value), channel_id=1, source_target_pairs={{0,24},{1,25},{2,26},{3,27},{4,28},{5,29},{6,30},{7,31},{8,0},{9,1... | collective-permute-start | bytes 319496 | tf_op jit(solution)/shard_map/ppermute | solution.py:80
  15.8 5.4 %collective-permute-done.5.refs_2_ = bf16[208,256]{1,0:T(8,128)(2,1)S(1)} collective-permute-done((bf16[208,256]{1,0:T(8,128)(2,1)}, bf16[208,256]{1,0:T(8,128)(2,1)S(1)}, u32[]{:S(2)}, u32[]{:S(2)}) %collective-permute-start.5) | collective-permute-done | bytes 106528 | tf_op jit(solution)/shard_map/ppermute | solution.py:80
  24.4 5.3 %collective-permute-start.3 = (bf16[208,256]{1,0:T(8,128)(2,1)}, bf16[208,256]{1,0:T(8,128)(2,1)S(1)}, u32[]{:S(2)}, u32[]{:S(2)}) collective-permute-start(bf16[208,256]{1,0:T(8,128)(2,1)} %get-tuple-element.147.value), channel_id=1, source_target_pairs={{0,24},{1,25},{2,26},{3,27},{4,28},{5,29},{6,30},{7,31},{8,0},{9,1... | collective-permute-start | bytes 319496 | tf_op jit(solution)/shard_map/ppermute | solution.py:80
  29.9 2.0 %collective-permute-start.1 = (bf16[208,256]{1,0:T(8,128)(2,1)}, bf16[208,256]{1,0:T(8,128)(2,1)S(1)}, u32[]{:S(2)}, u32[]{:S(2)}) collective-permute-start(bf16[208,256]{1,0:T(8,128)(2,1)} %get-tuple-element.147.value), channel_id=1, source_target_pairs={{0,8},{1,9},{2,10},{3,11},{4,12},{5,13},{6,14},{7,15},{8,16},{9,17... | collective-permute-start | bytes 319496 | tf_op jit(solution)/shard_map/ppermute | solution.py:80
  33.5 4.8 %collective-permute-done.2.refs_2_ = bf16[208,256]{1,0:T(8,128)(2,1)S(1)} collective-permute-done((bf16[208,256]{1,0:T(8,128)(2,1)}, bf16[208,256]{1,0:T(8,128)(2,1)S(1)}, u32[]{:S(2)}, u32[]{:S(2)}) %collective-permute-start.2) | collective-permute-done | bytes 106528 | tf_op jit(solution)/shard_map/ppermute | solution.py:80
  43.2 3.4 %collective-permute-done.12.refs_0_.second = bf16[4,208,256]{2,1,0:T(8,128)(2,1)S(1)} collective-permute-done((bf16[4,208,256]{2,1,0:T(8,128)(2,1)S(1)}, bf16[4,208,256]{2,1,0:T(8,128)(2,1)S(1)}, u32[]{:S(2)}, u32[]{:S(2)}) %collective-permute-start.12) | collective-permute-done | bytes 426016 | tf_op jit(solution)/shard_map/ppermute | solution.py:75
  46.5 4.5 %collective-permute-done.11.value.first = bf16[4,208,256]{2,1,0:T(8,128)(2,1)S(1)} collective-permute-done((bf16[4,208,256]{2,1,0:T(8,128)(2,1)S(1)}, bf16[4,208,256]{2,1,0:T(8,128)(2,1)S(1)}, u32[]{:S(2)}, u32[]{:S(2)}) %collective-permute-start.11) | collective-permute-done | bytes 426016 | tf_op jit(solution)/shard_map/ppermute | solution.py:75
  55.5 2.3 %collective-permute-done.14.weights = bf16[16,208,256]{2,1,0:T(8,128)(2,1)S(1)} collective-permute-done((bf16[16,208,256]{2,1,0:T(8,128)(2,1)S(1)}, bf16[16,208,256]{2,1,0:T(8,128)(2,1)S(1)}, u32[]{:S(2)}, u32[]{:S(2)}) %collective-permute-start.14) | collective-permute-done | bytes 1703968 | tf_op jit(solution)/shard_map/ppermute | solution.py:86
  59.5 3.6 %collective-permute-done.16.weights = bf16[16,208,256]{2,1,0:T(8,128)(2,1)S(1)} collective-permute-done((bf16[16,208,256]{2,1,0:T(8,128)(2,1)S(1)}, bf16[16,208,256]{2,1,0:T(8,128)(2,1)S(1)}, u32[]{:S(2)}, u32[]{:S(2)}) %collective-permute-start.16) | collective-permute-done | bytes 1703968 | tf_op jit(solution)/shard_map/ppermute | solution.py:86
  63.1 2.1 %shard_map.518 = (f32[256,512]{1,0:T(8,128)S(1)}, f32[256,512]{1,0:T(8,128)S(1)}, f32[256,512]{1,0:T(8,128)S(1)}, f32[272,512]{1,0:T(8,128)S(1)}, bf16[16,208,256]{2,1,0:T(8,128)(2,1)S(1)}) custom-call(f32[272,512]{1,0:T(8,128)S(1)} %get-tuple-element.170.u2, f32[256,512]{1,0:T(8,128)S(1)} %get-tuple-element.171.s1, ...), custom_call_target="tpu_custom_call" | custom-call | flops 1024 | bytes 1024 | tf_op jit(solution)/shard_map/pallas_call | solution.py:38
  65.9 2.0 %shard_map.520 = (f32[256,512]{1,0:T(8,128)S(1)}, f32[256,512]{1,0:T(8,128)S(1)}, f32[256,512]{1,0:T(8,128)S(1)}, f32[8,128]{1,0:T(8,128)}, bf16[16,208,256]{2,1,0:T(8,128)(2,1)S(1)}) custom-call(f32[272,512]{1,0:T(8,128)S(1)} %get-tuple-element.170.u2, f32[256,512]{1,0:T(8,128)S(1)} %get-tuple-element.171.s1, bf16[272,128]{1,0:T(8,128)(2,1)S(1)} %get-tuple-element.165.cond, ...), custom_call_target="tpu_custom_call" | custom-call | flops 1024 | bytes 1024 | tf_op jit(solution)/shard_map/pallas_call | solution.py:38
  68.9 1.8 %collective-permute-start.20 = (bf16[8,208,256]{2,1,0:T(8,128)(2,1)S(1)}, bf16[8,208,256]{2,1,0:T(8,128)(2,1)S(1)}, u32[]{:S(2)}, u32[]{:S(2)}) collective-permute-start(bf16[8,208,256]{2,1,0:T(8,128)(2,1)S(1)} %get-tuple-element.205), channel_id=1, source_target_pairs={{0,4},{1,3},{2,6},{3,1},{4,0},{5,7},{6,2},{7,5},{8,12},{9,11},{10,... | collective-permute-start | bytes 2555912 | tf_op jit(solution)/shard_map/ppermute | solution.py:75
  70.7 1.9 %shard_map.522 = (f32[256,512]{1,0:T(8,128)S(1)}, f32[8,128]{1,0:T(8,128)}, f32[256,512]{1,0:T(8,128)S(1)}, bf16[16,208,256]{2,1,0:T(8,128)(2,1)S(1)}) custom-call(f32[256,512]{1,0:T(8,128)S(1)} %get-tuple-element.184.g2, f32[272,512]{1,0:T(8,128)S(1)} %get-tuple-element.163.x, bf16[256,512]{1,0:T(8,128)(2,1)S(1)} %get-tuple-element.185.lag, ...), custom_call_target="tpu_custom_call" | custom-call | flops 1024 | bytes 1024 | tf_op jit(solution)/shard_map/pallas_call | solution.py:38
  75.0 6.7 %collective-permute-done.20.near_got = bf16[8,208,256]{2,1,0:T(8,128)(2,1)S(1)} collective-permute-done((bf16[8,208,256]{2,1,0:T(8,128)(2,1)S(1)}, bf16[8,208,256]{2,1,0:T(8,128)(2,1)S(1)}, u32[]{:S(2)}, u32[]{:S(2)}) %collective-permute-start.20) | collective-permute-done | bytes 852000 | tf_op jit(solution)/shard_map/ppermute | solution.py:75
  85.5 7.4 %collective-permute-done.22.last_got = bf16[4,208,256]{2,1,0:T(8,128)(2,1)S(1)} collective-permute-done((bf16[4,208,256]{2,1,0:T(8,128)(2,1)S(1)}, bf16[4,208,256]{2,1,0:T(8,128)(2,1)S(1)}, u32[]{:S(2)}, u32[]{:S(2)}) %collective-permute-start.22) | collective-permute-done | bytes 426016 | tf_op jit(solution)/shard_map/ppermute | solution.py:75
  93.7 3.5 %collective-permute-start.24 = (bf16[208,256]{1,0:T(8,128)(2,1)S(1)}, bf16[208,256]{1,0:T(8,128)(2,1)S(1)}, u32[]{:S(2)}, u32[]{:S(2)}) collective-permute-start(bf16[208,256]{1,0:T(8,128)(2,1)S(1)} %get-tuple-element.212), channel_id=1, source_target_pairs={{0,24},{1,25},{2,26},{3,27},{4,28},{5,29},{6,30},{7,31},{8,0},{9,1... | collective-permute-start | bytes 319496 | tf_op jit(solution)/shard_map/ppermute | solution.py:80
  97.3 2.8 %collective-permute-done.23.refs_0_.refs_1_ = bf16[208,256]{1,0:T(8,128)(2,1)S(1)} collective-permute-done((bf16[208,256]{1,0:T(8,128)(2,1)S(1)}, bf16[208,256]{1,0:T(8,128)(2,1)S(1)}, u32[]{:S(2)}, u32[]{:S(2)}) %collective-permute-start.23) | collective-permute-done | bytes 106528 | tf_op jit(solution)/shard_map/ppermute | solution.py:80
  103.0 7.2 %collective-permute-start.30 = (bf16[208,256]{1,0:T(8,128)(2,1)S(1)}, bf16[208,256]{1,0:T(8,128)(2,1)S(1)}, u32[]{:S(2)}, u32[]{:S(2)}) collective-permute-start(bf16[208,256]{1,0:T(8,128)(2,1)S(1)} %get-tuple-element.221), channel_id=1, source_target_pairs={{0,16},{1,17},{2,18},{3,19},{4,20},{5,21},{6,22},{7,23},{8,24},{9,... | collective-permute-start | bytes 319496 | tf_op jit(solution)/shard_map/ppermute | solution.py:80
  113.8 2.6 %collective-permute-start.27 = (bf16[208,256]{1,0:T(8,128)(2,1)S(1)}, bf16[208,256]{1,0:T(8,128)(2,1)S(1)}, u32[]{:S(2)}, u32[]{:S(2)}) collective-permute-start(bf16[208,256]{1,0:T(8,128)(2,1)S(1)} %get-tuple-element.216), channel_id=1, source_target_pairs={{0,16},{1,17},{2,18},{3,19},{4,20},{5,21},{6,22},{7,23},{8,24},{9,... | collective-permute-start | bytes 319496 | tf_op jit(solution)/shard_map/ppermute | solution.py:80
  116.4 7.4 %collective-permute-done.30.refs_2_ = bf16[208,256]{1,0:T(8,128)(2,1)S(1)} collective-permute-done((bf16[208,256]{1,0:T(8,128)(2,1)S(1)}, bf16[208,256]{1,0:T(8,128)(2,1)S(1)}, u32[]{:S(2)}, u32[]{:S(2)}) %collective-permute-start.30) | collective-permute-done | bytes 106528 | tf_op jit(solution)/shard_map/ppermute | solution.py:80
  127.0 10.1 %all_to_all.5 = f32[16,1,128]{2,1,0:T(1,128)S(1)} all-to-all(f32[16,1,128]{2,1,0:T(1,128)S(1)} %shard_map.535), channel_id=1, replica_groups=mesh['tm'=16,'mp'=2] {'tm'}, dimensions={0} | all-to-all | bytes 16384 | tf_op jit(solution)/shard_map/all_to_all | solution.py:914
  137.3 2.4 %shard_map.536 = (f32[1,1]{1,0:T(1,128)}, f32[512,256]{1,0:T(8,128)}, f32[512,128]{1,0:T(8,128)}, f32[512,128]{1,0:T(8,128)}, f32[512,128]{1,0:T(8,128)}, /*inde...) custom-call(s32[8]{0:T(128)S(1)} %copy-done.21, ...), custom_call_target="tpu_custom_call" | custom-call | flops 1024 | bytes 1024 | tf_op jit(solution)/shard_map/pallas_call | solution.py:38
  (128 shorter events, 37.8 us)
Async XLA Ops:
  3.6 17.7 %collective-permute-start = (bf16[512,256]{1,0:T(8,128)(2,1)}, bf16[512,256]{1,0:T(8,128)(2,1)S(1)}, u32[]{:S(2)}, u32[]{:S(2)}) collective-permute-start(bf16[512,256]{1,0:T(8,128)(2,1)} %get-tuple-element.146), channel_id=1, source_target_pairs={{0,2},{2,4},{4,6},{6,8},{8,10},{10,12},{12,14},{14,16},{16,18},{18... | collective-permute-start | bytes 786440 | tf_op jit(solution)/shard_map/ppermute | solution.py:92
  12.1 9.2 %collective-permute-start.5 = (bf16[208,256]{1,0:T(8,128)(2,1)}, bf16[208,256]{1,0:T(8,128)(2,1)S(1)}, u32[]{:S(2)}, u32[]{:S(2)}) collective-permute-start(bf16[208,256]{1,0:T(8,128)(2,1)} %get-tuple-element.149.value), channel_id=1, source_target_pairs={{0,16},{1,17},{2,18},{3,19},{4,20},{5,21},{6,22},{7,23},{8,24},{9,... | collective-permute-start | bytes 319496 | tf_op jit(solution)/shard_map/ppermute | solution.py:80
  12.1 9.2 %collective-permute-start.4 = (bf16[208,256]{1,0:T(8,128)(2,1)}, bf16[208,256]{1,0:T(8,128)(2,1)S(1)}, u32[]{:S(2)}, u32[]{:S(2)}) collective-permute-start(bf16[208,256]{1,0:T(8,128)(2,1)} %get-tuple-element.149.value), channel_id=1, source_target_pairs={{0,8},{1,9},{2,10},{3,11},{4,12},{5,13},{6,14},{7,15},{8,16},{9,17... | collective-permute-start | bytes 319496 | tf_op jit(solution)/shard_map/ppermute | solution.py:80
  21.3 18.1 %collective-permute-start.9 = (bf16[4,208,256]{2,1,0:T(8,128)(2,1)S(1)}, bf16[4,208,256]{2,1,0:T(8,128)(2,1)S(1)}, u32[]{:S(2)}, u32[]{:S(2)}) collective-permute-start(bf16[4,208,256]{2,1,0:T(8,128)(2,1)S(1)} %get-tuple-element.155.group), channel_id=1, source_target_pairs={{0,4},{1,3},{2,6},{3,1},{4,0},{5,7},{6,2},{7,5},{8,12},{9,11},{10,... | collective-permute-start | bytes 1277960 | tf_op jit(solution)/shard_map/ppermute | solution.py:75
  22.9 16.5 %collective-permute-start.8 = (bf16[4,208,256]{2,1,0:T(8,128)(2,1)S(1)}, bf16[4,208,256]{2,1,0:T(8,128)(2,1)S(1)}, u32[]{:S(2)}, u32[]{:S(2)}) collective-permute-start(bf16[4,208,256]{2,1,0:T(8,128)(2,1)S(1)} %get-tuple-element.155.group), channel_id=1, source_target_pairs={{0,2},{1,5},{2,0},{3,7},{4,6},{5,1},{6,4},{7,3},{8,10},{9,13},{10,... | collective-permute-start | bytes 1277960 | tf_op jit(solution)/shard_map/ppermute | solution.py:75
  24.4 9.1 %collective-permute-start.3 = (bf16[208,256]{1,0:T(8,128)(2,1)}, bf16[208,256]{1,0:T(8,128)(2,1)S(1)}, u32[]{:S(2)}, u32[]{:S(2)}) collective-permute-start(bf16[208,256]{1,0:T(8,128)(2,1)} %get-tuple-element.147.value), channel_id=1, source_target_pairs={{0,24},{1,25},{2,26},{3,27},{4,28},{5,29},{6,30},{7,31},{8,0},{9,1... | collective-permute-start | bytes 319496 | tf_op jit(solution)/shard_map/ppermute | solution.py:80
  29.7 8.6 %collective-permute-start.2 = (bf16[208,256]{1,0:T(8,128)(2,1)}, bf16[208,256]{1,0:T(8,128)(2,1)S(1)}, u32[]{:S(2)}, u32[]{:S(2)}) collective-permute-start(bf16[208,256]{1,0:T(8,128)(2,1)} %get-tuple-element.147.value), channel_id=1, source_target_pairs={{0,16},{1,17},{2,18},{3,19},{4,20},{5,21},{6,22},{7,23},{8,24},{9,... | collective-permute-start | bytes 319496 | tf_op jit(solution)/shard_map/ppermute | solution.py:80
  29.9 8.3 %collective-permute-start.1 = (bf16[208,256]{1,0:T(8,128)(2,1)}, bf16[208,256]{1,0:T(8,128)(2,1)S(1)}, u32[]{:S(2)}, u32[]{:S(2)}) collective-permute-start(bf16[208,256]{1,0:T(8,128)(2,1)} %get-tuple-element.147.value), channel_id=1, source_target_pairs={{0,8},{1,9},{2,10},{3,11},{4,12},{5,13},{6,14},{7,15},{8,16},{9,17... | collective-permute-start | bytes 319496 | tf_op jit(solution)/shard_map/ppermute | solution.py:80
  38.3 8.2 %collective-permute-start.12 = (bf16[4,208,256]{2,1,0:T(8,128)(2,1)S(1)}, bf16[4,208,256]{2,1,0:T(8,128)(2,1)S(1)}, u32[]{:S(2)}, u32[]{:S(2)}) collective-permute-start(bf16[4,208,256]{2,1,0:T(8,128)(2,1)S(1)} %get-tuple-element.161.group), channel_id=1, source_target_pairs={{0,4},{1,3},{2,6},{3,1},{4,0},{5,7},{6,2},{7,5},{8,12},{9,11},{10,... | collective-permute-start | bytes 1277960 | tf_op jit(solution)/shard_map/ppermute | solution.py:75
  38.7 12.3 %collective-permute-start.11 = (bf16[4,208,256]{2,1,0:T(8,128)(2,1)S(1)}, bf16[4,208,256]{2,1,0:T(8,128)(2,1)S(1)}, u32[]{:S(2)}, u32[]{:S(2)}) collective-permute-start(bf16[4,208,256]{2,1,0:T(8,128)(2,1)S(1)} %get-tuple-element.161.group), channel_id=1, source_target_pairs={{0,2},{1,5},{2,0},{3,7},{4,6},{5,1},{6,4},{7,3},{8,10},{9,13},{10,... | collective-permute-start | bytes 1277960 | tf_op jit(solution)/shard_map/ppermute | solution.py:75
  39.4 14.5 %collective-permute-start.13 = (bf16[4,208,256]{2,1,0:T(8,128)(2,1)S(1)}, bf16[4,208,256]{2,1,0:T(8,128)(2,1)S(1)}, u32[]{:S(2)}, u32[]{:S(2)}) collective-permute-start(bf16[4,208,256]{2,1,0:T(8,128)(2,1)S(1)} %get-tuple-element.167), channel_id=1, source_target_pairs={{0,4},{1,3},{2,6},{3,1},{4,0},{5,7},{6,2},{7,5},{8,12},{9,11},{10,... | collective-permute-start | bytes 1277960 | tf_op jit(solution)/shard_map/ppermute | solution.py:75
  42.5 10.4 %collective-permute-start.10 = (f32[8,2176]{1,0:T(8,128)S(1)}, f32[8,2176]{1,0:T(8,128)S(1)}, u32[]{:S(2)}, u32[]{:S(2)}) collective-permute-start(f32[8,2176]{1,0:T(8,128)S(1)} %get-tuple-element.160), channel_id=1, source_target_pairs={{1,2},{2,1},{3,4},{4,3},{5,6},{6,5},{7,8},{8,7},{9,10},{10,9},{11,... | collective-permute-start | bytes 208904 | tf_op jit(solution)/shard_map/ppermute | solution.py:99
  51.0 8.2 %collective-permute-start.15 = (bf16[4,208,256]{2,1,0:T(8,128)(2,1)S(1)}, bf16[4,208,256]{2,1,0:T(8,128)(2,1)S(1)}, u32[]{:S(2)}, u32[]{:S(2)}) collective-permute-start(bf16[4,208,256]{2,1,0:T(8,128)(2,1)S(1)} %get-tuple-element.174), channel_id=1, source_target_pairs={{0,4},{1,3},{2,6},{3,1},{4,0},{5,7},{6,2},{7,5},{8,12},{9,11},{10,... | collective-permute-start | bytes 1277960 | tf_op jit(solution)/shard_map/ppermute | solution.py:75
  68.9 12.8 %collective-permute-start.20 = (bf16[8,208,256]{2,1,0:T(8,128)(2,1)S(1)}, bf16[8,208,256]{2,1,0:T(8,128)(2,1)S(1)}, u32[]{:S(2)}, u32[]{:S(2)}) collective-permute-start(bf16[8,208,256]{2,1,0:T(8,128)(2,1)S(1)} %get-tuple-element.205), channel_id=1, source_target_pairs={{0,4},{1,3},{2,6},{3,1},{4,0},{5,7},{6,2},{7,5},{8,12},{9,11},{10,... | collective-permute-start | bytes 2555912 | tf_op jit(solution)/shard_map/ppermute | solution.py:75
  74.4 7.5 %collective-permute-start.18 = (f32[256,1024]{1,0:T(8,128)S(1)}, f32[256,1024]{1,0:T(8,128)S(1)}, u32[]{:S(2)}, u32[]{:S(2)}) collective-permute-start(f32[256,1024]{1,0:T(8,128)S(1)} %get-tuple-element.200), channel_id=1, source_target_pairs={{0,1},{1,0},{2,3},{3,2},{4,5},{5,4},{6,7},{7,6},{8,9},{9,8},{10,11... | collective-permute-start | bytes 3145736 | tf_op jit(solution)/shard_map/ppermute | solution.py:86
  74.5 8.6 %collective-permute-start.19 = (bf16[16,208,256]{2,1,0:T(8,128)(2,1)S(1)}, bf16[16,208,256]{2,1,0:T(8,128)(2,1)S(1)}, u32[]{:S(2)}, u32[]{:S(2)}) collective-permute-start(bf16[16,208,256]{2,1,0:T(8,128)(2,1)S(1)} %get-tuple-element.204), channel_id=1, source_target_pairs={{0,1},{1,0},{2,3},{3,2},{4,5},{5,4},{6,7},{7,6},{8,9},{9,8},{10,11... | collective-permute-start | bytes 5111816 | tf_op jit(solution)/shard_map/ppermute | solution.py:86
  81.8 11.1 %collective-permute-start.22 = (bf16[4,208,256]{2,1,0:T(8,128)(2,1)S(1)}, bf16[4,208,256]{2,1,0:T(8,128)(2,1)S(1)}, u32[]{:S(2)}, u32[]{:S(2)}) collective-permute-start(bf16[4,208,256]{2,1,0:T(8,128)(2,1)S(1)} %get-tuple-element.210), channel_id=1, source_target_pairs={{0,2},{1,5},{2,0},{3,7},{4,6},{5,1},{6,4},{7,3},{8,10},{9,13},{10,... | collective-permute-start | bytes 1277960 | tf_op jit(solution)/shard_map/ppermute | solution.py:75
  83.7 16.3 %collective-permute-start.21 = (bf16[8,208,256]{2,1,0:T(8,128)(2,1)S(1)}, bf16[8,208,256]{2,1,0:T(8,128)(2,1)S(1)}, u32[]{:S(2)}, u32[]{:S(2)}) collective-permute-start(bf16[8,208,256]{2,1,0:T(8,128)(2,1)S(1)} %get-tuple-element.209), channel_id=1, source_target_pairs={{0,4},{1,3},{2,6},{3,1},{4,0},{5,7},{6,2},{7,5},{8,12},{9,11},{10,... | collective-permute-start | bytes 2555912 | tf_op jit(solution)/shard_map/ppermute | solution.py:75
  100.7 10.9 %collective-permute-start.25 = (bf16[4,208,256]{2,1,0:T(8,128)(2,1)S(1)}, bf16[4,208,256]{2,1,0:T(8,128)(2,1)S(1)}, u32[]{:S(2)}, u32[]{:S(2)}) collective-permute-start(bf16[4,208,256]{2,1,0:T(8,128)(2,1)S(1)} %get-tuple-element.213), channel_id=1, source_target_pairs={{0,2},{1,5},{2,0},{3,7},{4,6},{5,1},{6,4},{7,3},{8,10},{9,13},{10,... | collective-permute-start | bytes 1277960 | tf_op jit(solution)/shard_map/ppermute | solution.py:75
  101.5 23.1 %collective-permute-start.29 = (bf16[512,256]{1,0:T(8,128)(2,1)S(1)}, bf16[512,256]{1,0:T(8,128)(2,1)S(1)}, u32[]{:S(2)}, u32[]{:S(2)}) collective-permute-start(bf16[512,256]{1,0:T(8,128)(2,1)S(1)} %shard_map.531), channel_id=1, source_target_pairs={{2,0},{4,2},{6,4},{8,6},{10,8},{12,10},{14,12},{16,14},{18,16},{20... | collective-permute-start | bytes 786440 | tf_op jit(solution)/shard_map/ppermute | solution.py:92
  103.0 20.8 %collective-permute-start.30 = (bf16[208,256]{1,0:T(8,128)(2,1)S(1)}, bf16[208,256]{1,0:T(8,128)(2,1)S(1)}, u32[]{:S(2)}, u32[]{:S(2)}) collective-permute-start(bf16[208,256]{1,0:T(8,128)(2,1)S(1)} %get-tuple-element.221), channel_id=1, source_target_pairs={{0,16},{1,17},{2,18},{3,19},{4,20},{5,21},{6,22},{7,23},{8,24},{9,... | collective-permute-start | bytes 319496 | tf_op jit(solution)/shard_map/ppermute | solution.py:80
  112.2 12.4 %collective-permute-start.26 = (bf16[208,256]{1,0:T(8,128)(2,1)S(1)}, bf16[208,256]{1,0:T(8,128)(2,1)S(1)}, u32[]{:S(2)}, u32[]{:S(2)}) collective-permute-start(bf16[208,256]{1,0:T(8,128)(2,1)S(1)} %get-tuple-element.215), channel_id=1, source_target_pairs={{0,8},{1,9},{2,10},{3,11},{4,12},{5,13},{6,14},{7,15},{8,16},{9,17... | collective-permute-start | bytes 319496 | tf_op jit(solution)/shard_map/ppermute | solution.py:80
  113.8 11.1 %collective-permute-start.27 = (bf16[208,256]{1,0:T(8,128)(2,1)S(1)}, bf16[208,256]{1,0:T(8,128)(2,1)S(1)}, u32[]{:S(2)}, u32[]{:S(2)}) collective-permute-start(bf16[208,256]{1,0:T(8,128)(2,1)S(1)} %get-tuple-element.216), channel_id=1, source_target_pairs={{0,16},{1,17},{2,18},{3,19},{4,20},{5,21},{6,22},{7,23},{8,24},{9,... | collective-permute-start | bytes 319496 | tf_op jit(solution)/shard_map/ppermute | solution.py:80
  116.4 8.6 %collective-permute-start.28 = (bf16[208,256]{1,0:T(8,128)(2,1)S(1)}, bf16[208,256]{1,0:T(8,128)(2,1)S(1)}, u32[]{:S(2)}, u32[]{:S(2)}) collective-permute-start(bf16[208,256]{1,0:T(8,128)(2,1)S(1)} %get-tuple-element.217), channel_id=1, source_target_pairs={{0,24},{1,25},{2,26},{3,27},{4,28},{5,29},{6,30},{7,31},{8,0},{9,1... | collective-permute-start | bytes 319496 | tf_op jit(solution)/shard_map/ppermute | solution.py:80
  (35 other events, 807.0 us)

commit v7 on v6

--- a/solution.py
+++ b/solution.py
@@ -906,11 +906,11 @@
     grads1, sent1, _ = near_summed(grads1, sent1, unread=(terms2[1], terms2[-1]))
     terms1, _ = far_terms(grads1, across(sent1, 0))
     sum2, squares2 = totals(terms2)
-    push = call(push_body, struct((held_rows, width), BF16), push)
-    push = shifted(push, "tm", -hop)
-    sum1, squares1 = totals(terms1, (push,))
+    sum1, squares1 = totals(terms1)
     squares = call(add_body, TOKEN, squares1, squares2)
     sent = call(spread_body, struct((parts, 1, LANES)), squares, swap_cores(squares))
+    push = call(push_body, struct((held_rows, width), BF16), push, unread=(sent,))
+    push = shifted(push, "tm", -hop)
     squares = lax.all_to_all(sent, "tm", split_axis=0, concat_axis=0, tiled=True)
     outs = [struct((1, 1)), struct((held_rows, width))]
     for view in views[0::3]:

time: 140 us -> 141 us (level)
  blocking collectives: 10.1 us -> 15.1 us
  starting transfers between devices: 47.2 us -> 42.3 us
    all_to_all x1, blocking collectives: 10.1 us -> 15.1 us  [on_device(): lax.all_to_all(sent, 'tm', split_axis=0, concat_axis=0, tiled=True)]
    ppermute x12, starting transfers between devices: 27.4 us -> 22.6 us  [along_far(): lax.ppermute(value, BOTH, route(lambda i, c: (i // NEAR + distance) % far...]
    ppermute x10, waiting for transfers between devices: 23.9 us -> 27.9 us  [across(): return lax.ppermute(value, BOTH, route(lambda i, c: i ^ 1 + (c ^ bit)))]
    ppermute x12, waiting for transfers between devices: 21.9 us -> 19.2 us  [along_far(): lax.ppermute(value, BOTH, route(lambda i, c: (i // NEAR + distance) % far...]
where the time goes in v7:
time: 141 us
  waiting for transfers between devices  55.8 us (40%)
  starting transfers between devices  42.3 us (30%)
  Pallas kernels  24.6 us (17%)
  blocking collectives  15.1 us (11%)
  local copies, waits for them, and re-layouts  2 us (1%)
    ppermute x10, waiting for transfers between devices, across(): return lax.ppermute(value, BOTH, route(lambda i, c: i ^ 1 + (c ^ bit)))  27.9 us
    pallas_call x33, Pallas kernels, call(): pl.pallas_call(body, out_shape=out_shape, in_specs=specs, scratch_shapes=...  24.6 us
    ppermute x12, starting transfers between devices, along_far(): lax.ppermute(value, BOTH, route(lambda i, c: (i // NEAR + distance) % far...  22.6 us
    ppermute x12, waiting for transfers between devices, along_far(): lax.ppermute(value, BOTH, route(lambda i, c: (i // NEAR + distance) % far...  19.2 us
    all_to_all x1, blocking collectives, on_device(): lax.all_to_all(sent, 'tm', split_axis=0, concat_axis=0, tiled=True)  15.1 us
    ppermute x10, starting transfers between devices, across(): return lax.ppermute(value, BOTH, route(lambda i, c: i ^ 1 + (c ^ bit)))  11.9 us
    ppermute x7, waiting for transfers between devices, swap_cores(): return lax.ppermute(value, 'mp', [(0, 1), (1, 0)])  8.77 us
    ppermute x2, starting transfers between devices, shifted(): return lax.ppermute(value, axis, pairs)  6.15 us
  transfers between devices with their start and end apart: 32, of which 17 were waited for; matrix products, arithmetic and copies ran while one was open for 0% of the time, Pallas kernels for 11%

profile of v7, /device:TPU:0, one launch (start us, length us, event | category | flops | bytes accessed | tf_op | source)
XLA Modules:
  0.0 141.1 jit_solution(1926836928714701045)
XLA Ops:
  0.7 2.9 %shard_map.504 = (bf16[208,256]{1,0:T(8,128)(2,1)}, bf16[208,256]{1,0:T(8,128)(2,1)}, bf16[512,256]{1,0:T(8,128)(2,1)}) custom-call(s32[8]{0:T(128)} %who.7, f32[512,128]{1,0:T(8,128)} %bitcast.75, f32[2,32,256]{2,1,0:T(8,128)} %bitcast.79, f32[2,32,256]{2,1,0:T(8,128)} %bitcast.81, f32[2,2,16,80]{3,2,1,0:T(8,128)} %bitcast.83, f32[2,2,16,109]{3,2,1,0:T(8,128)} %bitcast.85, ...), custom_call_target="tpu_custom_call" | custom-call | flops 1024 | bytes 1024 | tf_op jit(solution)/shard_map/pallas_call | solution.py:38
  3.6 4.9 %collective-permute-start = (bf16[512,256]{1,0:T(8,128)(2,1)}, bf16[512,256]{1,0:T(8,128)(2,1)S(1)}, u32[]{:S(2)}, u32[]{:S(2)}) collective-permute-start(bf16[512,256]{1,0:T(8,128)(2,1)} %get-tuple-element.146), channel_id=1, source_target_pairs={{0,2},{2,4},{4,6},{6,8},{8,10},{10,12},{12,14},{14,16},{16,18},{18... | collective-permute-start | bytes 786440 | tf_op jit(solution)/shard_map/ppermute | solution.py:92
  8.5 3.6 %collective-permute-start.6 = (bf16[208,256]{1,0:T(8,128)(2,1)}, bf16[208,256]{1,0:T(8,128)(2,1)S(1)}, u32[]{:S(2)}, u32[]{:S(2)}) collective-permute-start(bf16[208,256]{1,0:T(8,128)(2,1)} %get-tuple-element.149.value), channel_id=1, source_target_pairs={{0,24},{1,25},{2,26},{3,27},{4,28},{5,29},{6,30},{7,31},{8,0},{9,1... | collective-permute-start | bytes 319496 | tf_op jit(solution)/shard_map/ppermute | solution.py:80
  15.8 5.4 %collective-permute-done.5.refs_2_ = bf16[208,256]{1,0:T(8,128)(2,1)S(1)} collective-permute-done((bf16[208,256]{1,0:T(8,128)(2,1)}, bf16[208,256]{1,0:T(8,128)(2,1)S(1)}, u32[]{:S(2)}, u32[]{:S(2)}) %collective-permute-start.5) | collective-permute-done | bytes 106528 | tf_op jit(solution)/shard_map/ppermute | solution.py:80
  24.4 5.3 %collective-permute-start.3 = (bf16[208,256]{1,0:T(8,128)(2,1)}, bf16[208,256]{1,0:T(8,128)(2,1)S(1)}, u32[]{:S(2)}, u32[]{:S(2)}) collective-permute-start(bf16[208,256]{1,0:T(8,128)(2,1)} %get-tuple-element.147.value), channel_id=1, source_target_pairs={{0,24},{1,25},{2,26},{3,27},{4,28},{5,29},{6,30},{7,31},{8,0},{9,1... | collective-permute-start | bytes 319496 | tf_op jit(solution)/shard_map/ppermute | solution.py:80
  29.9 2.0 %collective-permute-start.1 = (bf16[208,256]{1,0:T(8,128)(2,1)}, bf16[208,256]{1,0:T(8,128)(2,1)S(1)}, u32[]{:S(2)}, u32[]{:S(2)}) collective-permute-start(bf16[208,256]{1,0:T(8,128)(2,1)} %get-tuple-element.147.value), channel_id=1, source_target_pairs={{0,8},{1,9},{2,10},{3,11},{4,12},{5,13},{6,14},{7,15},{8,16},{9,17... | collective-permute-start | bytes 319496 | tf_op jit(solution)/shard_map/ppermute | solution.py:80
  33.5 4.8 %collective-permute-done.2.refs_2_ = bf16[208,256]{1,0:T(8,128)(2,1)S(1)} collective-permute-done((bf16[208,256]{1,0:T(8,128)(2,1)}, bf16[208,256]{1,0:T(8,128)(2,1)S(1)}, u32[]{:S(2)}, u32[]{:S(2)}) %collective-permute-start.2) | collective-permute-done | bytes 106528 | tf_op jit(solution)/shard_map/ppermute | solution.py:80
  43.2 3.4 %collective-permute-done.12.refs_0_.second = bf16[4,208,256]{2,1,0:T(8,128)(2,1)S(1)} collective-permute-done((bf16[4,208,256]{2,1,0:T(8,128)(2,1)S(1)}, bf16[4,208,256]{2,1,0:T(8,128)(2,1)S(1)}, u32[]{:S(2)}, u32[]{:S(2)}) %collective-permute-start.12) | collective-permute-done | bytes 426016 | tf_op jit(solution)/shard_map/ppermute | solution.py:75
  46.5 4.5 %collective-permute-done.11.value.first = bf16[4,208,256]{2,1,0:T(8,128)(2,1)S(1)} collective-permute-done((bf16[4,208,256]{2,1,0:T(8,128)(2,1)S(1)}, bf16[4,208,256]{2,1,0:T(8,128)(2,1)S(1)}, u32[]{:S(2)}, u32[]{:S(2)}) %collective-permute-start.11) | collective-permute-done | bytes 426016 | tf_op jit(solution)/shard_map/ppermute | solution.py:75
  55.5 2.3 %collective-permute-done.14.weights = bf16[16,208,256]{2,1,0:T(8,128)(2,1)S(1)} collective-permute-done((bf16[16,208,256]{2,1,0:T(8,128)(2,1)S(1)}, bf16[16,208,256]{2,1,0:T(8,128)(2,1)S(1)}, u32[]{:S(2)}, u32[]{:S(2)}) %collective-permute-start.14) | collective-permute-done | bytes 1703968 | tf_op jit(solution)/shard_map/ppermute | solution.py:86
  59.5 3.6 %collective-permute-done.16.weights = bf16[16,208,256]{2,1,0:T(8,128)(2,1)S(1)} collective-permute-done((bf16[16,208,256]{2,1,0:T(8,128)(2,1)S(1)}, bf16[16,208,256]{2,1,0:T(8,128)(2,1)S(1)}, u32[]{:S(2)}, u32[]{:S(2)}) %collective-permute-start.16) | collective-permute-done | bytes 1703968 | tf_op jit(solution)/shard_map/ppermute | solution.py:86
  63.1 2.1 %shard_map.518 = (f32[256,512]{1,0:T(8,128)S(1)}, f32[256,512]{1,0:T(8,128)S(1)}, f32[256,512]{1,0:T(8,128)S(1)}, f32[272,512]{1,0:T(8,128)S(1)}, bf16[16,208,256]{2,1,0:T(8,128)(2,1)S(1)}) custom-call(f32[272,512]{1,0:T(8,128)S(1)} %get-tuple-element.170.u2, f32[256,512]{1,0:T(8,128)S(1)} %get-tuple-element.171.s1, ...), custom_call_target="tpu_custom_call" | custom-call | flops 1024 | bytes 1024 | tf_op jit(solution)/shard_map/pallas_call | solution.py:38
  65.9 2.0 %shard_map.520 = (f32[256,512]{1,0:T(8,128)S(1)}, f32[256,512]{1,0:T(8,128)S(1)}, f32[256,512]{1,0:T(8,128)S(1)}, f32[8,128]{1,0:T(8,128)}, bf16[16,208,256]{2,1,0:T(8,128)(2,1)S(1)}) custom-call(f32[272,512]{1,0:T(8,128)S(1)} %get-tuple-element.170.u2, f32[256,512]{1,0:T(8,128)S(1)} %get-tuple-element.171.s1, bf16[272,128]{1,0:T(8,128)(2,1)S(1)} %get-tuple-element.165.cond, ...), custom_call_target="tpu_custom_call" | custom-call | flops 1024 | bytes 1024 | tf_op jit(solution)/shard_map/pallas_call | solution.py:38
  70.7 1.9 %shard_map.522 = (f32[256,512]{1,0:T(8,128)S(1)}, f32[8,128]{1,0:T(8,128)}, f32[256,512]{1,0:T(8,128)S(1)}, bf16[16,208,256]{2,1,0:T(8,128)(2,1)S(1)}) custom-call(f32[256,512]{1,0:T(8,128)S(1)} %get-tuple-element.184.g2, f32[272,512]{1,0:T(8,128)S(1)} %get-tuple-element.163.x, bf16[256,512]{1,0:T(8,128)(2,1)S(1)} %get-tuple-element.185.lag, ...), custom_call_target="tpu_custom_call" | custom-call | flops 1024 | bytes 1024 | tf_op jit(solution)/shard_map/pallas_call | solution.py:38
  75.0 6.7 %collective-permute-done.20.near_got = bf16[8,208,256]{2,1,0:T(8,128)(2,1)S(1)} collective-permute-done((bf16[8,208,256]{2,1,0:T(8,128)(2,1)S(1)}, bf16[8,208,256]{2,1,0:T(8,128)(2,1)S(1)}, u32[]{:S(2)}, u32[]{:S(2)}) %collective-permute-start.20) | collective-permute-done | bytes 852000 | tf_op jit(solution)/shard_map/ppermute | solution.py:75
  85.5 7.4 %collective-permute-done.22.last_got = bf16[4,208,256]{2,1,0:T(8,128)(2,1)S(1)} collective-permute-done((bf16[4,208,256]{2,1,0:T(8,128)(2,1)S(1)}, bf16[4,208,256]{2,1,0:T(8,128)(2,1)S(1)}, u32[]{:S(2)}, u32[]{:S(2)}) %collective-permute-start.22) | collective-permute-done | bytes 426016 | tf_op jit(solution)/shard_map/ppermute | solution.py:75
  93.7 3.5 %collective-permute-start.24 = (bf16[208,256]{1,0:T(8,128)(2,1)S(1)}, bf16[208,256]{1,0:T(8,128)(2,1)S(1)}, u32[]{:S(2)}, u32[]{:S(2)}) collective-permute-start(bf16[208,256]{1,0:T(8,128)(2,1)S(1)} %get-tuple-element.212), channel_id=1, source_target_pairs={{0,24},{1,25},{2,26},{3,27},{4,28},{5,29},{6,30},{7,31},{8,0},{9,1... | collective-permute-start | bytes 319496 | tf_op jit(solution)/shard_map/ppermute | solution.py:80
  97.3 2.8 %collective-permute-done.23.refs_0_.refs_1_ = bf16[208,256]{1,0:T(8,128)(2,1)S(1)} collective-permute-done((bf16[208,256]{1,0:T(8,128)(2,1)S(1)}, bf16[208,256]{1,0:T(8,128)(2,1)S(1)}, u32[]{:S(2)}, u32[]{:S(2)}) %collective-permute-start.23) | collective-permute-done | bytes 106528 | tf_op jit(solution)/shard_map/ppermute | solution.py:80
  103.3 5.5 %collective-permute-done.25.last_got = bf16[4,208,256]{2,1,0:T(8,128)(2,1)S(1)} collective-permute-done((bf16[4,208,256]{2,1,0:T(8,128)(2,1)S(1)}, bf16[4,208,256]{2,1,0:T(8,128)(2,1)S(1)}, u32[]{:S(2)}, u32[]{:S(2)}) %collective-permute-start.25) | collective-permute-done | bytes 426016 | tf_op jit(solution)/shard_map/ppermute | solution.py:75
  111.2 2.7 %collective-permute-start.27 = (bf16[208,256]{1,0:T(8,128)(2,1)S(1)}, bf16[208,256]{1,0:T(8,128)(2,1)S(1)}, u32[]{:S(2)}, u32[]{:S(2)}) collective-permute-start(bf16[208,256]{1,0:T(8,128)(2,1)S(1)} %get-tuple-element.216), channel_id=1, source_target_pairs={{0,16},{1,17},{2,18},{3,19},{4,20},{5,21},{6,22},{7,23},{8,24},{9,... | collective-permute-start | bytes 319496 | tf_op jit(solution)/shard_map/ppermute | solution.py:80
  115.0 2.2 %collective-permute-done.26.refs_1_ = bf16[208,256]{1,0:T(8,128)(2,1)S(1)} collective-permute-done((bf16[208,256]{1,0:T(8,128)(2,1)S(1)}, bf16[208,256]{1,0:T(8,128)(2,1)S(1)}, u32[]{:S(2)}, u32[]{:S(2)}) %collective-permute-start.26) | collective-permute-done | bytes 106528 | tf_op jit(solution)/shard_map/ppermute | solution.py:80
  117.2 2.7 %collective-permute-done.27.refs_2_ = bf16[208,256]{1,0:T(8,128)(2,1)S(1)} collective-permute-done((bf16[208,256]{1,0:T(8,128)(2,1)S(1)}, bf16[208,256]{1,0:T(8,128)(2,1)S(1)}, u32[]{:S(2)}, u32[]{:S(2)}) %collective-permute-start.27) | collective-permute-done | bytes 106528 | tf_op jit(solution)/shard_map/ppermute | solution.py:80
  123.4 15.1 %all_to_all.5 = f32[16,1,128]{2,1,0:T(1,128)S(1)} all-to-all(f32[16,1,128]{2,1,0:T(1,128)S(1)} %shard_map.534.refs_0_), channel_id=1, replica_groups=mesh['tm'=16,'mp'=2] {'tm'}, dimensions={0} | all-to-all | bytes 16384 | tf_op jit(solution)/shard_map/all_to_all | solution.py:914
  138.6 2.5 %shard_map.536 = (f32[1,1]{1,0:T(1,128)}, f32[512,256]{1,0:T(8,128)}, f32[512,128]{1,0:T(8,128)}, f32[512,128]{1,0:T(8,128)}, f32[512,128]{1,0:T(8,128)}, /*inde...) custom-call(s32[8]{0:T(128)S(1)} %copy-done.21, ...), custom_call_target="tpu_custom_call" | custom-call | flops 1024 | bytes 1024 | tf_op jit(solution)/shard_map/pallas_call | solution.py:38
  (128 shorter events, 40.1 us)
Async XLA Ops:
  3.6 17.7 %collective-permute-start = (bf16[512,256]{1,0:T(8,128)(2,1)}, bf16[512,256]{1,0:T(8,128)(2,1)S(1)}, u32[]{:S(2)}, u32[]{:S(2)}) collective-permute-start(bf16[512,256]{1,0:T(8,128)(2,1)} %get-tuple-element.146), channel_id=1, source_target_pairs={{0,2},{2,4},{4,6},{6,8},{8,10},{10,12},{12,14},{14,16},{16,18},{18... | collective-permute-start | bytes 786440 | tf_op jit(solution)/shard_map/ppermute | solution.py:92
  8.5 7.4 %collective-permute-start.6 = (bf16[208,256]{1,0:T(8,128)(2,1)}, bf16[208,256]{1,0:T(8,128)(2,1)S(1)}, u32[]{:S(2)}, u32[]{:S(2)}) collective-permute-start(bf16[208,256]{1,0:T(8,128)(2,1)} %get-tuple-element.149.value), channel_id=1, source_target_pairs={{0,24},{1,25},{2,26},{3,27},{4,28},{5,29},{6,30},{7,31},{8,0},{9,1... | collective-permute-start | bytes 319496 | tf_op jit(solution)/shard_map/ppermute | solution.py:80
  12.1 9.2 %collective-permute-start.5 = (bf16[208,256]{1,0:T(8,128)(2,1)}, bf16[208,256]{1,0:T(8,128)(2,1)S(1)}, u32[]{:S(2)}, u32[]{:S(2)}) collective-permute-start(bf16[208,256]{1,0:T(8,128)(2,1)} %get-tuple-element.149.value), channel_id=1, source_target_pairs={{0,16},{1,17},{2,18},{3,19},{4,20},{5,21},{6,22},{7,23},{8,24},{9,... | collective-permute-start | bytes 319496 | tf_op jit(solution)/shard_map/ppermute | solution.py:80
  12.1 9.2 %collective-permute-start.4 = (bf16[208,256]{1,0:T(8,128)(2,1)}, bf16[208,256]{1,0:T(8,128)(2,1)S(1)}, u32[]{:S(2)}, u32[]{:S(2)}) collective-permute-start(bf16[208,256]{1,0:T(8,128)(2,1)} %get-tuple-element.149.value), channel_id=1, source_target_pairs={{0,8},{1,9},{2,10},{3,11},{4,12},{5,13},{6,14},{7,15},{8,16},{9,17... | collective-permute-start | bytes 319496 | tf_op jit(solution)/shard_map/ppermute | solution.py:80
  21.3 18.1 %collective-permute-start.9 = (bf16[4,208,256]{2,1,0:T(8,128)(2,1)S(1)}, bf16[4,208,256]{2,1,0:T(8,128)(2,1)S(1)}, u32[]{:S(2)}, u32[]{:S(2)}) collective-permute-start(bf16[4,208,256]{2,1,0:T(8,128)(2,1)S(1)} %get-tuple-element.155.group), channel_id=1, source_target_pairs={{0,4},{1,3},{2,6},{3,1},{4,0},{5,7},{6,2},{7,5},{8,12},{9,11},{10,... | collective-permute-start | bytes 1277960 | tf_op jit(solution)/shard_map/ppermute | solution.py:75
  22.9 16.5 %collective-permute-start.8 = (bf16[4,208,256]{2,1,0:T(8,128)(2,1)S(1)}, bf16[4,208,256]{2,1,0:T(8,128)(2,1)S(1)}, u32[]{:S(2)}, u32[]{:S(2)}) collective-permute-start(bf16[4,208,256]{2,1,0:T(8,128)(2,1)S(1)} %get-tuple-element.155.group), channel_id=1, source_target_pairs={{0,2},{1,5},{2,0},{3,7},{4,6},{5,1},{6,4},{7,3},{8,10},{9,13},{10,... | collective-permute-start | bytes 1277960 | tf_op jit(solution)/shard_map/ppermute | solution.py:75
  24.4 9.1 %collective-permute-start.3 = (bf16[208,256]{1,0:T(8,128)(2,1)}, bf16[208,256]{1,0:T(8,128)(2,1)S(1)}, u32[]{:S(2)}, u32[]{:S(2)}) collective-permute-start(bf16[208,256]{1,0:T(8,128)(2,1)} %get-tuple-element.147.value), channel_id=1, source_target_pairs={{0,24},{1,25},{2,26},{3,27},{4,28},{5,29},{6,30},{7,31},{8,0},{9,1... | collective-permute-start | bytes 319496 | tf_op jit(solution)/shard_map/ppermute | solution.py:80
  29.7 8.6 %collective-permute-start.2 = (bf16[208,256]{1,0:T(8,128)(2,1)}, bf16[208,256]{1,0:T(8,128)(2,1)S(1)}, u32[]{:S(2)}, u32[]{:S(2)}) collective-permute-start(bf16[208,256]{1,0:T(8,128)(2,1)} %get-tuple-element.147.value), channel_id=1, source_target_pairs={{0,16},{1,17},{2,18},{3,19},{4,20},{5,21},{6,22},{7,23},{8,24},{9,... | collective-permute-start | bytes 319496 | tf_op jit(solution)/shard_map/ppermute | solution.py:80
  29.9 8.3 %collective-permute-start.1 = (bf16[208,256]{1,0:T(8,128)(2,1)}, bf16[208,256]{1,0:T(8,128)(2,1)S(1)}, u32[]{:S(2)}, u32[]{:S(2)}) collective-permute-start(bf16[208,256]{1,0:T(8,128)(2,1)} %get-tuple-element.147.value), channel_id=1, source_target_pairs={{0,8},{1,9},{2,10},{3,11},{4,12},{5,13},{6,14},{7,15},{8,16},{9,17... | collective-permute-start | bytes 319496 | tf_op jit(solution)/shard_map/ppermute | solution.py:80
  38.3 8.2 %collective-permute-start.12 = (bf16[4,208,256]{2,1,0:T(8,128)(2,1)S(1)}, bf16[4,208,256]{2,1,0:T(8,128)(2,1)S(1)}, u32[]{:S(2)}, u32[]{:S(2)}) collective-permute-start(bf16[4,208,256]{2,1,0:T(8,128)(2,1)S(1)} %get-tuple-element.161.group), channel_id=1, source_target_pairs={{0,4},{1,3},{2,6},{3,1},{4,0},{5,7},{6,2},{7,5},{8,12},{9,11},{10,... | collective-permute-start | bytes 1277960 | tf_op jit(solution)/shard_map/ppermute | solution.py:75
  38.7 12.3 %collective-permute-start.11 = (bf16[4,208,256]{2,1,0:T(8,128)(2,1)S(1)}, bf16[4,208,256]{2,1,0:T(8,128)(2,1)S(1)}, u32[]{:S(2)}, u32[]{:S(2)}) collective-permute-start(bf16[4,208,256]{2,1,0:T(8,128)(2,1)S(1)} %get-tuple-element.161.group), channel_id=1, source_target_pairs={{0,2},{1,5},{2,0},{3,7},{4,6},{5,1},{6,4},{7,3},{8,10},{9,13},{10,... | collective-permute-start | bytes 1277960 | tf_op jit(solution)/shard_map/ppermute | solution.py:75
  39.4 14.5 %collective-permute-start.13 = (bf16[4,208,256]{2,1,0:T(8,128)(2,1)S(1)}, bf16[4,208,256]{2,1,0:T(8,128)(2,1)S(1)}, u32[]{:S(2)}, u32[]{:S(2)}) collective-permute-start(bf16[4,208,256]{2,1,0:T(8,128)(2,1)S(1)} %get-tuple-element.167), channel_id=1, source_target_pairs={{0,4},{1,3},{2,6},{3,1},{4,0},{5,7},{6,2},{7,5},{8,12},{9,11},{10,... | collective-permute-start | bytes 1277960 | tf_op jit(solution)/shard_map/ppermute | solution.py:75
  42.5 10.4 %collective-permute-start.10 = (f32[8,2176]{1,0:T(8,128)S(1)}, f32[8,2176]{1,0:T(8,128)S(1)}, u32[]{:S(2)}, u32[]{:S(2)}) collective-permute-start(f32[8,2176]{1,0:T(8,128)S(1)} %get-tuple-element.160), channel_id=1, source_target_pairs={{1,2},{2,1},{3,4},{4,3},{5,6},{6,5},{7,8},{8,7},{9,10},{10,9},{11,... | collective-permute-start | bytes 208904 | tf_op jit(solution)/shard_map/ppermute | solution.py:99
  51.0 8.2 %collective-permute-start.15 = (bf16[4,208,256]{2,1,0:T(8,128)(2,1)S(1)}, bf16[4,208,256]{2,1,0:T(8,128)(2,1)S(1)}, u32[]{:S(2)}, u32[]{:S(2)}) collective-permute-start(bf16[4,208,256]{2,1,0:T(8,128)(2,1)S(1)} %get-tuple-element.174), channel_id=1, source_target_pairs={{0,4},{1,3},{2,6},{3,1},{4,0},{5,7},{6,2},{7,5},{8,12},{9,11},{10,... | collective-permute-start | bytes 1277960 | tf_op jit(solution)/shard_map/ppermute | solution.py:75
  68.9 12.8 %collective-permute-start.20 = (bf16[8,208,256]{2,1,0:T(8,128)(2,1)S(1)}, bf16[8,208,256]{2,1,0:T(8,128)(2,1)S(1)}, u32[]{:S(2)}, u32[]{:S(2)}) collective-permute-start(bf16[8,208,256]{2,1,0:T(8,128)(2,1)S(1)} %get-tuple-element.205), channel_id=1, source_target_pairs={{0,4},{1,3},{2,6},{3,1},{4,0},{5,7},{6,2},{7,5},{8,12},{9,11},{10,... | collective-permute-start | bytes 2555912 | tf_op jit(solution)/shard_map/ppermute | solution.py:75
  74.4 7.5 %collective-permute-start.18 = (f32[256,1024]{1,0:T(8,128)S(1)}, f32[256,1024]{1,0:T(8,128)S(1)}, u32[]{:S(2)}, u32[]{:S(2)}) collective-permute-start(f32[256,1024]{1,0:T(8,128)S(1)} %get-tuple-element.200), channel_id=1, source_target_pairs={{0,1},{1,0},{2,3},{3,2},{4,5},{5,4},{6,7},{7,6},{8,9},{9,8},{10,11... | collective-permute-start | bytes 3145736 | tf_op jit(solution)/shard_map/ppermute | solution.py:86
  74.5 8.6 %collective-permute-start.19 = (bf16[16,208,256]{2,1,0:T(8,128)(2,1)S(1)}, bf16[16,208,256]{2,1,0:T(8,128)(2,1)S(1)}, u32[]{:S(2)}, u32[]{:S(2)}) collective-permute-start(bf16[16,208,256]{2,1,0:T(8,128)(2,1)S(1)} %get-tuple-element.204), channel_id=1, source_target_pairs={{0,1},{1,0},{2,3},{3,2},{4,5},{5,4},{6,7},{7,6},{8,9},{9,8},{10,11... | collective-permute-start | bytes 5111816 | tf_op jit(solution)/shard_map/ppermute | solution.py:86
  81.8 11.1 %collective-permute-start.22 = (bf16[4,208,256]{2,1,0:T(8,128)(2,1)S(1)}, bf16[4,208,256]{2,1,0:T(8,128)(2,1)S(1)}, u32[]{:S(2)}, u32[]{:S(2)}) collective-permute-start(bf16[4,208,256]{2,1,0:T(8,128)(2,1)S(1)} %get-tuple-element.210), channel_id=1, source_target_pairs={{0,2},{1,5},{2,0},{3,7},{4,6},{5,1},{6,4},{7,3},{8,10},{9,13},{10,... | collective-permute-start | bytes 1277960 | tf_op jit(solution)/shard_map/ppermute | solution.py:75
  83.7 16.3 %collective-permute-start.21 = (bf16[8,208,256]{2,1,0:T(8,128)(2,1)S(1)}, bf16[8,208,256]{2,1,0:T(8,128)(2,1)S(1)}, u32[]{:S(2)}, u32[]{:S(2)}) collective-permute-start(bf16[8,208,256]{2,1,0:T(8,128)(2,1)S(1)} %get-tuple-element.209), channel_id=1, source_target_pairs={{0,4},{1,3},{2,6},{3,1},{4,0},{5,7},{6,2},{7,5},{8,12},{9,11},{10,... | collective-permute-start | bytes 2555912 | tf_op jit(solution)/shard_map/ppermute | solution.py:75
  100.7 8.1 %collective-permute-start.25 = (bf16[4,208,256]{2,1,0:T(8,128)(2,1)S(1)}, bf16[4,208,256]{2,1,0:T(8,128)(2,1)S(1)}, u32[]{:S(2)}, u32[]{:S(2)}) collective-permute-start(bf16[4,208,256]{2,1,0:T(8,128)(2,1)S(1)} %get-tuple-element.213), channel_id=1, source_target_pairs={{0,2},{1,5},{2,0},{3,7},{4,6},{5,1},{6,4},{7,3},{8,10},{9,13},{10,... | collective-permute-start | bytes 1277960 | tf_op jit(solution)/shard_map/ppermute | solution.py:75
  101.5 12.7 %collective-permute-start.29 = (bf16[208,256]{1,0:T(8,128)(2,1)S(1)}, bf16[208,256]{1,0:T(8,128)(2,1)S(1)}, u32[]{:S(2)}, u32[]{:S(2)}) collective-permute-start(bf16[208,256]{1,0:T(8,128)(2,1)S(1)} %get-tuple-element.220), channel_id=1, source_target_pairs={{0,16},{1,17},{2,18},{3,19},{4,20},{5,21},{6,22},{7,23},{8,24},{9,... | collective-permute-start | bytes 319496 | tf_op jit(solution)/shard_map/ppermute | solution.py:80
  109.6 7.6 %collective-permute-start.26 = (bf16[208,256]{1,0:T(8,128)(2,1)S(1)}, bf16[208,256]{1,0:T(8,128)(2,1)S(1)}, u32[]{:S(2)}, u32[]{:S(2)}) collective-permute-start(bf16[208,256]{1,0:T(8,128)(2,1)S(1)} %get-tuple-element.215), channel_id=1, source_target_pairs={{0,8},{1,9},{2,10},{3,11},{4,12},{5,13},{6,14},{7,15},{8,16},{9,17... | collective-permute-start | bytes 319496 | tf_op jit(solution)/shard_map/ppermute | solution.py:80
  111.2 8.7 %collective-permute-start.27 = (bf16[208,256]{1,0:T(8,128)(2,1)S(1)}, bf16[208,256]{1,0:T(8,128)(2,1)S(1)}, u32[]{:S(2)}, u32[]{:S(2)}) collective-permute-start(bf16[208,256]{1,0:T(8,128)(2,1)S(1)} %get-tuple-element.216), channel_id=1, source_target_pairs={{0,16},{1,17},{2,18},{3,19},{4,20},{5,21},{6,22},{7,23},{8,24},{9,... | collective-permute-start | bytes 319496 | tf_op jit(solution)/shard_map/ppermute | solution.py:80
  122.1 16.4 %collective-permute-start.31 = (bf16[512,256]{1,0:T(8,128)(2,1)S(1)}, bf16[512,256]{1,0:T(8,128)(2,1)S(1)}, u32[]{:S(2)}, u32[]{:S(2)}) collective-permute-start(bf16[512,256]{1,0:T(8,128)(2,1)S(1)} %shard_map.535), channel_id=1, source_target_pairs={{2,0},{4,2},{6,4},{8,6},{10,8},{12,10},{14,12},{16,14},{18,16},{20... | collective-permute-start | bytes 786440 | tf_op jit(solution)/shard_map/ppermute | solution.py:92
  (35 other events, 702.1 us)

commit v8 on v6

--- a/solution.py
+++ b/solution.py
@@ -854,13 +854,14 @@
     *sums, grad_oth = middle(w2_oth)
     mixed, skip_total, g2, _, grad_own = middle(w2_own, *sums, *gate_two)
 
-    def totals(terms, unread=()):
+    def totals(terms, unread=(), flops=1024):
         return call(
             functools.partial(square_body, rows, mel, clips, speakers, len(terms)),
             (struct((total, 256)), struct((8, LANES))),
             *terms,
             scalars=(speaker_ids,),
             unread=unread,
+            flops=flops,
         )
 
     def backward(weights, tanh_a, sig_b, hidden, *earlier, unread):
@@ -904,11 +905,11 @@
     last_got = across(sent2, 0)
     terms2, _ = far_terms(grads2, last_got, LONG)
     grads1, sent1, _ = near_summed(grads1, sent1, unread=(terms2[1], terms2[-1]))
-    terms1, _ = far_terms(grads1, across(sent1, 0))
-    sum2, squares2 = totals(terms2)
-    push = call(push_body, struct((held_rows, width), BF16), push)
+    terms1, token = far_terms(grads1, across(sent1, 0))
+    sum2, squares2 = totals(terms2, (token,))
+    push = call(push_body, struct((held_rows, width), BF16), push, unread=(squares2,))
     push = shifted(push, "tm", -hop)
-    sum1, squares1 = totals(terms1, (push,))
+    sum1, squares1 = totals(terms1, flops=LONG // 5)
     squares = call(add_body, TOKEN, squares1, squares2)
     sent = call(spread_body, struct((parts, 1, LANES)), squares, swap_cores(squares))
     squares = lax.all_to_all(sent, "tm", split_axis=0, concat_axis=0, tiled=True)

time: 140 us -> 138 us (0.986)
  starting transfers between devices: 47.2 us -> 42.3 us
  blocking collectives: 10.1 us -> 12.9 us
    ppermute x12, starting transfers between devices: 27.4 us -> 22.6 us  [along_far(): lax.ppermute(value, BOTH, route(lambda i, c: (i // NEAR + distance) % far...]
    ppermute x10, waiting for transfers between devices: 23.9 us -> 27.9 us  [across(): return lax.ppermute(value, BOTH, route(lambda i, c: i ^ 1 + (c ^ bit)))]
    ppermute x12, waiting for transfers between devices: 21.9 us -> 17.9 us  [along_far(): lax.ppermute(value, BOTH, route(lambda i, c: (i // NEAR + distance) % far...]
    all_to_all x1, blocking collectives: 10.1 us -> 12.9 us  [on_device(): lax.all_to_all(sent, 'tm', split_axis=0, concat_axis=0, tiled=True)]
  transfers between devices with their start and end apart: 32 -> 32, of which waited for: 17 -> 17; matrix products, arithmetic and copies ran while one was open for 0% -> 0% of each run, Pallas kernels for 11% -> 12%
where the time goes in v8:
time: 138 us; the launch traced here: 137 us
  waiting for transfers between devices  54.6 us (40%)
  starting transfers between devices  42.3 us (31%)
  Pallas kernels  24.2 us (18%)
  blocking collectives  12.9 us (9%)
  local copies, waits for them, and re-layouts  2 us (1%)
    ppermute x10, waiting for transfers between devices, across(): return lax.ppermute(value, BOTH, route(lambda i, c: i ^ 1 + (c ^ bit)))  27.9 us
    pallas_call x33, Pallas kernels, call(): pl.pallas_call(body, out_shape=out_shape, in_specs=specs, scratch_shapes=...  24.2 us
    ppermute x12, starting transfers between devices, along_far(): lax.ppermute(value, BOTH, route(lambda i, c: (i // NEAR + distance) % far...  22.6 us
    ppermute x12, waiting for transfers between devices, along_far(): lax.ppermute(value, BOTH, route(lambda i, c: (i // NEAR + distance) % far...  17.9 us
    all_to_all x1, blocking collectives, on_device(): lax.all_to_all(sent, 'tm', split_axis=0, concat_axis=0, tiled=True)  12.9 us
    ppermute x10, starting transfers between devices, across(): return lax.ppermute(value, BOTH, route(lambda i, c: i ^ 1 + (c ^ bit)))  11.9 us
    ppermute x7, waiting for transfers between devices, swap_cores(): return lax.ppermute(value, 'mp', [(0, 1), (1, 0)])  8.77 us
    ppermute x2, starting transfers between devices, shifted(): return lax.ppermute(value, axis, pairs)  6.15 us
  transfers between devices with their start and end apart: 32, of which 17 were waited for; matrix products, arithmetic and copies ran while one was open for 0% of the time, Pallas kernels for 12%

profile of v8, /device:TPU:0, one launch (start us, length us, event | category | flops | bytes accessed | tf_op | source)
XLA Modules:
  0.0 137.2 jit_solution(201580509717223200)
XLA Ops:
  0.7 2.9 %shard_map.504 = (bf16[208,256]{1,0:T(8,128)(2,1)}, bf16[208,256]{1,0:T(8,128)(2,1)}, bf16[512,256]{1,0:T(8,128)(2,1)}) custom-call(s32[8]{0:T(128)} %who.7, f32[512,128]{1,0:T(8,128)} %bitcast.75, f32[2,32,256]{2,1,0:T(8,128)} %bitcast.79, f32[2,32,256]{2,1,0:T(8,128)} %bitcast.81, f32[2,2,16,80]{3,2,1,0:T(8,128)} %bitcast.83, f32[2,2,16,109]{3,2,1,0:T(8,128)} %bitcast.85, ...), custom_call_target="tpu_custom_call" | custom-call | flops 1024 | bytes 1024 | tf_op jit(solution)/shard_map/pallas_call | solution.py:38
  3.6 4.9 %collective-permute-start = (bf16[512,256]{1,0:T(8,128)(2,1)}, bf16[512,256]{1,0:T(8,128)(2,1)S(1)}, u32[]{:S(2)}, u32[]{:S(2)}) collective-permute-start(bf16[512,256]{1,0:T(8,128)(2,1)} %get-tuple-element.147), channel_id=1, source_target_pairs={{0,2},{2,4},{4,6},{6,8},{8,10},{10,12},{12,14},{14,16},{16,18},{18... | collective-permute-start | bytes 786440 | tf_op jit(solution)/shard_map/ppermute | solution.py:92
  8.5 3.6 %collective-permute-start.6 = (bf16[208,256]{1,0:T(8,128)(2,1)}, bf16[208,256]{1,0:T(8,128)(2,1)S(1)}, u32[]{:S(2)}, u32[]{:S(2)}) collective-permute-start(bf16[208,256]{1,0:T(8,128)(2,1)} %get-tuple-element.150.value), channel_id=1, source_target_pairs={{0,24},{1,25},{2,26},{3,27},{4,28},{5,29},{6,30},{7,31},{8,0},{9,1... | collective-permute-start | bytes 319496 | tf_op jit(solution)/shard_map/ppermute | solution.py:80
  15.8 5.4 %collective-permute-done.5.refs_2_ = bf16[208,256]{1,0:T(8,128)(2,1)S(1)} collective-permute-done((bf16[208,256]{1,0:T(8,128)(2,1)}, bf16[208,256]{1,0:T(8,128)(2,1)S(1)}, u32[]{:S(2)}, u32[]{:S(2)}) %collective-permute-start.5) | collective-permute-done | bytes 106528 | tf_op jit(solution)/shard_map/ppermute | solution.py:80
  24.4 5.3 %collective-permute-start.3 = (bf16[208,256]{1,0:T(8,128)(2,1)}, bf16[208,256]{1,0:T(8,128)(2,1)S(1)}, u32[]{:S(2)}, u32[]{:S(2)}) collective-permute-start(bf16[208,256]{1,0:T(8,128)(2,1)} %get-tuple-element.148.value), channel_id=1, source_target_pairs={{0,24},{1,25},{2,26},{3,27},{4,28},{5,29},{6,30},{7,31},{8,0},{9,1... | collective-permute-start | bytes 319496 | tf_op jit(solution)/shard_map/ppermute | solution.py:80
  29.9 2.0 %collective-permute-start.1 = (bf16[208,256]{1,0:T(8,128)(2,1)}, bf16[208,256]{1,0:T(8,128)(2,1)S(1)}, u32[]{:S(2)}, u32[]{:S(2)}) collective-permute-start(bf16[208,256]{1,0:T(8,128)(2,1)} %get-tuple-element.148.value), channel_id=1, source_target_pairs={{0,8},{1,9},{2,10},{3,11},{4,12},{5,13},{6,14},{7,15},{8,16},{9,17... | collective-permute-start | bytes 319496 | tf_op jit(solution)/shard_map/ppermute | solution.py:80
  33.5 4.8 %collective-permute-done.2.refs_2_ = bf16[208,256]{1,0:T(8,128)(2,1)S(1)} collective-permute-done((bf16[208,256]{1,0:T(8,128)(2,1)}, bf16[208,256]{1,0:T(8,128)(2,1)S(1)}, u32[]{:S(2)}, u32[]{:S(2)}) %collective-permute-start.2) | collective-permute-done | bytes 106528 | tf_op jit(solution)/shard_map/ppermute | solution.py:80
  43.2 3.4 %collective-permute-done.12.refs_0_.second = bf16[4,208,256]{2,1,0:T(8,128)(2,1)S(1)} collective-permute-done((bf16[4,208,256]{2,1,0:T(8,128)(2,1)S(1)}, bf16[4,208,256]{2,1,0:T(8,128)(2,1)S(1)}, u32[]{:S(2)}, u32[]{:S(2)}) %collective-permute-start.12) | collective-permute-done | bytes 426016 | tf_op jit(solution)/shard_map/ppermute | solution.py:75
  46.5 4.5 %collective-permute-done.11.value.first = bf16[4,208,256]{2,1,0:T(8,128)(2,1)S(1)} collective-permute-done((bf16[4,208,256]{2,1,0:T(8,128)(2,1)S(1)}, bf16[4,208,256]{2,1,0:T(8,128)(2,1)S(1)}, u32[]{:S(2)}, u32[]{:S(2)}) %collective-permute-start.11) | collective-permute-done | bytes 426016 | tf_op jit(solution)/shard_map/ppermute | solution.py:75
  55.5 2.3 %collective-permute-done.14.weights = bf16[16,208,256]{2,1,0:T(8,128)(2,1)S(1)} collective-permute-done((bf16[16,208,256]{2,1,0:T(8,128)(2,1)S(1)}, bf16[16,208,256]{2,1,0:T(8,128)(2,1)S(1)}, u32[]{:S(2)}, u32[]{:S(2)}) %collective-permute-start.14) | collective-permute-done | bytes 1703968 | tf_op jit(solution)/shard_map/ppermute | solution.py:86
  59.5 3.6 %collective-permute-done.16.weights = bf16[16,208,256]{2,1,0:T(8,128)(2,1)S(1)} collective-permute-done((bf16[16,208,256]{2,1,0:T(8,128)(2,1)S(1)}, bf16[16,208,256]{2,1,0:T(8,128)(2,1)S(1)}, u32[]{:S(2)}, u32[]{:S(2)}) %collective-permute-start.16) | collective-permute-done | bytes 1703968 | tf_op jit(solution)/shard_map/ppermute | solution.py:86
  63.1 2.1 %shard_map.518 = (f32[256,512]{1,0:T(8,128)S(1)}, f32[256,512]{1,0:T(8,128)S(1)}, f32[256,512]{1,0:T(8,128)S(1)}, f32[272,512]{1,0:T(8,128)S(1)}, bf16[16,208,256]{2,1,0:T(8,128)(2,1)S(1)}) custom-call(f32[272,512]{1,0:T(8,128)S(1)} %get-tuple-element.171.u2, f32[256,512]{1,0:T(8,128)S(1)} %get-tuple-element.172.s1, ...), custom_call_target="tpu_custom_call" | custom-call | flops 1024 | bytes 1024 | tf_op jit(solution)/shard_map/pallas_call | solution.py:38
  65.9 2.0 %shard_map.520 = (f32[256,512]{1,0:T(8,128)S(1)}, f32[256,512]{1,0:T(8,128)S(1)}, f32[256,512]{1,0:T(8,128)S(1)}, f32[8,128]{1,0:T(8,128)}, bf16[16,208,256]{2,1,0:T(8,128)(2,1)S(1)}) custom-call(f32[272,512]{1,0:T(8,128)S(1)} %get-tuple-element.171.u2, f32[256,512]{1,0:T(8,128)S(1)} %get-tuple-element.172.s1, bf16[272,128]{1,0:T(8,128)(2,1)S(1)} %get-tuple-element.166.cond, ...), custom_call_target="tpu_custom_call" | custom-call | flops 1024 | bytes 1024 | tf_op jit(solution)/shard_map/pallas_call | solution.py:38
  70.7 1.9 %shard_map.522 = (f32[256,512]{1,0:T(8,128)S(1)}, f32[8,128]{1,0:T(8,128)}, f32[256,512]{1,0:T(8,128)S(1)}, bf16[16,208,256]{2,1,0:T(8,128)(2,1)S(1)}) custom-call(f32[256,512]{1,0:T(8,128)S(1)} %get-tuple-element.185.g2, f32[272,512]{1,0:T(8,128)S(1)} %get-tuple-element.164.x, bf16[256,512]{1,0:T(8,128)(2,1)S(1)} %get-tuple-element.186.lag, ...), custom_call_target="tpu_custom_call" | custom-call | flops 1024 | bytes 1024 | tf_op jit(solution)/shard_map/pallas_call | solution.py:38
  75.0 6.7 %collective-permute-done.20.near_got = bf16[8,208,256]{2,1,0:T(8,128)(2,1)S(1)} collective-permute-done((bf16[8,208,256]{2,1,0:T(8,128)(2,1)S(1)}, bf16[8,208,256]{2,1,0:T(8,128)(2,1)S(1)}, u32[]{:S(2)}, u32[]{:S(2)}) %collective-permute-start.20) | collective-permute-done | bytes 852000 | tf_op jit(solution)/shard_map/ppermute | solution.py:75
  85.5 7.4 %collective-permute-done.22.last_got = bf16[4,208,256]{2,1,0:T(8,128)(2,1)S(1)} collective-permute-done((bf16[4,208,256]{2,1,0:T(8,128)(2,1)S(1)}, bf16[4,208,256]{2,1,0:T(8,128)(2,1)S(1)}, u32[]{:S(2)}, u32[]{:S(2)}) %collective-permute-start.22) | collective-permute-done | bytes 426016 | tf_op jit(solution)/shard_map/ppermute | solution.py:75
  93.7 3.5 %collective-permute-start.24 = (bf16[208,256]{1,0:T(8,128)(2,1)S(1)}, bf16[208,256]{1,0:T(8,128)(2,1)S(1)}, u32[]{:S(2)}, u32[]{:S(2)}) collective-permute-start(bf16[208,256]{1,0:T(8,128)(2,1)S(1)} %get-tuple-element.213), channel_id=1, source_target_pairs={{0,24},{1,25},{2,26},{3,27},{4,28},{5,29},{6,30},{7,31},{8,0},{9,1... | collective-permute-start | bytes 319496 | tf_op jit(solution)/shard_map/ppermute | solution.py:80
  97.3 2.8 %collective-permute-done.23.refs_0_.refs_1_ = bf16[208,256]{1,0:T(8,128)(2,1)S(1)} collective-permute-done((bf16[208,256]{1,0:T(8,128)(2,1)S(1)}, bf16[208,256]{1,0:T(8,128)(2,1)S(1)}, u32[]{:S(2)}, u32[]{:S(2)}) %collective-permute-start.23) | collective-permute-done | bytes 106528 | tf_op jit(solution)/shard_map/ppermute | solution.py:80
  101.5 1.9 %collective-permute-start.29 = (bf16[208,256]{1,0:T(8,128)(2,1)S(1)}, bf16[208,256]{1,0:T(8,128)(2,1)S(1)}, u32[]{:S(2)}, u32[]{:S(2)}) collective-permute-start(bf16[208,256]{1,0:T(8,128)(2,1)S(1)} %get-tuple-element.221), channel_id=1, source_target_pairs={{0,16},{1,17},{2,18},{3,19},{4,20},{5,21},{6,22},{7,23},{8,24},{9,... | collective-permute-start | bytes 319496 | tf_op jit(solution)/shard_map/ppermute | solution.py:80
  103.3 5.5 %collective-permute-done.25.last_got = bf16[4,208,256]{2,1,0:T(8,128)(2,1)S(1)} collective-permute-done((bf16[4,208,256]{2,1,0:T(8,128)(2,1)S(1)}, bf16[4,208,256]{2,1,0:T(8,128)(2,1)S(1)}, u32[]{:S(2)}, u32[]{:S(2)}) %collective-permute-start.25) | collective-permute-done | bytes 426016 | tf_op jit(solution)/shard_map/ppermute | solution.py:75
  110.7 2.7 %collective-permute-start.27 = (bf16[208,256]{1,0:T(8,128)(2,1)S(1)}, bf16[208,256]{1,0:T(8,128)(2,1)S(1)}, u32[]{:S(2)}, u32[]{:S(2)}) collective-permute-start(bf16[208,256]{1,0:T(8,128)(2,1)S(1)} %get-tuple-element.217), channel_id=1, source_target_pairs={{0,16},{1,17},{2,18},{3,19},{4,20},{5,21},{6,22},{7,23},{8,24},{9,... | collective-permute-start | bytes 319496 | tf_op jit(solution)/shard_map/ppermute | solution.py:80
  116.7 2.8 %collective-permute-done.27.refs_2_ = bf16[208,256]{1,0:T(8,128)(2,1)S(1)} collective-permute-done((bf16[208,256]{1,0:T(8,128)(2,1)S(1)}, bf16[208,256]{1,0:T(8,128)(2,1)S(1)}, u32[]{:S(2)}, u32[]{:S(2)}) %collective-permute-start.27) | collective-permute-done | bytes 106528 | tf_op jit(solution)/shard_map/ppermute | solution.py:80
  121.7 12.9 %all_to_all.5 = f32[16,1,128]{2,1,0:T(1,128)S(1)} all-to-all(f32[16,1,128]{2,1,0:T(1,128)S(1)} %shard_map.534), channel_id=1, replica_groups=mesh['tm'=16,'mp'=2] {'tm'}, dimensions={0} | all-to-all | bytes 16384 | tf_op jit(solution)/shard_map/all_to_all | solution.py:915
  134.8 2.5 %shard_map.536 = (f32[1,1]{1,0:T(1,128)}, f32[512,256]{1,0:T(8,128)}, f32[512,128]{1,0:T(8,128)}, f32[512,128]{1,0:T(8,128)}, f32[512,128]{1,0:T(8,128)}, /*inde...) custom-call(s32[8]{0:T(128)S(1)} %copy-done.22, ...), custom_call_target="tpu_custom_call" | custom-call | flops 1024 | bytes 1024 | tf_op jit(solution)/shard_map/pallas_call | solution.py:38
  (128 shorter events, 38.7 us)
Async XLA Ops:
  3.6 17.7 %collective-permute-start = (bf16[512,256]{1,0:T(8,128)(2,1)}, bf16[512,256]{1,0:T(8,128)(2,1)S(1)}, u32[]{:S(2)}, u32[]{:S(2)}) collective-permute-start(bf16[512,256]{1,0:T(8,128)(2,1)} %get-tuple-element.147), channel_id=1, source_target_pairs={{0,2},{2,4},{4,6},{6,8},{8,10},{10,12},{12,14},{14,16},{16,18},{18... | collective-permute-start | bytes 786440 | tf_op jit(solution)/shard_map/ppermute | solution.py:92
  8.5 7.4 %collective-permute-start.6 = (bf16[208,256]{1,0:T(8,128)(2,1)}, bf16[208,256]{1,0:T(8,128)(2,1)S(1)}, u32[]{:S(2)}, u32[]{:S(2)}) collective-permute-start(bf16[208,256]{1,0:T(8,128)(2,1)} %get-tuple-element.150.value), channel_id=1, source_target_pairs={{0,24},{1,25},{2,26},{3,27},{4,28},{5,29},{6,30},{7,31},{8,0},{9,1... | collective-permute-start | bytes 319496 | tf_op jit(solution)/shard_map/ppermute | solution.py:80
  12.1 9.2 %collective-permute-start.5 = (bf16[208,256]{1,0:T(8,128)(2,1)}, bf16[208,256]{1,0:T(8,128)(2,1)S(1)}, u32[]{:S(2)}, u32[]{:S(2)}) collective-permute-start(bf16[208,256]{1,0:T(8,128)(2,1)} %get-tuple-element.150.value), channel_id=1, source_target_pairs={{0,16},{1,17},{2,18},{3,19},{4,20},{5,21},{6,22},{7,23},{8,24},{9,... | collective-permute-start | bytes 319496 | tf_op jit(solution)/shard_map/ppermute | solution.py:80
  12.1 9.2 %collective-permute-start.4 = (bf16[208,256]{1,0:T(8,128)(2,1)}, bf16[208,256]{1,0:T(8,128)(2,1)S(1)}, u32[]{:S(2)}, u32[]{:S(2)}) collective-permute-start(bf16[208,256]{1,0:T(8,128)(2,1)} %get-tuple-element.150.value), channel_id=1, source_target_pairs={{0,8},{1,9},{2,10},{3,11},{4,12},{5,13},{6,14},{7,15},{8,16},{9,17... | collective-permute-start | bytes 319496 | tf_op jit(solution)/shard_map/ppermute | solution.py:80
  21.3 18.1 %collective-permute-start.9 = (bf16[4,208,256]{2,1,0:T(8,128)(2,1)S(1)}, bf16[4,208,256]{2,1,0:T(8,128)(2,1)S(1)}, u32[]{:S(2)}, u32[]{:S(2)}) collective-permute-start(bf16[4,208,256]{2,1,0:T(8,128)(2,1)S(1)} %get-tuple-element.156.group), channel_id=1, source_target_pairs={{0,4},{1,3},{2,6},{3,1},{4,0},{5,7},{6,2},{7,5},{8,12},{9,11},{10,... | collective-permute-start | bytes 1277960 | tf_op jit(solution)/shard_map/ppermute | solution.py:75
  22.9 16.5 %collective-permute-start.8 = (bf16[4,208,256]{2,1,0:T(8,128)(2,1)S(1)}, bf16[4,208,256]{2,1,0:T(8,128)(2,1)S(1)}, u32[]{:S(2)}, u32[]{:S(2)}) collective-permute-start(bf16[4,208,256]{2,1,0:T(8,128)(2,1)S(1)} %get-tuple-element.156.group), channel_id=1, source_target_pairs={{0,2},{1,5},{2,0},{3,7},{4,6},{5,1},{6,4},{7,3},{8,10},{9,13},{10,... | collective-permute-start | bytes 1277960 | tf_op jit(solution)/shard_map/ppermute | solution.py:75
  24.4 9.1 %collective-permute-start.3 = (bf16[208,256]{1,0:T(8,128)(2,1)}, bf16[208,256]{1,0:T(8,128)(2,1)S(1)}, u32[]{:S(2)}, u32[]{:S(2)}) collective-permute-start(bf16[208,256]{1,0:T(8,128)(2,1)} %get-tuple-element.148.value), channel_id=1, source_target_pairs={{0,24},{1,25},{2,26},{3,27},{4,28},{5,29},{6,30},{7,31},{8,0},{9,1... | collective-permute-start | bytes 319496 | tf_op jit(solution)/shard_map/ppermute | solution.py:80
  29.7 8.6 %collective-permute-start.2 = (bf16[208,256]{1,0:T(8,128)(2,1)}, bf16[208,256]{1,0:T(8,128)(2,1)S(1)}, u32[]{:S(2)}, u32[]{:S(2)}) collective-permute-start(bf16[208,256]{1,0:T(8,128)(2,1)} %get-tuple-element.148.value), channel_id=1, source_target_pairs={{0,16},{1,17},{2,18},{3,19},{4,20},{5,21},{6,22},{7,23},{8,24},{9,... | collective-permute-start | bytes 319496 | tf_op jit(solution)/shard_map/ppermute | solution.py:80
  29.9 8.3 %collective-permute-start.1 = (bf16[208,256]{1,0:T(8,128)(2,1)}, bf16[208,256]{1,0:T(8,128)(2,1)S(1)}, u32[]{:S(2)}, u32[]{:S(2)}) collective-permute-start(bf16[208,256]{1,0:T(8,128)(2,1)} %get-tuple-element.148.value), channel_id=1, source_target_pairs={{0,8},{1,9},{2,10},{3,11},{4,12},{5,13},{6,14},{7,15},{8,16},{9,17... | collective-permute-start | bytes 319496 | tf_op jit(solution)/shard_map/ppermute | solution.py:80
  38.3 8.2 %collective-permute-start.12 = (bf16[4,208,256]{2,1,0:T(8,128)(2,1)S(1)}, bf16[4,208,256]{2,1,0:T(8,128)(2,1)S(1)}, u32[]{:S(2)}, u32[]{:S(2)}) collective-permute-start(bf16[4,208,256]{2,1,0:T(8,128)(2,1)S(1)} %get-tuple-element.162.group), channel_id=1, source_target_pairs={{0,4},{1,3},{2,6},{3,1},{4,0},{5,7},{6,2},{7,5},{8,12},{9,11},{10,... | collective-permute-start | bytes 1277960 | tf_op jit(solution)/shard_map/ppermute | solution.py:75
  38.7 12.3 %collective-permute-start.11 = (bf16[4,208,256]{2,1,0:T(8,128)(2,1)S(1)}, bf16[4,208,256]{2,1,0:T(8,128)(2,1)S(1)}, u32[]{:S(2)}, u32[]{:S(2)}) collective-permute-start(bf16[4,208,256]{2,1,0:T(8,128)(2,1)S(1)} %get-tuple-element.162.group), channel_id=1, source_target_pairs={{0,2},{1,5},{2,0},{3,7},{4,6},{5,1},{6,4},{7,3},{8,10},{9,13},{10,... | collective-permute-start | bytes 1277960 | tf_op jit(solution)/shard_map/ppermute | solution.py:75
  39.4 14.5 %collective-permute-start.13 = (bf16[4,208,256]{2,1,0:T(8,128)(2,1)S(1)}, bf16[4,208,256]{2,1,0:T(8,128)(2,1)S(1)}, u32[]{:S(2)}, u32[]{:S(2)}) collective-permute-start(bf16[4,208,256]{2,1,0:T(8,128)(2,1)S(1)} %get-tuple-element.168), channel_id=1, source_target_pairs={{0,4},{1,3},{2,6},{3,1},{4,0},{5,7},{6,2},{7,5},{8,12},{9,11},{10,... | collective-permute-start | bytes 1277960 | tf_op jit(solution)/shard_map/ppermute | solution.py:75
  42.5 10.4 %collective-permute-start.10 = (f32[8,2176]{1,0:T(8,128)S(1)}, f32[8,2176]{1,0:T(8,128)S(1)}, u32[]{:S(2)}, u32[]{:S(2)}) collective-permute-start(f32[8,2176]{1,0:T(8,128)S(1)} %get-tuple-element.161), channel_id=1, source_target_pairs={{1,2},{2,1},{3,4},{4,3},{5,6},{6,5},{7,8},{8,7},{9,10},{10,9},{11,... | collective-permute-start | bytes 208904 | tf_op jit(solution)/shard_map/ppermute | solution.py:99
  51.0 8.2 %collective-permute-start.15 = (bf16[4,208,256]{2,1,0:T(8,128)(2,1)S(1)}, bf16[4,208,256]{2,1,0:T(8,128)(2,1)S(1)}, u32[]{:S(2)}, u32[]{:S(2)}) collective-permute-start(bf16[4,208,256]{2,1,0:T(8,128)(2,1)S(1)} %get-tuple-element.175), channel_id=1, source_target_pairs={{0,4},{1,3},{2,6},{3,1},{4,0},{5,7},{6,2},{7,5},{8,12},{9,11},{10,... | collective-permute-start | bytes 1277960 | tf_op jit(solution)/shard_map/ppermute | solution.py:75
  68.9 12.8 %collective-permute-start.20 = (bf16[8,208,256]{2,1,0:T(8,128)(2,1)S(1)}, bf16[8,208,256]{2,1,0:T(8,128)(2,1)S(1)}, u32[]{:S(2)}, u32[]{:S(2)}) collective-permute-start(bf16[8,208,256]{2,1,0:T(8,128)(2,1)S(1)} %get-tuple-element.206), channel_id=1, source_target_pairs={{0,4},{1,3},{2,6},{3,1},{4,0},{5,7},{6,2},{7,5},{8,12},{9,11},{10,... | collective-permute-start | bytes 2555912 | tf_op jit(solution)/shard_map/ppermute | solution.py:75
  74.4 7.5 %collective-permute-start.18 = (f32[256,1024]{1,0:T(8,128)S(1)}, f32[256,1024]{1,0:T(8,128)S(1)}, u32[]{:S(2)}, u32[]{:S(2)}) collective-permute-start(f32[256,1024]{1,0:T(8,128)S(1)} %get-tuple-element.201), channel_id=1, source_target_pairs={{0,1},{1,0},{2,3},{3,2},{4,5},{5,4},{6,7},{7,6},{8,9},{9,8},{10,11... | collective-permute-start | bytes 3145736 | tf_op jit(solution)/shard_map/ppermute | solution.py:86
  74.5 8.6 %collective-permute-start.19 = (bf16[16,208,256]{2,1,0:T(8,128)(2,1)S(1)}, bf16[16,208,256]{2,1,0:T(8,128)(2,1)S(1)}, u32[]{:S(2)}, u32[]{:S(2)}) collective-permute-start(bf16[16,208,256]{2,1,0:T(8,128)(2,1)S(1)} %get-tuple-element.205), channel_id=1, source_target_pairs={{0,1},{1,0},{2,3},{3,2},{4,5},{5,4},{6,7},{7,6},{8,9},{9,8},{10,11... | collective-permute-start | bytes 5111816 | tf_op jit(solution)/shard_map/ppermute | solution.py:86
  81.8 11.1 %collective-permute-start.22 = (bf16[4,208,256]{2,1,0:T(8,128)(2,1)S(1)}, bf16[4,208,256]{2,1,0:T(8,128)(2,1)S(1)}, u32[]{:S(2)}, u32[]{:S(2)}) collective-permute-start(bf16[4,208,256]{2,1,0:T(8,128)(2,1)S(1)} %get-tuple-element.211), channel_id=1, source_target_pairs={{0,2},{1,5},{2,0},{3,7},{4,6},{5,1},{6,4},{7,3},{8,10},{9,13},{10,... | collective-permute-start | bytes 1277960 | tf_op jit(solution)/shard_map/ppermute | solution.py:75
  83.7 16.3 %collective-permute-start.21 = (bf16[8,208,256]{2,1,0:T(8,128)(2,1)S(1)}, bf16[8,208,256]{2,1,0:T(8,128)(2,1)S(1)}, u32[]{:S(2)}, u32[]{:S(2)}) collective-permute-start(bf16[8,208,256]{2,1,0:T(8,128)(2,1)S(1)} %get-tuple-element.210), channel_id=1, source_target_pairs={{0,4},{1,3},{2,6},{3,1},{4,0},{5,7},{6,2},{7,5},{8,12},{9,11},{10,... | collective-permute-start | bytes 2555912 | tf_op jit(solution)/shard_map/ppermute | solution.py:75
  100.7 8.1 %collective-permute-start.25 = (bf16[4,208,256]{2,1,0:T(8,128)(2,1)S(1)}, bf16[4,208,256]{2,1,0:T(8,128)(2,1)S(1)}, u32[]{:S(2)}, u32[]{:S(2)}) collective-permute-start(bf16[4,208,256]{2,1,0:T(8,128)(2,1)S(1)} %get-tuple-element.214), channel_id=1, source_target_pairs={{0,2},{1,5},{2,0},{3,7},{4,6},{5,1},{6,4},{7,3},{8,10},{9,13},{10,... | collective-permute-start | bytes 1277960 | tf_op jit(solution)/shard_map/ppermute | solution.py:75
  101.5 12.2 %collective-permute-start.29 = (bf16[208,256]{1,0:T(8,128)(2,1)S(1)}, bf16[208,256]{1,0:T(8,128)(2,1)S(1)}, u32[]{:S(2)}, u32[]{:S(2)}) collective-permute-start(bf16[208,256]{1,0:T(8,128)(2,1)S(1)} %get-tuple-element.221), channel_id=1, source_target_pairs={{0,16},{1,17},{2,18},{3,19},{4,20},{5,21},{6,22},{7,23},{8,24},{9,... | collective-permute-start | bytes 319496 | tf_op jit(solution)/shard_map/ppermute | solution.py:80
  109.0 7.6 %collective-permute-start.26 = (bf16[208,256]{1,0:T(8,128)(2,1)S(1)}, bf16[208,256]{1,0:T(8,128)(2,1)S(1)}, u32[]{:S(2)}, u32[]{:S(2)}) collective-permute-start(bf16[208,256]{1,0:T(8,128)(2,1)S(1)} %get-tuple-element.216), channel_id=1, source_target_pairs={{0,8},{1,9},{2,10},{3,11},{4,12},{5,13},{6,14},{7,15},{8,16},{9,17... | collective-permute-start | bytes 319496 | tf_op jit(solution)/shard_map/ppermute | solution.py:80
  110.7 8.7 %collective-permute-start.27 = (bf16[208,256]{1,0:T(8,128)(2,1)S(1)}, bf16[208,256]{1,0:T(8,128)(2,1)S(1)}, u32[]{:S(2)}, u32[]{:S(2)}) collective-permute-start(bf16[208,256]{1,0:T(8,128)(2,1)S(1)} %get-tuple-element.217), channel_id=1, source_target_pairs={{0,16},{1,17},{2,18},{3,19},{4,20},{5,21},{6,22},{7,23},{8,24},{9,... | collective-permute-start | bytes 319496 | tf_op jit(solution)/shard_map/ppermute | solution.py:80
  114.5 20.2 %collective-permute-start.31 = (bf16[512,256]{1,0:T(8,128)(2,1)S(1)}, bf16[512,256]{1,0:T(8,128)(2,1)S(1)}, u32[]{:S(2)}, u32[]{:S(2)}) collective-permute-start(bf16[512,256]{1,0:T(8,128)(2,1)S(1)} %shard_map.535), channel_id=1, source_target_pairs={{2,0},{4,2},{6,4},{8,6},{10,8},{12,10},{14,12},{16,14},{18,16},{20... | collective-permute-start | bytes 786440 | tf_op jit(solution)/shard_map/ppermute | solution.py:92
  (35 other events, 452.3 us)

commit v9 on v8

--- a/solution.py
+++ b/solution.py
@@ -904,7 +904,7 @@
     grads1, sent1, _ = cores_summed(grad_own, grad_oth, (summed, token))
     last_got = across(sent2, 0)
     terms2, _ = far_terms(grads2, last_got, LONG)
-    grads1, sent1, _ = near_summed(grads1, sent1, unread=(terms2[1], terms2[-1]))
+    grads1, sent1, _ = near_summed(grads1, sent1, unread=(terms2[1],))
     terms1, token = far_terms(grads1, across(sent1, 0))
     sum2, squares2 = totals(terms2, (token,))
     push = call(push_body, struct((held_rows, width), BF16), push, unread=(squares2,))

time: 138 us -> 137 us (level)
  starting transfers between devices: 42.3 us -> 37.6 us
  waiting for transfers between devices: 54.6 us -> 58.7 us
    ppermute x12, starting transfers between devices: 22.6 us -> 18.6 us  [along_far(): lax.ppermute(value, BOTH, route(lambda i, c: (i // NEAR + distance) % far...]
    ppermute x12, waiting for transfers between devices: 17.9 us -> 21.5 us  [along_far(): lax.ppermute(value, BOTH, route(lambda i, c: (i // NEAR + distance) % far...]
where the time goes in v9:
time: 137 us
  waiting for transfers between devices  58.7 us (43%)
  starting transfers between devices  37.6 us (27%)
  Pallas kernels  24.2 us (18%)
  blocking collectives  13.5 us (10%)
  local copies, waits for them, and re-layouts  2 us (1%)
    ppermute x10, waiting for transfers between devices, across(): return lax.ppermute(value, BOTH, route(lambda i, c: i ^ 1 + (c ^ bit)))  28.4 us
    pallas_call x33, Pallas kernels, call(): pl.pallas_call(body, out_shape=out_shape, in_specs=specs, scratch_shapes=...  24.2 us
    ppermute x12, waiting for transfers between devices, along_far(): lax.ppermute(value, BOTH, route(lambda i, c: (i // NEAR + distance) % far...  21.5 us
    ppermute x12, starting transfers between devices, along_far(): lax.ppermute(value, BOTH, route(lambda i, c: (i // NEAR + distance) % far...  18.6 us
    all_to_all x1, blocking collectives, on_device(): lax.all_to_all(sent, 'tm', split_axis=0, concat_axis=0, tiled=True)  13.5 us
    ppermute x10, starting transfers between devices, across(): return lax.ppermute(value, BOTH, route(lambda i, c: i ^ 1 + (c ^ bit)))  11.1 us
    ppermute x7, waiting for transfers between devices, swap_cores(): return lax.ppermute(value, 'mp', [(0, 1), (1, 0)])  8.77 us
    ppermute x2, starting transfers between devices, shifted(): return lax.ppermute(value, axis, pairs)  6.15 us
  transfers between devices with their start and end apart: 32, of which 17 were waited for; matrix products, arithmetic and copies ran while one was open for 0% of the time, Pallas kernels for 12%

profile of v9, /device:TPU:0, one launch (start us, length us, event | category | flops | bytes accessed | tf_op | source)
XLA Modules:
  0.0 137.1 jit_solution(18358269562966416170)
XLA Ops:
  0.7 2.9 %shard_map.504 = (bf16[208,256]{1,0:T(8,128)(2,1)}, bf16[208,256]{1,0:T(8,128)(2,1)}, bf16[512,256]{1,0:T(8,128)(2,1)}) custom-call(s32[8]{0:T(128)} %who.7, f32[512,128]{1,0:T(8,128)} %bitcast.75, f32[2,32,256]{2,1,0:T(8,128)} %bitcast.79, f32[2,32,256]{2,1,0:T(8,128)} %bitcast.81, f32[2,2,16,80]{3,2,1,0:T(8,128)} %bitcast.83, f32[2,2,16,109]{3,2,1,0:T(8,128)} %bitcast.85, ...), custom_call_target="tpu_custom_call" | custom-call | flops 1024 | bytes 1024 | tf_op jit(solution)/shard_map/pallas_call | solution.py:38
  3.6 4.9 %collective-permute-start = (bf16[512,256]{1,0:T(8,128)(2,1)}, bf16[512,256]{1,0:T(8,128)(2,1)S(1)}, u32[]{:S(2)}, u32[]{:S(2)}) collective-permute-start(bf16[512,256]{1,0:T(8,128)(2,1)} %get-tuple-element.147), channel_id=1, source_target_pairs={{0,2},{2,4},{4,6},{6,8},{8,10},{10,12},{12,14},{14,16},{16,18},{18... | collective-permute-start | bytes 786440 | tf_op jit(solution)/shard_map/ppermute | solution.py:92
  8.5 3.6 %collective-permute-start.6 = (bf16[208,256]{1,0:T(8,128)(2,1)}, bf16[208,256]{1,0:T(8,128)(2,1)S(1)}, u32[]{:S(2)}, u32[]{:S(2)}) collective-permute-start(bf16[208,256]{1,0:T(8,128)(2,1)} %get-tuple-element.150.value), channel_id=1, source_target_pairs={{0,24},{1,25},{2,26},{3,27},{4,28},{5,29},{6,30},{7,31},{8,0},{9,1... | collective-permute-start | bytes 319496 | tf_op jit(solution)/shard_map/ppermute | solution.py:80
  15.8 5.4 %collective-permute-done.5.refs_2_ = bf16[208,256]{1,0:T(8,128)(2,1)S(1)} collective-permute-done((bf16[208,256]{1,0:T(8,128)(2,1)}, bf16[208,256]{1,0:T(8,128)(2,1)S(1)}, u32[]{:S(2)}, u32[]{:S(2)}) %collective-permute-start.5) | collective-permute-done | bytes 106528 | tf_op jit(solution)/shard_map/ppermute | solution.py:80
  24.4 5.3 %collective-permute-start.3 = (bf16[208,256]{1,0:T(8,128)(2,1)}, bf16[208,256]{1,0:T(8,128)(2,1)S(1)}, u32[]{:S(2)}, u32[]{:S(2)}) collective-permute-start(bf16[208,256]{1,0:T(8,128)(2,1)} %get-tuple-element.148.value), channel_id=1, source_target_pairs={{0,24},{1,25},{2,26},{3,27},{4,28},{5,29},{6,30},{7,31},{8,0},{9,1... | collective-permute-start | bytes 319496 | tf_op jit(solution)/shard_map/ppermute | solution.py:80
  29.9 2.0 %collective-permute-start.1 = (bf16[208,256]{1,0:T(8,128)(2,1)}, bf16[208,256]{1,0:T(8,128)(2,1)S(1)}, u32[]{:S(2)}, u32[]{:S(2)}) collective-permute-start(bf16[208,256]{1,0:T(8,128)(2,1)} %get-tuple-element.148.value), channel_id=1, source_target_pairs={{0,8},{1,9},{2,10},{3,11},{4,12},{5,13},{6,14},{7,15},{8,16},{9,17... | collective-permute-start | bytes 319496 | tf_op jit(solution)/shard_map/ppermute | solution.py:80
  33.5 4.8 %collective-permute-done.2.refs_2_ = bf16[208,256]{1,0:T(8,128)(2,1)S(1)} collective-permute-done((bf16[208,256]{1,0:T(8,128)(2,1)}, bf16[208,256]{1,0:T(8,128)(2,1)S(1)}, u32[]{:S(2)}, u32[]{:S(2)}) %collective-permute-start.2) | collective-permute-done | bytes 106528 | tf_op jit(solution)/shard_map/ppermute | solution.py:80
  43.2 3.4 %collective-permute-done.12.refs_0_.second = bf16[4,208,256]{2,1,0:T(8,128)(2,1)S(1)} collective-permute-done((bf16[4,208,256]{2,1,0:T(8,128)(2,1)S(1)}, bf16[4,208,256]{2,1,0:T(8,128)(2,1)S(1)}, u32[]{:S(2)}, u32[]{:S(2)}) %collective-permute-start.12) | collective-permute-done | bytes 426016 | tf_op jit(solution)/shard_map/ppermute | solution.py:75
  46.5 4.5 %collective-permute-done.11.value.first = bf16[4,208,256]{2,1,0:T(8,128)(2,1)S(1)} collective-permute-done((bf16[4,208,256]{2,1,0:T(8,128)(2,1)S(1)}, bf16[4,208,256]{2,1,0:T(8,128)(2,1)S(1)}, u32[]{:S(2)}, u32[]{:S(2)}) %collective-permute-start.11) | collective-permute-done | bytes 426016 | tf_op jit(solution)/shard_map/ppermute | solution.py:75
  51.0 1.8 %collective-permute-start.15 = (bf16[4,208,256]{2,1,0:T(8,128)(2,1)S(1)}, bf16[4,208,256]{2,1,0:T(8,128)(2,1)S(1)}, u32[]{:S(2)}, u32[]{:S(2)}) collective-permute-start(bf16[4,208,256]{2,1,0:T(8,128)(2,1)S(1)} %get-tuple-element.175), channel_id=1, source_target_pairs={{0,4},{1,3},{2,6},{3,1},{4,0},{5,7},{6,2},{7,5},{8,12},{9,11},{10,... | collective-permute-start | bytes 1277960 | tf_op jit(solution)/shard_map/ppermute | solution.py:75
  55.5 2.3 %collective-permute-done.14.weights = bf16[16,208,256]{2,1,0:T(8,128)(2,1)S(1)} collective-permute-done((bf16[16,208,256]{2,1,0:T(8,128)(2,1)S(1)}, bf16[16,208,256]{2,1,0:T(8,128)(2,1)S(1)}, u32[]{:S(2)}, u32[]{:S(2)}) %collective-permute-start.14) | collective-permute-done | bytes 1703968 | tf_op jit(solution)/shard_map/ppermute | solution.py:86
  59.5 3.6 %collective-permute-done.16.weights = bf16[16,208,256]{2,1,0:T(8,128)(2,1)S(1)} collective-permute-done((bf16[16,208,256]{2,1,0:T(8,128)(2,1)S(1)}, bf16[16,208,256]{2,1,0:T(8,128)(2,1)S(1)}, u32[]{:S(2)}, u32[]{:S(2)}) %collective-permute-start.16) | collective-permute-done | bytes 1703968 | tf_op jit(solution)/shard_map/ppermute | solution.py:86
  63.1 2.1 %shard_map.518 = (f32[256,512]{1,0:T(8,128)S(1)}, f32[256,512]{1,0:T(8,128)S(1)}, f32[256,512]{1,0:T(8,128)S(1)}, f32[272,512]{1,0:T(8,128)S(1)}, bf16[16,208,256]{2,1,0:T(8,128)(2,1)S(1)}) custom-call(f32[272,512]{1,0:T(8,128)S(1)} %get-tuple-element.171.u2, f32[256,512]{1,0:T(8,128)S(1)} %get-tuple-element.172.s1, ...), custom_call_target="tpu_custom_call" | custom-call | flops 1024 | bytes 1024 | tf_op jit(solution)/shard_map/pallas_call | solution.py:38
  65.9 2.0 %shard_map.520 = (f32[256,512]{1,0:T(8,128)S(1)}, f32[256,512]{1,0:T(8,128)S(1)}, f32[256,512]{1,0:T(8,128)S(1)}, f32[8,128]{1,0:T(8,128)}, bf16[16,208,256]{2,1,0:T(8,128)(2,1)S(1)}) custom-call(f32[272,512]{1,0:T(8,128)S(1)} %get-tuple-element.171.u2, f32[256,512]{1,0:T(8,128)S(1)} %get-tuple-element.172.s1, bf16[272,128]{1,0:T(8,128)(2,1)S(1)} %get-tuple-element.166.cond, ...), custom_call_target="tpu_custom_call" | custom-call | flops 1024 | bytes 1024 | tf_op jit(solution)/shard_map/pallas_call | solution.py:38
  68.9 1.8 %collective-permute-start.20 = (bf16[8,208,256]{2,1,0:T(8,128)(2,1)S(1)}, bf16[8,208,256]{2,1,0:T(8,128)(2,1)S(1)}, u32[]{:S(2)}, u32[]{:S(2)}) collective-permute-start(bf16[8,208,256]{2,1,0:T(8,128)(2,1)S(1)} %get-tuple-element.206), channel_id=1, source_target_pairs={{0,4},{1,3},{2,6},{3,1},{4,0},{5,7},{6,2},{7,5},{8,12},{9,11},{10,... | collective-permute-start | bytes 2555912 | tf_op jit(solution)/shard_map/ppermute | solution.py:75
  70.7 1.9 %shard_map.522 = (f32[256,512]{1,0:T(8,128)S(1)}, f32[8,128]{1,0:T(8,128)}, f32[256,512]{1,0:T(8,128)S(1)}, bf16[16,208,256]{2,1,0:T(8,128)(2,1)S(1)}) custom-call(f32[256,512]{1,0:T(8,128)S(1)} %get-tuple-element.185.g2, f32[272,512]{1,0:T(8,128)S(1)} %get-tuple-element.164.x, bf16[256,512]{1,0:T(8,128)(2,1)S(1)} %get-tuple-element.186.lag, ...), custom_call_target="tpu_custom_call" | custom-call | flops 1024 | bytes 1024 | tf_op jit(solution)/shard_map/pallas_call | solution.py:38
  75.0 6.7 %collective-permute-done.20.near_got = bf16[8,208,256]{2,1,0:T(8,128)(2,1)S(1)} collective-permute-done((bf16[8,208,256]{2,1,0:T(8,128)(2,1)S(1)}, bf16[8,208,256]{2,1,0:T(8,128)(2,1)S(1)}, u32[]{:S(2)}, u32[]{:S(2)}) %collective-permute-start.20) | collective-permute-done | bytes 852000 | tf_op jit(solution)/shard_map/ppermute | solution.py:75
  85.5 7.4 %collective-permute-done.22.last_got = bf16[4,208,256]{2,1,0:T(8,128)(2,1)S(1)} collective-permute-done((bf16[4,208,256]{2,1,0:T(8,128)(2,1)S(1)}, bf16[4,208,256]{2,1,0:T(8,128)(2,1)S(1)}, u32[]{:S(2)}, u32[]{:S(2)}) %collective-permute-start.22) | collective-permute-done | bytes 426016 | tf_op jit(solution)/shard_map/ppermute | solution.py:75
  93.7 6.2 %collective-permute-done.23.refs_0_.refs_1_ = bf16[208,256]{1,0:T(8,128)(2,1)S(1)} collective-permute-done((bf16[208,256]{1,0:T(8,128)(2,1)S(1)}, bf16[208,256]{1,0:T(8,128)(2,1)S(1)}, u32[]{:S(2)}, u32[]{:S(2)}) %collective-permute-start.23) | collective-permute-done | bytes 106528 | tf_op jit(solution)/shard_map/ppermute | solution.py:80
  102.8 6.0 %collective-permute-done.24.last_got = bf16[4,208,256]{2,1,0:T(8,128)(2,1)S(1)} collective-permute-done((bf16[4,208,256]{2,1,0:T(8,128)(2,1)S(1)}, bf16[4,208,256]{2,1,0:T(8,128)(2,1)S(1)}, u32[]{:S(2)}, u32[]{:S(2)}) %collective-permute-start.24) | collective-permute-done | bytes 426016 | tf_op jit(solution)/shard_map/ppermute | solution.py:75
  109.4 3.4 %collective-permute-start.27 = (bf16[208,256]{1,0:T(8,128)(2,1)S(1)}, bf16[208,256]{1,0:T(8,128)(2,1)S(1)}, u32[]{:S(2)}, u32[]{:S(2)}) collective-permute-start(bf16[208,256]{1,0:T(8,128)(2,1)S(1)} %get-tuple-element.217), channel_id=1, source_target_pairs={{0,24},{1,25},{2,26},{3,27},{4,28},{5,29},{6,30},{7,31},{8,0},{9,1... | collective-permute-start | bytes 319496 | tf_op jit(solution)/shard_map/ppermute | solution.py:80
  116.5 2.3 %collective-permute-done.26.refs_2_ = bf16[208,256]{1,0:T(8,128)(2,1)S(1)} collective-permute-done((bf16[208,256]{1,0:T(8,128)(2,1)S(1)}, bf16[208,256]{1,0:T(8,128)(2,1)S(1)}, u32[]{:S(2)}, u32[]{:S(2)}) %collective-permute-start.26) | collective-permute-done | bytes 106528 | tf_op jit(solution)/shard_map/ppermute | solution.py:80
  121.1 13.5 %all_to_all.5 = f32[16,1,128]{2,1,0:T(1,128)S(1)} all-to-all(f32[16,1,128]{2,1,0:T(1,128)S(1)} %shard_map.534), channel_id=1, replica_groups=mesh['tm'=16,'mp'=2] {'tm'}, dimensions={0} | all-to-all | bytes 16384 | tf_op jit(solution)/shard_map/all_to_all | solution.py:915
  134.7 2.5 %shard_map.536 = (f32[1,1]{1,0:T(1,128)}, f32[512,256]{1,0:T(8,128)}, f32[512,128]{1,0:T(8,128)}, f32[512,128]{1,0:T(8,128)}, f32[512,128]{1,0:T(8,128)}, /*inde...) custom-call(s32[8]{0:T(128)S(1)} %copy-done.22, ...), custom_call_target="tpu_custom_call" | custom-call | flops 1024 | bytes 1024 | tf_op jit(solution)/shard_map/pallas_call | solution.py:38
  (128 shorter events, 35.5 us)
Async XLA Ops:
  3.6 17.7 %collective-permute-start = (bf16[512,256]{1,0:T(8,128)(2,1)}, bf16[512,256]{1,0:T(8,128)(2,1)S(1)}, u32[]{:S(2)}, u32[]{:S(2)}) collective-permute-start(bf16[512,256]{1,0:T(8,128)(2,1)} %get-tuple-element.147), channel_id=1, source_target_pairs={{0,2},{2,4},{4,6},{6,8},{8,10},{10,12},{12,14},{14,16},{16,18},{18... | collective-permute-start | bytes 786440 | tf_op jit(solution)/shard_map/ppermute | solution.py:92
  12.1 9.2 %collective-permute-start.5 = (bf16[208,256]{1,0:T(8,128)(2,1)}, bf16[208,256]{1,0:T(8,128)(2,1)S(1)}, u32[]{:S(2)}, u32[]{:S(2)}) collective-permute-start(bf16[208,256]{1,0:T(8,128)(2,1)} %get-tuple-element.150.value), channel_id=1, source_target_pairs={{0,16},{1,17},{2,18},{3,19},{4,20},{5,21},{6,22},{7,23},{8,24},{9,... | collective-permute-start | bytes 319496 | tf_op jit(solution)/shard_map/ppermute | solution.py:80
  12.1 9.2 %collective-permute-start.4 = (bf16[208,256]{1,0:T(8,128)(2,1)}, bf16[208,256]{1,0:T(8,128)(2,1)S(1)}, u32[]{:S(2)}, u32[]{:S(2)}) collective-permute-start(bf16[208,256]{1,0:T(8,128)(2,1)} %get-tuple-element.150.value), channel_id=1, source_target_pairs={{0,8},{1,9},{2,10},{3,11},{4,12},{5,13},{6,14},{7,15},{8,16},{9,17... | collective-permute-start | bytes 319496 | tf_op jit(solution)/shard_map/ppermute | solution.py:80
  21.3 18.1 %collective-permute-start.9 = (bf16[4,208,256]{2,1,0:T(8,128)(2,1)S(1)}, bf16[4,208,256]{2,1,0:T(8,128)(2,1)S(1)}, u32[]{:S(2)}, u32[]{:S(2)}) collective-permute-start(bf16[4,208,256]{2,1,0:T(8,128)(2,1)S(1)} %get-tuple-element.156.group), channel_id=1, source_target_pairs={{0,4},{1,3},{2,6},{3,1},{4,0},{5,7},{6,2},{7,5},{8,12},{9,11},{10,... | collective-permute-start | bytes 1277960 | tf_op jit(solution)/shard_map/ppermute | solution.py:75
  22.9 16.5 %collective-permute-start.8 = (bf16[4,208,256]{2,1,0:T(8,128)(2,1)S(1)}, bf16[4,208,256]{2,1,0:T(8,128)(2,1)S(1)}, u32[]{:S(2)}, u32[]{:S(2)}) collective-permute-start(bf16[4,208,256]{2,1,0:T(8,128)(2,1)S(1)} %get-tuple-element.156.group), channel_id=1, source_target_pairs={{0,2},{1,5},{2,0},{3,7},{4,6},{5,1},{6,4},{7,3},{8,10},{9,13},{10,... | collective-permute-start | bytes 1277960 | tf_op jit(solution)/shard_map/ppermute | solution.py:75
  24.4 9.1 %collective-permute-start.3 = (bf16[208,256]{1,0:T(8,128)(2,1)}, bf16[208,256]{1,0:T(8,128)(2,1)S(1)}, u32[]{:S(2)}, u32[]{:S(2)}) collective-permute-start(bf16[208,256]{1,0:T(8,128)(2,1)} %get-tuple-element.148.value), channel_id=1, source_target_pairs={{0,24},{1,25},{2,26},{3,27},{4,28},{5,29},{6,30},{7,31},{8,0},{9,1... | collective-permute-start | bytes 319496 | tf_op jit(solution)/shard_map/ppermute | solution.py:80
  29.7 8.6 %collective-permute-start.2 = (bf16[208,256]{1,0:T(8,128)(2,1)}, bf16[208,256]{1,0:T(8,128)(2,1)S(1)}, u32[]{:S(2)}, u32[]{:S(2)}) collective-permute-start(bf16[208,256]{1,0:T(8,128)(2,1)} %get-tuple-element.148.value), channel_id=1, source_target_pairs={{0,16},{1,17},{2,18},{3,19},{4,20},{5,21},{6,22},{7,23},{8,24},{9,... | collective-permute-start | bytes 319496 | tf_op jit(solution)/shard_map/ppermute | solution.py:80
  29.9 8.3 %collective-permute-start.1 = (bf16[208,256]{1,0:T(8,128)(2,1)}, bf16[208,256]{1,0:T(8,128)(2,1)S(1)}, u32[]{:S(2)}, u32[]{:S(2)}) collective-permute-start(bf16[208,256]{1,0:T(8,128)(2,1)} %get-tuple-element.148.value), channel_id=1, source_target_pairs={{0,8},{1,9},{2,10},{3,11},{4,12},{5,13},{6,14},{7,15},{8,16},{9,17... | collective-permute-start | bytes 319496 | tf_op jit(solution)/shard_map/ppermute | solution.py:80
  38.3 8.2 %collective-permute-start.12 = (bf16[4,208,256]{2,1,0:T(8,128)(2,1)S(1)}, bf16[4,208,256]{2,1,0:T(8,128)(2,1)S(1)}, u32[]{:S(2)}, u32[]{:S(2)}) collective-permute-start(bf16[4,208,256]{2,1,0:T(8,128)(2,1)S(1)} %get-tuple-element.162.group), channel_id=1, source_target_pairs={{0,4},{1,3},{2,6},{3,1},{4,0},{5,7},{6,2},{7,5},{8,12},{9,11},{10,... | collective-permute-start | bytes 1277960 | tf_op jit(solution)/shard_map/ppermute | solution.py:75
  38.7 12.3 %collective-permute-start.11 = (bf16[4,208,256]{2,1,0:T(8,128)(2,1)S(1)}, bf16[4,208,256]{2,1,0:T(8,128)(2,1)S(1)}, u32[]{:S(2)}, u32[]{:S(2)}) collective-permute-start(bf16[4,208,256]{2,1,0:T(8,128)(2,1)S(1)} %get-tuple-element.162.group), channel_id=1, source_target_pairs={{0,2},{1,5},{2,0},{3,7},{4,6},{5,1},{6,4},{7,3},{8,10},{9,13},{10,... | collective-permute-start | bytes 1277960 | tf_op jit(solution)/shard_map/ppermute | solution.py:75
  39.4 14.5 %collective-permute-start.13 = (bf16[4,208,256]{2,1,0:T(8,128)(2,1)S(1)}, bf16[4,208,256]{2,1,0:T(8,128)(2,1)S(1)}, u32[]{:S(2)}, u32[]{:S(2)}) collective-permute-start(bf16[4,208,256]{2,1,0:T(8,128)(2,1)S(1)} %get-tuple-element.168), channel_id=1, source_target_pairs={{0,4},{1,3},{2,6},{3,1},{4,0},{5,7},{6,2},{7,5},{8,12},{9,11},{10,... | collective-permute-start | bytes 1277960 | tf_op jit(solution)/shard_map/ppermute | solution.py:75
  42.5 10.4 %collective-permute-start.10 = (f32[8,2176]{1,0:T(8,128)S(1)}, f32[8,2176]{1,0:T(8,128)S(1)}, u32[]{:S(2)}, u32[]{:S(2)}) collective-permute-start(f32[8,2176]{1,0:T(8,128)S(1)} %get-tuple-element.161), channel_id=1, source_target_pairs={{1,2},{2,1},{3,4},{4,3},{5,6},{6,5},{7,8},{8,7},{9,10},{10,9},{11,... | collective-permute-start | bytes 208904 | tf_op jit(solution)/shard_map/ppermute | solution.py:99
  51.0 8.2 %collective-permute-start.15 = (bf16[4,208,256]{2,1,0:T(8,128)(2,1)S(1)}, bf16[4,208,256]{2,1,0:T(8,128)(2,1)S(1)}, u32[]{:S(2)}, u32[]{:S(2)}) collective-permute-start(bf16[4,208,256]{2,1,0:T(8,128)(2,1)S(1)} %get-tuple-element.175), channel_id=1, source_target_pairs={{0,4},{1,3},{2,6},{3,1},{4,0},{5,7},{6,2},{7,5},{8,12},{9,11},{10,... | collective-permute-start | bytes 1277960 | tf_op jit(solution)/shard_map/ppermute | solution.py:75
  68.9 12.8 %collective-permute-start.20 = (bf16[8,208,256]{2,1,0:T(8,128)(2,1)S(1)}, bf16[8,208,256]{2,1,0:T(8,128)(2,1)S(1)}, u32[]{:S(2)}, u32[]{:S(2)}) collective-permute-start(bf16[8,208,256]{2,1,0:T(8,128)(2,1)S(1)} %get-tuple-element.206), channel_id=1, source_target_pairs={{0,4},{1,3},{2,6},{3,1},{4,0},{5,7},{6,2},{7,5},{8,12},{9,11},{10,... | collective-permute-start | bytes 2555912 | tf_op jit(solution)/shard_map/ppermute | solution.py:75
  74.5 8.6 %collective-permute-start.19 = (bf16[16,208,256]{2,1,0:T(8,128)(2,1)S(1)}, bf16[16,208,256]{2,1,0:T(8,128)(2,1)S(1)}, u32[]{:S(2)}, u32[]{:S(2)}) collective-permute-start(bf16[16,208,256]{2,1,0:T(8,128)(2,1)S(1)} %get-tuple-element.205), channel_id=1, source_target_pairs={{0,1},{1,0},{2,3},{3,2},{4,5},{5,4},{6,7},{7,6},{8,9},{9,8},{10,11... | collective-permute-start | bytes 5111816 | tf_op jit(solution)/shard_map/ppermute | solution.py:86
  81.8 11.1 %collective-permute-start.22 = (bf16[4,208,256]{2,1,0:T(8,128)(2,1)S(1)}, bf16[4,208,256]{2,1,0:T(8,128)(2,1)S(1)}, u32[]{:S(2)}, u32[]{:S(2)}) collective-permute-start(bf16[4,208,256]{2,1,0:T(8,128)(2,1)S(1)} %get-tuple-element.211), channel_id=1, source_target_pairs={{0,2},{1,5},{2,0},{3,7},{4,6},{5,1},{6,4},{7,3},{8,10},{9,13},{10,... | collective-permute-start | bytes 1277960 | tf_op jit(solution)/shard_map/ppermute | solution.py:75
  83.7 16.3 %collective-permute-start.21 = (bf16[8,208,256]{2,1,0:T(8,128)(2,1)S(1)}, bf16[8,208,256]{2,1,0:T(8,128)(2,1)S(1)}, u32[]{:S(2)}, u32[]{:S(2)}) collective-permute-start(bf16[8,208,256]{2,1,0:T(8,128)(2,1)S(1)} %get-tuple-element.210), channel_id=1, source_target_pairs={{0,4},{1,3},{2,6},{3,1},{4,0},{5,7},{6,2},{7,5},{8,12},{9,11},{10,... | collective-permute-start | bytes 2555912 | tf_op jit(solution)/shard_map/ppermute | solution.py:75
  100.6 8.1 %collective-permute-start.24 = (bf16[4,208,256]{2,1,0:T(8,128)(2,1)S(1)}, bf16[4,208,256]{2,1,0:T(8,128)(2,1)S(1)}, u32[]{:S(2)}, u32[]{:S(2)}) collective-permute-start(bf16[4,208,256]{2,1,0:T(8,128)(2,1)S(1)} %get-tuple-element.213), channel_id=1, source_target_pairs={{0,2},{1,5},{2,0},{3,7},{4,6},{5,1},{6,4},{7,3},{8,10},{9,13},{10,... | collective-permute-start | bytes 1277960 | tf_op jit(solution)/shard_map/ppermute | solution.py:75
  100.6 12.2 %collective-permute-start.28 = (bf16[208,256]{1,0:T(8,128)(2,1)S(1)}, bf16[208,256]{1,0:T(8,128)(2,1)S(1)}, u32[]{:S(2)}, u32[]{:S(2)}) collective-permute-start(bf16[208,256]{1,0:T(8,128)(2,1)S(1)} %get-tuple-element.220), channel_id=1, source_target_pairs={{0,16},{1,17},{2,18},{3,19},{4,20},{5,21},{6,22},{7,23},{8,24},{9,... | collective-permute-start | bytes 319496 | tf_op jit(solution)/shard_map/ppermute | solution.py:80
  102.2 10.6 %collective-permute-start.29 = (bf16[208,256]{1,0:T(8,128)(2,1)S(1)}, bf16[208,256]{1,0:T(8,128)(2,1)S(1)}, u32[]{:S(2)}, u32[]{:S(2)}) collective-permute-start(bf16[208,256]{1,0:T(8,128)(2,1)S(1)} %get-tuple-element.221), channel_id=1, source_target_pairs={{0,24},{1,25},{2,26},{3,27},{4,28},{5,29},{6,30},{7,31},{8,0},{9,1... | collective-permute-start | bytes 319496 | tf_op jit(solution)/shard_map/ppermute | solution.py:80
  108.9 7.5 %collective-permute-start.25 = (bf16[208,256]{1,0:T(8,128)(2,1)S(1)}, bf16[208,256]{1,0:T(8,128)(2,1)S(1)}, u32[]{:S(2)}, u32[]{:S(2)}) collective-permute-start(bf16[208,256]{1,0:T(8,128)(2,1)S(1)} %get-tuple-element.215), channel_id=1, source_target_pairs={{0,8},{1,9},{2,10},{3,11},{4,12},{5,13},{6,14},{7,15},{8,16},{9,17... | collective-permute-start | bytes 319496 | tf_op jit(solution)/shard_map/ppermute | solution.py:80
  109.0 9.8 %collective-permute-start.26 = (bf16[208,256]{1,0:T(8,128)(2,1)S(1)}, bf16[208,256]{1,0:T(8,128)(2,1)S(1)}, u32[]{:S(2)}, u32[]{:S(2)}) collective-permute-start(bf16[208,256]{1,0:T(8,128)(2,1)S(1)} %get-tuple-element.216), channel_id=1, source_target_pairs={{0,16},{1,17},{2,18},{3,19},{4,20},{5,21},{6,22},{7,23},{8,24},{9,... | collective-permute-start | bytes 319496 | tf_op jit(solution)/shard_map/ppermute | solution.py:80
  109.4 9.4 %collective-permute-start.27 = (bf16[208,256]{1,0:T(8,128)(2,1)S(1)}, bf16[208,256]{1,0:T(8,128)(2,1)S(1)}, u32[]{:S(2)}, u32[]{:S(2)}) collective-permute-start(bf16[208,256]{1,0:T(8,128)(2,1)S(1)} %get-tuple-element.217), channel_id=1, source_target_pairs={{0,24},{1,25},{2,26},{3,27},{4,28},{5,29},{6,30},{7,31},{8,0},{9,1... | collective-permute-start | bytes 319496 | tf_op jit(solution)/shard_map/ppermute | solution.py:80
  113.7 20.9 %collective-permute-start.31 = (bf16[512,256]{1,0:T(8,128)(2,1)S(1)}, bf16[512,256]{1,0:T(8,128)(2,1)S(1)}, u32[]{:S(2)}, u32[]{:S(2)}) collective-permute-start(bf16[512,256]{1,0:T(8,128)(2,1)S(1)} %shard_map.535), channel_id=1, source_target_pairs={{2,0},{4,2},{6,4},{8,6},{10,8},{12,10},{14,12},{16,14},{18,16},{20... | collective-permute-start | bytes 786440 | tf_op jit(solution)/shard_map/ppermute | solution.py:92
  (35 other events, 462.8 us)
